TPU v7x, 128 devices: a whole 4x4x4 slice. The times are simulated.
128 devices in a mesh: sec: 4 (over x), site: 32 (over y, z, core).
Axes of the slice: x: 4, y: 4, z: 4, core: 2. Of those that a mesh axis runs over, the one named last changes fastest.
Arguments:
- tensors: bfloat16 [128, 4, 32, 4096], P(('sec', 'site')), may hold values from -6 to 6
- left_env: bfloat16 [128, 2, 32, 4096], P(('sec', 'site')), may hold values from -1.5 to 1.5, as said below
- right_env: bfloat16 [128, 2, 32, 4096], P(('sec', 'site')), may hold values from -1.5 to 1.5, as said below
- kept_rows: int32 [128, 32], P(('sec', 'site')), may hold values from 16 to 64
- coupling: float32 [4, 4], replicated, may hold values from -1 to 1
Outputs:
- new_tensors: bfloat16 [128, 4, 32, 4096], P(('sec', 'site'))
- new_left_env: bfloat16 [128, 2, 32, 4096], P(('sec', 'site'))
Inputs may be any that keep to these rules, and one draw needn't show every extreme that they name: `left_env`: every 64 x 64 block is symmetric. `right_env`: every 64 x 64 block is symmetric.
All inputs are finite; a program needn't handle non-finite values.
Results may differ from a plain program's by a relative error of at most 0.01.
Values may be sent and summed in bfloat16 or wider, within the bound.
No kernel may reach another device: no remote copies, remote signals or barrier semaphores. Data moves between devices by JAX's collectives and lax.ppermute only.
A program may use at most 256 MiB of HBM per device.

v0:
```python
import jax
import jax.numpy as jnp
from jax import lax
from jax.sharding import PartitionSpec as P

NN = 8
NS = 4
BS = 64
PHYS = 4
ITERS = 4
NB = 32


CHARGE_NUMBER = (0, 1, 1, 2)
CHARGE_SPIN = (0, 1, -1, 0)
OCCUPANCY = (0.0, 1.0, 1.0, 2.0)
STEP_SIZE = 0.06
EPSILON = 1e-06


def passed_along(value, axis, steps):
    count = lax.axis_size(axis)
    leading, last = (max(0, -steps), min(count, count - steps))
    return lax.ppermute(value, axis, [(source, source + steps) for source in range(leading, last)])


def to_blocks(source):
    return source.reshape(source.shape[:-2] + (NN, NS, BS, BS))


def to_flat(source):
    return source.reshape(source.shape[:-4] + (NB, BS * BS))


def move_sectors(source, by_number, by_spin):
    return jnp.roll(source, (by_number, by_spin), axis=(-4, -3))


def keep_values(values):
    return values


def pair_work(
    tensor_left, tensor_part, first_state, env_left, env_right, kept_mask, coupling, combine
):
    states = tensor_part.shape[0]
    number_table = jnp.array(CHARGE_NUMBER, jnp.int32)
    spin_table = jnp.array(CHARGE_SPIN, jnp.int32)
    pieces = []
    for left_state in range(PHYS):
        shifted = move_sectors(tensor_part, -CHARGE_NUMBER[left_state], -CHARGE_SPIN[left_state])
        pieces.append(
            jnp.einsum(
                "nzab,tnzbc->tnzac",
                tensor_left[left_state],
                shifted,
                preferred_element_type=jnp.float32,
            )
        )
    vector = jnp.stack(pieces).astype(jnp.bfloat16)
    right_shifted = []
    for left_state in range(PHYS):
        column = []
        for right_slot in range(states):
            right_state = first_state + right_slot
            column.append(
                jnp.roll(
                    env_right,
                    (
                        -(CHARGE_NUMBER[left_state] + number_table[right_state]),
                        -(CHARGE_SPIN[left_state] + spin_table[right_state]),
                    ),
                    axis=(-4, -3),
                )
            )
        right_shifted.append(column)
    for repeat in range(ITERS):
        applied = jnp.einsum(
            "nzab,stnzbc->stnzac", env_left[0], vector, preferred_element_type=jnp.float32
        )
        applied = applied + coupling[:, :, None, None, None, None] * jnp.einsum(
            "nzab,stnzbc->stnzac", env_left[1], vector, preferred_element_type=jnp.float32
        )
        right_rows = []
        for left_state in range(PHYS):
            column = []
            for right_slot in range(states):
                moved = right_shifted[left_state][right_slot]
                part = vector[left_state, right_slot]
                energy_term = jnp.einsum(
                    "nzab,nzbc->nzac", part, moved[0], preferred_element_type=jnp.float32
                )
                density_term = jnp.einsum(
                    "nzab,nzbc->nzac", part, moved[1], preferred_element_type=jnp.float32
                )
                column.append(energy_term + coupling[left_state, right_slot] * density_term)
            right_rows.append(jnp.stack(column))
        applied = applied + jnp.stack(right_rows)
        current = vector.astype(jnp.float32)
        numerator, denominator = combine((jnp.sum(current * applied), jnp.sum(current * current)))
        vector = (current - STEP_SIZE * (applied - numerator / denominator * current)).astype(
            jnp.bfloat16
        )
    projected = jnp.zeros((states, NN, NS, BS, BS), jnp.float32)
    for left_state in range(PHYS):
        contribution = jnp.einsum(
            "nzba,tnzbc->tnzac",
            tensor_left[left_state],
            vector[left_state],
            preferred_element_type=jnp.float32,
        )
        projected = projected + move_sectors(
            contribution, CHARGE_NUMBER[left_state], CHARGE_SPIN[left_state]
        )
    projected = projected * kept_mask[None, :, :, :, None]
    squares = combine((jnp.sum(projected * projected),))[0]
    factor = lax.rsqrt(squares / (PHYS * NB * BS * BS) + EPSILON)
    return (projected * factor).astype(jnp.bfloat16)


def grow_env(tensor_left, env_left):
    mixed_env = (env_left[0].astype(jnp.float32) + env_left[1].astype(jnp.float32)).astype(
        jnp.bfloat16
    )
    total_energy = jnp.zeros((NN, NS, BS, BS), jnp.float32)
    total_density = jnp.zeros((NN, NS, BS, BS), jnp.float32)
    for left_state in range(PHYS):
        half_energy = jnp.einsum(
            "nzba,nzbc->nzac",
            tensor_left[left_state],
            mixed_env,
            preferred_element_type=jnp.float32,
        ).astype(jnp.bfloat16)
        half_density = jnp.einsum(
            "nzba,nzbc->nzac",
            tensor_left[left_state],
            env_left[1],
            preferred_element_type=jnp.float32,
        ).astype(jnp.bfloat16)
        whole_energy = jnp.einsum(
            "nzab,nzbc->nzac",
            half_energy,
            tensor_left[left_state],
            preferred_element_type=jnp.float32,
        )
        whole_density = jnp.einsum(
            "nzab,nzbc->nzac",
            half_density,
            tensor_left[left_state],
            preferred_element_type=jnp.float32,
        )
        total_energy = total_energy + move_sectors(
            whole_energy, CHARGE_NUMBER[left_state], CHARGE_SPIN[left_state]
        )
        total_density = total_density + OCCUPANCY[left_state] * move_sectors(
            whole_density, CHARGE_NUMBER[left_state], CHARGE_SPIN[left_state]
        )
    return (jnp.stack([total_energy, total_density]) / (PHYS * BS)).astype(jnp.bfloat16)


def shards(tensors, left_env, right_env, kept_rows, coupling):
    across = lax.axis_size("site")
    position = lax.axis_index("sec") * across + lax.axis_index("site")
    tensor = to_blocks(tensors[0])
    env_left = to_blocks(left_env[0])
    env_right = to_blocks(right_env[0])
    row_ids = jnp.arange(BS, dtype=jnp.int32)
    own_mask = (row_ids[None, None, :] < kept_rows[0].reshape(NN, NS)[:, :, None]).astype(
        jnp.bfloat16
    )

    def bond_update(tensor, env_left, is_right):
        got_tensor, got_right = passed_along((tensor, env_right), ("sec", "site"), -1)
        made_tensor = pair_work(
            tensor,
            got_tensor,
            0,
            env_left,
            got_right,
            own_mask.astype(jnp.float32),
            coupling,
            keep_values,
        )
        made_env = grow_env(tensor, env_left)
        new_tensor, new_env = passed_along((made_tensor, made_env), ("sec", "site"), 1)
        return (jnp.where(is_right, new_tensor, tensor), jnp.where(is_right, new_env, env_left))

    odd_site = position % 2 == 1
    tensor, env_left = bond_update(tensor, env_left, odd_site)
    second_right = jnp.logical_and(jnp.logical_not(odd_site), position > 0)
    tensor, env_left = bond_update(tensor, env_left, second_right)
    return (to_flat(tensor)[None], to_flat(env_left)[None])


def solution(mesh):
    return jax.shard_map(
        shards,
        mesh=mesh,
        in_specs=(
            P(("sec", "site"), None, None, None),
            P(("sec", "site"), None, None, None),
            P(("sec", "site"), None, None, None),
            P(("sec", "site"), None),
            P(),
        ),
        out_specs=(P(("sec", "site"), None, None, None), P(("sec", "site"), None, None, None)),
        check_vma=False,
    )
```

profile of v0, /device:TPU:6, one launch (start us, length us, event | category | flops | bytes accessed | tf_op | source)
XLA Modules:
  0.0 1079.7 jit_solution(18197757149166235809)
XLA Ops:
  137.6 11.5 %fusion.35 = f32[8,4,4,4,64,64]{5,4,1,0,3,2:T(8,128)} fusion(bf16[4,4,8,4,64,64]{4,5,1,3,2,0:T(8,128)(2,1)} %get-tuple-element.18, bf16[8,4,64,64,1,1]{3,2,1,0,4,5:T(8,128)(2,1)S(1)} %copy-done.103), kind=kOutput, calls=%fused_computation.78 | convolution fusion | flops 268435456 | bytes 12845056 | tf_op jit(solution)/shard_map/nzab,stnzbc->stnzac/dot_general | solution.py:78
  167.5 17.2 %multiply_reduce_fusion.7 = (f32[]{:T(128)}, f32[4,4,8,4,64,64]{4,5,3,2,1,0:T(8,128)}) fusion(f32[1,4,8,4,64,64]{4,5,3,2,1,0:T(8,128)S(1)} %copy-done.141, f32[1,4,8,4,64,64]{4,5,3,2,1,0:T(8,128)} %maximum_bitcast_fusion.2, f32[1,4,8,4,64,64]{4,5,3,2,1,0:T(8,128)} %maximum_bitcast_fusion.1, f32[1,4,8,4,64,64]{4,5,3,2,1,0:T(8,128)} %maximum_bitcast_fusion, ...), kind=kOutput, calls=%fused_computation.65 | convolution fusion | flops 287309824 | bytes 29622340 | tf_op jit(solution)/shard_map/nzab,stnzbc->stnzac/dot_general | solution.py:81
  186.1 16.2 %multiply_reduce_fusion.4 = (f32[]{:T(128)}, bf16[4,4,8,4,64,64]{4,5,1,3,2,0:T(8,128)(2,1)S(1)}) fusion(bf16[4,4,8,4,64,64]{4,5,1,3,2,0:T(8,128)(2,1)} %get-tuple-element.18, f32[4,4,8,4,64,64]{4,5,3,2,1,0:T(8,128)} %get-tuple-element.59, f32[]{:T(128)S(6)} %div.36), kind=kLoop, calls=%fused_computation.61 | loop fusion | flops 20971520 | bytes 16777224 | tf_op jit(solution)/shard_map/reduce_sum | solution.py:100
  226.1 11.5 %fusion.32 = f32[8,4,4,4,64,64]{5,4,1,0,3,2:T(8,128)} fusion(bf16[4,4,8,4,64,64]{4,5,1,3,2,0:T(8,128)(2,1)} %copy-done.2, bf16[8,4,64,64,1,1]{3,2,1,0,4,5:T(8,128)(2,1)S(1)} %copy-done.104), kind=kOutput, calls=%fused_computation.75 | convolution fusion | flops 268435456 | bytes 12845056 | tf_op jit(solution)/shard_map/nzab,stnzbc->stnzac/dot_general | solution.py:78
  267.9 17.2 %multiply_reduce_fusion.5 = (f32[]{:T(128)}, f32[4,4,8,4,64,64]{4,5,3,2,1,0:T(8,128)}) fusion(f32[1,4,8,4,64,64]{4,5,3,2,1,0:T(8,128)S(1)} %copy-done.146, f32[1,4,8,4,64,64]{4,5,3,2,1,0:T(8,128)} %maximum_bitcast_fusion.6, f32[1,4,8,4,64,64]{4,5,3,2,1,0:T(8,128)} %maximum_bitcast_fusion.5, f32[1,4,8,4,64,64]{4,5,3,2,1,0:T(8,128)} %maximum_bitcast_fusion.4, ...), kind=kOutput, calls=%fused_computation.62 | convolution fusion | flops 287309824 | bytes 29622340 | tf_op jit(solution)/shard_map/nzab,stnzbc->stnzac/dot_general | solution.py:81
  286.5 16.7 %multiply_reduce_fusion.2 = (f32[]{:T(128)}, bf16[4,4,8,4,64,64]{4,5,1,3,2,0:T(8,128)(2,1)S(1)}) fusion(bf16[4,4,8,4,64,64]{4,5,1,3,2,0:T(8,128)(2,1)} %copy-done.2, f32[4,4,8,4,64,64]{4,5,3,2,1,0:T(8,128)} %get-tuple-element.61, f32[]{:T(128)S(6)} %div.37), kind=kLoop, calls=%fused_computation.58 | loop fusion | flops 20971520 | bytes 16777224 | tf_op jit(solution)/shard_map/reduce_sum | solution.py:100
  326.9 11.5 %fusion.29 = f32[8,4,4,4,64,64]{5,4,1,0,3,2:T(8,128)} fusion(bf16[4,4,8,4,64,64]{4,5,1,3,2,0:T(8,128)(2,1)} %copy-done.4, bf16[8,4,64,64,1,1]{3,2,1,0,4,5:T(8,128)(2,1)S(1)} %copy-done.105), kind=kOutput, calls=%fused_computation.72 | convolution fusion | flops 268435456 | bytes 12845056 | tf_op jit(solution)/shard_map/nzab,stnzbc->stnzac/dot_general | solution.py:78
  368.8 17.2 %multiply_reduce_fusion.3 = (f32[]{:T(128)}, f32[4,4,8,4,64,64]{4,5,3,2,1,0:T(8,128)}) fusion(f32[1,4,8,4,64,64]{4,5,3,2,1,0:T(8,128)S(1)} %copy-done.147, f32[1,4,8,4,64,64]{4,5,3,2,1,0:T(8,128)} %maximum_bitcast_fusion.10, f32[1,4,8,4,64,64]{4,5,3,2,1,0:T(8,128)} %maximum_bitcast_fusion.9, f32[1,4,8,4,64,64]{4,5,3,2,1,0:T(8,128)} %maximum_bitcast_fusion.8, ...), kind=kOutput, calls=%fused_computation.59 | convolution fusion | flops 287309824 | bytes 29622340 | tf_op jit(solution)/shard_map/nzab,stnzbc->stnzac/dot_general | solution.py:81
  387.3 16.2 %multiply_reduce_fusion = (f32[]{:T(128)}, bf16[4,4,8,4,64,64]{4,5,1,3,2,0:T(8,128)(2,1)S(1)}) fusion(bf16[4,4,8,4,64,64]{4,5,1,3,2,0:T(8,128)(2,1)} %copy-done.4, f32[4,4,8,4,64,64]{4,5,3,2,1,0:T(8,128)} %get-tuple-element.63, f32[]{:T(128)S(6)} %div.38), kind=kLoop, calls=%fused_computation.55 | loop fusion | flops 20971520 | bytes 16777224 | tf_op jit(solution)/shard_map/reduce_sum | solution.py:100
  427.3 11.5 %fusion.26 = f32[8,4,4,4,64,64]{5,4,1,0,3,2:T(8,128)} fusion(bf16[4,4,8,4,64,64]{4,5,1,3,2,0:T(8,128)(2,1)} %copy-done.6, bf16[8,4,64,64,1,1]{3,2,1,0,4,5:T(8,128)(2,1)S(1)} %copy-done.106), kind=kOutput, calls=%fused_computation.69 | convolution fusion | flops 268435456 | bytes 12845056 | tf_op jit(solution)/shard_map/nzab,stnzbc->stnzac/dot_general | solution.py:78
  469.4 17.2 %multiply_reduce_fusion.1 = (f32[]{:T(128)}, f32[4,4,8,4,64,64]{4,5,3,2,1,0:T(8,128)}) fusion(f32[1,4,8,4,64,64]{4,5,3,2,1,0:T(8,128)S(1)} %copy-done.143, f32[1,4,8,4,64,64]{4,5,3,2,1,0:T(8,128)} %maximum_bitcast_fusion.14, f32[1,4,8,4,64,64]{4,5,3,2,1,0:T(8,128)} %maximum_bitcast_fusion.13, f32[1,4,8,4,64,64]{4,5,3,2,1,0:T(8,128)} %maximum_bitcast_fusion.12, ...), kind=kOutput, calls=%fused_computation.56 | convolution fusion | flops 287309824 | bytes 29622340 | tf_op jit(solution)/shard_map/nzab,stnzbc->stnzac/dot_general | solution.py:81
  487.9 14.8 %fusion.21 = bf16[4,4,8,4,64,64]{4,5,1,3,2,0:T(8,128)(2,1)S(1)} fusion(bf16[4,4,8,4,64,64]{4,5,1,3,2,0:T(8,128)(2,1)} %copy-done.6, f32[4,4,8,4,64,64]{4,5,3,2,1,0:T(8,128)} %get-tuple-element.65, f32[]{:T(128)S(6)} %div.39), kind=kLoop, calls=%fused_computation.46 | loop fusion | flops 14680064 | bytes 16777220 | tf_op jit(solution)/shard_map/convert_element_type | solution.py:101
  527.0 23.9 %collective-permute-done.2 = bf16[4,8,4,64,64]{3,4,0,2,1:T(8,128)(2,1)} collective-permute-done((bf16[4,8,4,64,64]{3,4,0,2,1:T(8,128)(2,1)}, bf16[4,8,4,64,64]{3,4,0,2,1:T(8,128)(2,1)}, u32[]{:S(2)}, u32[]{:S(2)}) %collective-permute-start.2) | collective-permute-done | bytes 1048608 | tf_op jit(solution)/shard_map/ppermute | solution.py:24
  661.4 20.9 %fusion.1 = (f32[]{:T(128)}, f32[]{:T(128)}, f32[4,4,8,4,64,64]{4,5,3,2,1,0:T(8,128)}) fusion(bf16[1,4,8,4,64,64]{4,5,3,2,1,0:T(8,128)(2,1)S(1)} %convert_bitcast_fusion, bf16[1,4,8,4,64,64]{4,5,3,2,1,0:T(8,128)(2,1)S(1)} %convert_bitcast_fusion.1, bf16[1,4,8,4,64,64]{4,5,3,2,1,0:T(8,128)(2,1)S(1)} %convert_bitcast_fusion.2, ...), kind=kOutput, calls=%fused_computation.17 | convolution fusion | flops 304087040 | bytes 44566536 | tf_op jit(solution)/shard_map/nzab,stnzbc->stnzac/dot_general | solution.py:78
  683.6 9.7 fusion.4
  717.2 11.5 %fusion.368 = f32[8,4,4,4,64,64]{5,4,1,0,3,2:T(8,128)} fusion(bf16[4,4,8,4,64,64]{4,5,3,2,1,0:T(8,128)(2,1)} %copy-done.10, bf16[2,8,4,64,64]{4,3,2,1,0:T(8,128)(2,1)S(1)} %copy-done.88), kind=kOutput, calls=%fused_computation.856 | convolution fusion | flops 268435456 | bytes 13107200 | tf_op jit(solution)/shard_map/nzab,stnzbc->stnzac/dot_general | solution.py:81
  759.4 18.4 %fusion.6 = (f32[]{:T(128)}, f32[]{:T(128)}, f32[4,4,8,4,64,64]{4,5,3,2,1,0:T(8,128)}) fusion(bf16[4,4,8,4,64,64]{4,5,3,2,1,0:T(8,128)(2,1)S(1)} %copy-done.11, f32[1,4,8,4,64,64]{4,5,3,2,1,0:T(8,128)S(1)} %copy-done.142, f32[1,4,8,4,64,64]{4,5,3,2,1,0:T(8,128)} %maximum_bitcast_fusion.22, f32[1,4,8,4,64,64]{4,5,3,2,1,0:T(8,128)} %maximum_bitcast_fusion.21, ...), kind=kOutput, calls=%fused_computation.22 | convolution fusion | flops 291504128 | bytes 44566536 | tf_op jit(solution)/shard_map/nzab,stnzbc->stnzac/dot_general | solution.py:78
  779.1 14.8 %fusion.9 = bf16[4,4,8,4,64,64]{4,5,3,2,1,0:T(8,128)(2,1)S(1)} fusion(f32[4,4,8,4,64,64]{4,5,3,2,1,0:T(8,128)} %get-tuple-element.69, f32[]{:T(128)S(6)} %div.43, f32[4,4,8,4,64,64]{4,5,3,2,1,0:T(8,128)} %get-tuple-element.68, f32[]{:T(128)S(6)} %div.42, bf16[1,4,8,4,64,64]{4,5,3,2,1,0:T(8,128)(2,1)} %copy-done.97, ...), kind=kLoop, calls=%fused_computation.25 | loop fusion | flops 31457280 | bytes 25165832 | tf_op jit(solution)/shard_map/convert_element_type | solution.py:101
  817.7 11.5 %fusion.366 = f32[8,4,4,4,64,64]{5,4,1,0,3,2:T(8,128)} fusion(bf16[4,4,8,4,64,64]{4,5,3,2,1,0:T(8,128)(2,1)} %copy-done.8, bf16[2,8,4,64,64]{4,3,2,1,0:T(8,128)(2,1)S(1)} %copy-done.90), kind=kOutput, calls=%fused_computation.854 | convolution fusion | flops 268435456 | bytes 13107200 | tf_op jit(solution)/shard_map/nzab,stnzbc->stnzac/dot_general | solution.py:81
  859.8 18.3 %fusion.11 = (f32[]{:T(128)}, f32[]{:T(128)}, f32[4,4,8,4,64,64]{4,5,3,2,1,0:T(8,128)}) fusion(bf16[4,4,8,4,64,64]{4,5,3,2,1,0:T(8,128)(2,1)S(1)} %copy-done.9, f32[1,4,8,4,64,64]{4,5,3,2,1,0:T(8,128)S(1)} %copy-done.145, f32[1,4,8,4,64,64]{4,5,3,2,1,0:T(8,128)} %maximum_bitcast_fusion.26, f32[1,4,8,4,64,64]{4,5,3,2,1,0:T(8,128)} %maximum_bitcast_fusion.25, ...), kind=kOutput, calls=%fused_computation.27 | convolution fusion | flops 291504128 | bytes 44566536 | tf_op jit(solution)/shard_map/nzab,stnzbc->stnzac/dot_general | solution.py:78
  896.1 11.5 %fusion.364 = f32[8,4,4,4,64,64]{5,4,1,0,3,2:T(8,128)} fusion(bf16[4,4,8,4,64,64]{4,5,3,2,1,0:T(8,128)(2,1)} %copy-done, bf16[2,8,4,64,64]{4,3,2,1,0:T(8,128)(2,1)} %copy-done.86), kind=kOutput, calls=%fused_computation.852 | convolution fusion | flops 268435456 | bytes 17301504 | tf_op jit(solution)/shard_map/nzab,stnzbc->stnzac/dot_general | solution.py:81
  935.7 16.0 %add_bitcast_fusion = f32[4,4,8,4,64,64]{4,5,3,2,1,0:T(8,128)} fusion(f32[8,4,4,4,64,64]{5,4,1,0,3,2:T(8,128)} %fusion.364, bf16[4,4,8,4,64,64]{4,5,3,2,1,0:T(8,128)(2,1)} %copy-done, f32[4,4]{1,0:T(4,128)S(1)} %copy-done.238, bf16[2,8,4,64,64]{4,3,2,1,0:T(8,128)(2,1)S(1)} %copy-done.92), kind=kOutput, calls=%fused_computation.53 | convolution fusion | flops 272629760 | bytes 21497856 | tf_op jit(solution)/shard_map/nzab,stnzbc->stnzac/dot_general | solution.py:78
  992.5 13.9 %fusion.19 = bf16[4,4,8,4,64,64]{4,5,1,3,2,0:T(8,128)(2,1)S(1)} fusion(f32[]{:T(128)S(6)} %div.45, bf16[4,4,8,4,64,64]{4,5,3,2,1,0:T(8,128)(2,1)} %copy-done, f32[1,4,8,4,64,64]{4,5,1,3,2,0:T(8,128)} %copy-done.94, f32[4,4,8,4,64,64]{4,5,3,2,1,0:T(8,128)} %add_bitcast_fusion, f32[1,8,4,64,64]{3,4,2,1,0:T(8,128)S(1)} %copy-done.109, ...), kind=kLoop, calls=%fused_computation.35 | loop fusion | flops 22544384 | bytes 25165828 | tf_op jit(solution)/shard_map/convert_element_type | solution.py:101
  1035.7 33.2 %collective-permute-done.6 = bf16[2,8,4,64,64]{4,3,2,1,0:T(8,128)(2,1)S(1)} collective-permute-done((bf16[2,8,4,64,64]{4,3,2,1,0:T(8,128)(2,1)S(1)}, bf16[2,8,4,64,64]{4,3,2,1,0:T(8,128)(2,1)S(1)}, u32[]{:S(2)}, u32[]{:S(2)}) %collective-permute-start.6) | collective-permute-done | bytes 524320 | tf_op jit(solution)/shard_map/ppermute | solution.py:24
  (945 shorter events, 680.5 us)
Async XLA Ops:
  6.6 78.1 %collective-permute-start = (bf16[4,8,4,64,64]{3,4,0,2,1:T(8,128)(2,1)}, bf16[4,8,4,64,64]{3,4,0,2,1:T(8,128)(2,1)}, u32[]{:S(2)}, u32[]{:S(2)}) collective-permute-start(bf16[4,8,4,64,64]{3,4,0,2,1:T(8,128)(2,1)} %copy.601), channel_id=1, source_target_pairs={{1,0},{2,1},{3,2},{4,3},{5,4},{6,5},{7,6},{8,7},{9,8},{10,9},{11,1... | collective-permute-start | bytes 3145736 | tf_op jit(solution)/shard_map/ppermute | solution.py:24
  16.8 65.7 %collective-permute-start.1 = (bf16[2,8,4,64,64]{4,3,2,1,0:T(8,128)(2,1)}, bf16[2,8,4,64,64]{4,3,2,1,0:T(8,128)(2,1)S(1)}, u32[]{:S(2)}, u32[]{:S(2)}) collective-permute-start(bf16[2,8,4,64,64]{4,3,2,1,0:T(8,128)(2,1)} %reshape_squeeze.10), channel_id=1, source_target_pairs={{1,0},{2,1},{3,2},{4,3},{5,4},{6,5},{7,6},{8,7},{9,8},{10,9},{11,1... | collective-permute-start | bytes 1572872 | tf_op jit(solution)/shard_map/ppermute | solution.py:24
  67.7 456.0 %collective-permute-start.4 = (bf16[2,8,4,64,64]{4,3,2,1,0:T(8,128)(2,1)}, bf16[2,8,4,64,64]{4,3,2,1,0:T(8,128)(2,1)}, u32[]{:S(2)}, u32[]{:S(2)}) collective-permute-start(bf16[2,8,4,64,64]{4,3,2,1,0:T(8,128)(2,1)} %fusion.65), channel_id=1, source_target_pairs={{0,1},{1,2},{2,3},{3,4},{4,5},{5,6},{6,7},{7,8},{8,9},{9,10},{10,1... | collective-permute-start | bytes 1572872 | tf_op jit(solution)/shard_map/ppermute | solution.py:24
  83.7 44.0 %copy-start.60 = (bf16[8,4,64,64]{3,2,1,0:T(8,128)(2,1)}, bf16[8,4,64,64]{3,2,1,0:T(8,128)(2,1)S(1)}, u32[]{:S(2)}) copy-start(bf16[8,4,64,64]{3,2,1,0:T(8,128)(2,1)S(1)} %get-tuple-element.34) | copy-start | bytes 786436
  84.7 20.7 %copy-start.28 = (bf16[8,4,64,64]{3,2,1,0:T(8,128)(2,1)}, bf16[8,4,64,64]{3,2,1,0:T(8,128)(2,1)S(1)}, u32[]{:S(2)}) copy-start(bf16[8,4,64,64]{3,2,1,0:T(8,128)(2,1)S(1)} %get-tuple-element.74) | copy-start | bytes 786436
  84.7 21.4 %copy-start.44 = (bf16[8,4,64,64]{3,2,1,0:T(8,128)(2,1)}, bf16[8,4,64,64]{3,2,1,0:T(8,128)(2,1)S(1)}, u32[]{:S(2)}) copy-start(bf16[8,4,64,64]{3,2,1,0:T(8,128)(2,1)S(1)} %get-tuple-element.73) | copy-start | bytes 786436
  84.7 39.1 %copy-start.20 = (bf16[8,4,64,64]{3,2,1,0:T(8,128)(2,1)}, bf16[8,4,64,64]{3,2,1,0:T(8,128)(2,1)S(1)}, u32[]{:S(2)}) copy-start(bf16[8,4,64,64]{3,2,1,0:T(8,128)(2,1)S(1)} %get-tuple-element.36) | copy-start | bytes 786436
  84.7 51.0 %copy-start.12 = (bf16[8,4,64,64]{3,2,1,0:T(8,128)(2,1)}, bf16[8,4,64,64]{3,2,1,0:T(8,128)(2,1)S(1)}, u32[]{:S(2)}) copy-start(bf16[8,4,64,64]{3,2,1,0:T(8,128)(2,1)S(1)} %get-tuple-element.76) | copy-start | bytes 786436
  97.7 37.9 %copy-start.95 = (bf16[1,4,8,4,64,64]{4,5,1,3,2,0:T(8,128)(2,1)}, bf16[1,4,8,4,64,64]{4,5,1,3,2,0:T(8,128)(2,1)S(1)}, u32[]{:S(2)}) copy-start(bf16[1,4,8,4,64,64]{4,5,1,3,2,0:T(8,128)(2,1)S(1)} %convert_bitcast_fusion.7) | copy-start | bytes 3145732
  202.3 22.4 %copy-start.2 = (bf16[4,4,8,4,64,64]{4,5,1,3,2,0:T(8,128)(2,1)}, bf16[4,4,8,4,64,64]{4,5,1,3,2,0:T(8,128)(2,1)S(1)}, u32[]{:S(2)}) copy-start(bf16[4,4,8,4,64,64]{4,5,1,3,2,0:T(8,128)(2,1)S(1)} %get-tuple-element.16) | copy-start | bytes 12582916
  286.5 19.1 %copy-start.38 = (bf16[8,4,64,64]{3,2,1,0:T(8,128)(2,1)S(1)}, bf16[8,4,64,64]{3,2,1,0:T(8,128)(2,1)}, u32[]{:S(2)}) copy-start(bf16[8,4,64,64]{3,2,1,0:T(8,128)(2,1)} %copy-done.36) | copy-start | bytes 786436
  303.2 22.4 %copy-start.4 = (bf16[4,4,8,4,64,64]{4,5,1,3,2,0:T(8,128)(2,1)}, bf16[4,4,8,4,64,64]{4,5,1,3,2,0:T(8,128)(2,1)S(1)}, u32[]{:S(2)}) copy-start(bf16[4,4,8,4,64,64]{4,5,1,3,2,0:T(8,128)(2,1)S(1)} %get-tuple-element.14) | copy-start | bytes 12582916
  403.5 22.4 %copy-start.6 = (bf16[4,4,8,4,64,64]{4,5,1,3,2,0:T(8,128)(2,1)}, bf16[4,4,8,4,64,64]{4,5,1,3,2,0:T(8,128)(2,1)S(1)}, u32[]{:S(2)}) copy-start(bf16[4,4,8,4,64,64]{4,5,1,3,2,0:T(8,128)(2,1)S(1)} %get-tuple-element.12) | copy-start | bytes 12582916
  519.0 31.9 %collective-permute-start.2 = (bf16[4,8,4,64,64]{3,4,0,2,1:T(8,128)(2,1)}, bf16[4,8,4,64,64]{3,4,0,2,1:T(8,128)(2,1)}, u32[]{:S(2)}, u32[]{:S(2)}) collective-permute-start(bf16[4,8,4,64,64]{3,4,0,2,1:T(8,128)(2,1)} %multiply_convert_fusion.1), channel_id=1, source_target_pairs={{0,1},{1,2},{2,3},{3,4},{4,5},{5,6},{6,7},{7,8},{8,9},{9,10},{10,1... | collective-permute-start | bytes 3145736 | tf_op jit(solution)/shard_map/ppermute | solution.py:24
  554.0 43.8 %collective-permute-start.3 = (bf16[4,8,4,64,64]{3,4,0,2,1:T(8,128)(2,1)}, bf16[4,8,4,64,64]{3,4,0,2,1:T(8,128)(2,1)}, u32[]{:S(2)}, u32[]{:S(2)}) collective-permute-start(bf16[4,8,4,64,64]{3,4,0,2,1:T(8,128)(2,1)} %broadcast_select_fusion), channel_id=1, source_target_pairs={{1,0},{2,1},{3,2},{4,3},{5,4},{6,5},{7,6},{8,7},{9,8},{10,9},{11,1... | collective-permute-start | bytes 3145736 | tf_op jit(solution)/shard_map/ppermute | solution.py:24
  605.5 54.8 %copy-start.97 = (bf16[1,4,8,4,64,64]{4,5,3,2,1,0:T(8,128)(2,1)}, bf16[1,4,8,4,64,64]{4,5,3,2,1,0:T(8,128)(2,1)S(1)}, u32[]{:S(2)}) copy-start(bf16[1,4,8,4,64,64]{4,5,3,2,1,0:T(8,128)(2,1)S(1)} %convert_bitcast_fusion) | copy-start | bytes 3145732
  611.9 48.4 %copy-start.98 = (bf16[1,4,8,4,64,64]{4,5,3,2,1,0:T(8,128)(2,1)}, bf16[1,4,8,4,64,64]{4,5,3,2,1,0:T(8,128)(2,1)S(1)}, u32[]{:S(2)}) copy-start(bf16[1,4,8,4,64,64]{4,5,3,2,1,0:T(8,128)(2,1)S(1)} %convert_bitcast_fusion.1) | copy-start | bytes 3145732
  617.8 42.5 %copy-start.99 = (bf16[1,4,8,4,64,64]{4,5,3,2,1,0:T(8,128)(2,1)}, bf16[1,4,8,4,64,64]{4,5,3,2,1,0:T(8,128)(2,1)S(1)}, u32[]{:S(2)}) copy-start(bf16[1,4,8,4,64,64]{4,5,3,2,1,0:T(8,128)(2,1)S(1)} %convert_bitcast_fusion.2) | copy-start | bytes 3145732
  625.1 35.2 %copy-start.85 = (bf16[1,4,8,4,64,64]{4,5,3,2,1,0:T(8,128)(2,1)}, bf16[1,4,8,4,64,64]{4,5,3,2,1,0:T(8,128)(2,1)S(1)}, u32[]{:S(2)}) copy-start(bf16[1,4,8,4,64,64]{4,5,3,2,1,0:T(8,128)(2,1)S(1)} %convert_bitcast_fusion.3) | copy-start | bytes 3145732
  693.3 22.5 %copy-start.10 = (bf16[4,4,8,4,64,64]{4,5,3,2,1,0:T(8,128)(2,1)}, bf16[4,4,8,4,64,64]{4,5,3,2,1,0:T(8,128)(2,1)S(1)}, u32[]{:S(2)}) copy-start(bf16[4,4,8,4,64,64]{4,5,3,2,1,0:T(8,128)(2,1)S(1)} %fusion.4) | copy-start | bytes 12582916
  793.9 22.4 %copy-start.8 = (bf16[4,4,8,4,64,64]{4,5,3,2,1,0:T(8,128)(2,1)}, bf16[4,4,8,4,64,64]{4,5,3,2,1,0:T(8,128)(2,1)S(1)}, u32[]{:S(2)}) copy-start(bf16[4,4,8,4,64,64]{4,5,3,2,1,0:T(8,128)(2,1)S(1)} %fusion.9) | copy-start | bytes 12582916
  1025.8 43.1 %copy-start.93 = (bf16[2,8,4,64,64]{4,3,2,1,0:T(8,128)(2,1)S(1)}, bf16[2,8,4,64,64]{4,3,2,1,0:T(8,128)(2,1)}, u32[]{:S(2)}) copy-start(bf16[2,8,4,64,64]{4,3,2,1,0:T(8,128)(2,1)} %copy-done.86) | copy-start | bytes 1572868
  1025.8 44.9 %collective-permute-start.5 = (bf16[4,8,4,64,64]{3,4,0,2,1:T(8,128)(2,1)}, bf16[4,8,4,64,64]{3,4,0,2,1:T(8,128)(2,1)}, u32[]{:S(2)}, u32[]{:S(2)}) collective-permute-start(bf16[4,8,4,64,64]{3,4,0,2,1:T(8,128)(2,1)} %multiply_convert_fusion), channel_id=1, source_target_pairs={{0,1},{1,2},{2,3},{3,4},{4,5},{5,6},{6,7},{7,8},{8,9},{9,10},{10,1... | collective-permute-start | bytes 3145736 | tf_op jit(solution)/shard_map/ppermute | solution.py:24
  1033.7 35.2 %collective-permute-start.6 = (bf16[2,8,4,64,64]{4,3,2,1,0:T(8,128)(2,1)S(1)}, bf16[2,8,4,64,64]{4,3,2,1,0:T(8,128)(2,1)S(1)}, u32[]{:S(2)}, u32[]{:S(2)}) collective-permute-start(bf16[2,8,4,64,64]{4,3,2,1,0:T(8,128)(2,1)S(1)} %fusion.66), channel_id=1, source_target_pairs={{0,1},{1,2},{2,3},{3,4},{4,5},{5,6},{6,7},{7,8},{8,9},{9,10},{10,1... | collective-permute-start | bytes 1572872 | tf_op jit(solution)/shard_map/ppermute | solution.py:24
  (245 other events, 1332.1 us)
where the time goes:
time: 1090 us; the launch traced here: 1080 us
  matrix products  640 us (59%)
  other arithmetic  240 us (22%)
  local copies, waits for them, and re-layouts  105 us (10%)
  waiting for transfers between devices  57.1 us (5%)
  starting transfers between devices  21.2 us (2%)
  between operations  17 us (2%)
    dot_general x128, matrix products, pair_work(): jnp.einsum('nzab,nzbc->nzac', part, moved[1], preferred_element_type=jnp....  205 us
    dot_general x128, matrix products, pair_work(): jnp.einsum('nzab,nzbc->nzac', part, moved[0], preferred_element_type=jnp....  135 us
    dot_general x8, matrix products, pair_work(): jnp.einsum('nzab,stnzbc->stnzac', env_left[0], vector, preferred_element_...  119 us
    dot_general x8, matrix products, pair_work(): jnp.einsum('nzab,stnzbc->stnzac', env_left[1], vector, preferred_element_...  111 us
    another operation x31, other arithmetic, pair_work(): applied = applied + jnp.stack(right_rows)  77.1 us
    reduce_sum x5, other arithmetic, pair_work(): jnp.sum(current * current)  65.1 us
    convert_element_type x5, other arithmetic, pair_work(): (current - STEP_SIZE * (applied - numerator / denominator * current)).ast...  62.8 us
    ppermute x7, waiting for transfers between devices, passed_along(): lax.ppermute(value, axis, [(source, source + steps) for source in range(l...  57.1 us
  transfers between devices with their start and end apart: 7, of which 2 were waited for; matrix products, arithmetic and copies ran while one was open for 49% of the time, Pallas kernels for 0%

commit v1 on v0

v1 whole, which is shorter than its diff:
```python
import functools

import jax
import jax.numpy as jnp
from jax import lax
from jax.experimental import pallas as pl
from jax.experimental.pallas import tpu as pltpu
from jax.sharding import PartitionSpec as P

NN = 8
NS = 4
BS = 64
PHYS = 4
ITERS = 4
NB = 32
CHARGE_NUMBER = (0, 1, 1, 2)
CHARGE_SPIN = (0, 1, -1, 0)
OCCUPANCY = (0.0, 1.0, 1.0, 2.0)
STEP_SIZE = 0.06
EPSILON = 1e-06
LN = PHYS * BS
UNROLL = 8
F32, BF16 = jnp.float32, jnp.bfloat16


def dot(a, b):
    return jnp.dot(a, b, preferred_element_type=F32)


def sector(q, number, spin):
    n = lax.rem(lax.div(q, NS) + number + NN, NN)
    z = lax.rem(lax.rem(q, NS) + spin + NS, NS)
    return n * NS + z


def plus(q, s):
    return sector(q, CHARGE_NUMBER[s], CHARGE_SPIN[s])


def minus(q, s):
    return sector(q, -CHARGE_NUMBER[s], -CHARGE_SPIN[s])


def bond_kernel(coup_ref, kept_ref, a_ref, b_ref, l_ref, r_ref, new_ref, env_ref, v, y, w, at):
    def weight_row(s1):
        lane = lax.broadcasted_iota(jnp.int32, (1, LN), 1)
        row = jnp.full((1, LN), coup_ref[s1, PHYS - 1], F32)
        for s2 in reversed(range(PHYS - 1)):
            row = jnp.where(lane < (s2 + 1) * BS, coup_ref[s1, s2], row)
        return row

    rows = [weight_row(s1) for s1 in range(PHYS)]
    rows16 = [row.astype(BF16) for row in rows]

    def build(q, _):
        zero = jnp.zeros((BS, BS), BF16)
        for ch in range(2):
            for s2 in range(PHYS):
                block = r_ref[ch, plus(q, s2)]
                parts = [block if t == s2 else zero for t in range(PHYS)]
                w[q, ch * LN + s2 * BS : ch * LN + (s2 + 1) * BS] = jnp.concatenate(parts, 1)
        for s1 in range(PHYS):
            at[q, :, s1 * BS : (s1 + 1) * BS] = a_ref[s1, minus(q, s1)].T
        cat = jnp.concatenate([b_ref[s2, q] for s2 in range(PHYS)], 1)
        for s1 in range(PHYS):
            p = minus(q, s1)
            v[s1, p] = dot(a_ref[s1, p], cat).astype(BF16)
        return 0

    lax.fori_loop(0, NB, build, 0, unroll=UNROLL)

    def fold(x):
        total = x[0:8]
        for i in range(1, BS // 8):
            total = total + x[i * 8 : (i + 1) * 8]
        return total

    quot = None
    for it in range(ITERS):

        def right(q, _, it=it, quot=quot):
            xs, cs = [], []
            for s1 in range(PHYS):
                p = minus(q, s1)
                if it:
                    old = v[s1, p].astype(F32)
                    x = (old - STEP_SIZE * (y[s1, p] - quot * old)).astype(BF16)
                    v[s1, p] = x
                else:
                    x = v[s1, p]
                xs.append(x)
                cs.append(x * rows16[s1])
            lhs = jnp.concatenate([jnp.concatenate(xs, 0), jnp.concatenate(cs, 0)], 1)
            out = dot(lhs, w[q])
            for s1 in range(PHYS):
                y[s1, minus(q, s1)] = out[s1 * BS : (s1 + 1) * BS]
            return 0

        lax.fori_loop(0, NB, right, 0, unroll=UNROLL)

        def left(q, carry):
            num, den = carry
            lhs = jnp.concatenate([l_ref[0, q], l_ref[1, q]], 1)
            for s1 in range(PHYS):
                x = v[s1, q]
                out = dot(lhs, jnp.concatenate([x, x * rows16[s1]], 0)) + y[s1, q]
                y[s1, q] = out
                wide = x.astype(F32)
                num = num + fold(wide * out)
                den = den + fold(wide * wide)
            return num, den

        zeros = jnp.zeros((8, LN), F32)
        num, den = lax.fori_loop(0, NB, left, (zeros, zeros), unroll=UNROLL)
        quot = jnp.sum(num, keepdims=True) / jnp.sum(den, keepdims=True)

    row_ids = lax.broadcasted_iota(jnp.int32, (BS, LN), 0)

    def project(p, total):
        parts = []
        for s1 in range(PHYS):
            q = minus(p, s1)
            old = v[s1, q].astype(F32)
            parts.append((old - STEP_SIZE * (y[s1, q] - quot * old)).astype(BF16))
        out = dot(at[p], jnp.concatenate(parts, 0))
        out = jnp.where(row_ids < kept_ref[0, p], out, 0.0)
        w2[p] = out
        return total + fold(out * out)

    w2 = y.at[0]

    def project_all(p, total):
        return project(p, total)

    total = lax.fori_loop(0, NB, project_all, jnp.zeros((8, LN), F32), unroll=UNROLL)
    factor = lax.rsqrt(jnp.sum(total, keepdims=True) / (PHYS * NB * BS * BS) + EPSILON)

    def finish(p, _):
        out = (w2[p] * factor).astype(BF16)
        for s2 in range(PHYS):
            new_ref[s2, p] = out[:, s2 * BS : (s2 + 1) * BS]
        e0, e1 = l_ref[0, p], l_ref[1, p]
        mixed = (e0.astype(F32) + e1.astype(F32)).astype(BF16)
        both = jnp.concatenate([mixed, e1], 1)
        for s1 in range(PHYS):
            t = plus(p, s1)
            half = dot(at[t, :, s1 * BS : (s1 + 1) * BS], both).astype(BF16)
            v[s1, t, :, : 2 * BS] = half
        return 0

    lax.fori_loop(0, NB, finish, 0, unroll=UNROLL)

    def grow(p, _):
        energy = jnp.concatenate([v[s, p, :, :BS] for s in range(PHYS)], 1)
        density = jnp.concatenate(
            [v[s, p, :, BS : 2 * BS] * BF16(OCCUPANCY[s]) for s in range(PHYS)], 1
        )
        stack = jnp.concatenate([a_ref[s, minus(p, s)] for s in range(PHYS)], 0)
        out = (dot(jnp.concatenate([energy, density], 0), stack) * (1.0 / (PHYS * BS))).astype(BF16)
        env_ref[0, p] = out[:BS]
        env_ref[1, p] = out[BS:]
        return 0

    lax.fori_loop(0, NB, grow, 0, unroll=UNROLL)


def bond(coupling, kept, a, b, left, right):
    vmem = pl.BlockSpec(memory_space=pltpu.VMEM)
    smem = pl.BlockSpec(memory_space=pltpu.SMEM)
    return pl.pallas_call(
        bond_kernel,
        out_shape=(
            jax.ShapeDtypeStruct((PHYS, NB, BS, BS), BF16),
            jax.ShapeDtypeStruct((2, NB, BS, BS), BF16),
        ),
        in_specs=[smem, smem, vmem, vmem, vmem, vmem],
        out_specs=(vmem, vmem),
        scratch_shapes=[
            pltpu.VMEM((PHYS, NB, BS, LN), BF16),
            pltpu.VMEM((PHYS, NB, BS, LN), F32),
            pltpu.VMEM((NB, 2 * LN, LN), BF16),
            pltpu.VMEM((NB, BS, LN), BF16),
        ],
        compiler_params=pltpu.CompilerParams(vmem_limit_bytes=60 * 2**20),
    )(coupling, kept, a, b, left, right)


def blocks(x):
    return x.reshape(x.shape[0], NB, BS, BS)


def flat(x):
    return x.reshape(x.shape[0], NB, BS * BS)


def shards(tensors, left_env, right_env, kept_rows, coupling):
    across = lax.axis_size("site")
    count = lax.axis_size("sec") * across
    position = lax.axis_index("sec") * across + lax.axis_index("site")
    axes = ("sec", "site")
    tensor, left, right = tensors[0], left_env[0], right_env[0]

    inward = [(i, i + 1) for i in range(0, count, 2)]
    back = [(i, i - 1) for i in range(2, count, 2)]
    ahead = [(i, i + 1) for i in range(1, count - 1, 2)]
    a1 = lax.ppermute(tensor, axes, inward)
    l1 = lax.ppermute(left, axes, inward)
    k1 = lax.ppermute(kept_rows, axes, inward)
    b2 = lax.ppermute(tensor, axes, back)
    r2 = lax.ppermute(right, axes, back)
    new1, env1 = bond(coupling, k1, blocks(a1), blocks(tensor), blocks(l1), blocks(right))
    new2, env2 = bond(coupling, kept_rows, new1, blocks(b2), env1, blocks(r2))
    got_new = lax.ppermute(flat(new2), axes, ahead)
    got_env = lax.ppermute(flat(env2), axes, ahead)
    odd = position % 2 == 1
    first = position == 0
    out_new = jnp.where(odd, flat(new1), jnp.where(first, tensor, got_new))
    out_env = jnp.where(odd, flat(env1), jnp.where(first, left, got_env))
    return out_new[None], out_env[None]


def solution(mesh):
    sites = P(("sec", "site"), None, None, None)
    return jax.shard_map(
        shards,
        mesh=mesh,
        in_specs=(sites, sites, sites, P(("sec", "site"), None), P()),
        out_specs=(sites, sites),
        check_vma=False,
    )
```

time: 1090 us -> 181 us (0.17)
  matrix products: 640 us -> 0 us
  other arithmetic: 240 us -> 4.53 us
  Pallas kernels: 0 us -> 111 us
  local copies, waits for them, and re-layouts: 105 us -> 29.5 us
  waiting for transfers between devices: 57.1 us -> 18.4 us
  between operations: 17 us -> 0.73 us
    dot_general x304 -> x0, matrix products: 640 us -> none  [the longest x128 205 us: pair_work(): jnp.einsum('nzab,nzbc->nzac', part, moved[1], preferred_element_type=jnp....]
    pallas_call x0 -> x2, Pallas kernels: none -> 111 us  [bond(): pl.pallas_call(bond_kernel, out_shape=(jax.ShapeDtypeStruct((PHYS, NB, BS...]
    convert_element_type x12 -> x0, other arithmetic: 78.8 us -> none  [the longest x5 62.8 us: pair_work(): (current - STEP_SIZE * (applied - numerator / denominator * current)).ast...]
    another operation x31 -> x0, other arithmetic: 77.1 us -> none  [pair_work(): applied = applied + jnp.stack(right_rows)]
    reduce_sum x5 -> x0, other arithmetic: 65.1 us -> none  [pair_work(): jnp.sum(current * current)]
    slice x59 -> x0, local copies, waits for them, and re-layouts: 51.4 us -> none  [the longest x56 47.4 us: move_sectors(): return jnp.roll(source, (by_number, by_spin), axis=(-4, -3))]
    ppermute x7, waiting for transfers between devices: 57.1 us -> 18.4 us  [the longest x1 9.96 us: shards(): got_new = lax.ppermute(flat(new2), axes, ahead)]
    reshape x0 -> x8, local copies, waits for them, and re-layouts: none -> 22.7 us  [the longest x4 11.4 us: blocks(): return x.reshape(x.shape[0], NB, BS, BS)]
  transfers between devices with their start and end apart: 7 -> 7, of which waited for: 2 -> 3; matrix products, arithmetic and copies ran while one was open for 49% -> 16% of each run, Pallas kernels for 0% -> 0%
where the time goes in v1:
time: 181 us
  Pallas kernels  111 us (61%)
  local copies, waits for them, and re-layouts  29.5 us (16%)
  waiting for transfers between devices  18.4 us (10%)
  starting transfers between devices  16.8 us (9%)
  other arithmetic  4.53 us (3%)
    pallas_call x2, Pallas kernels, bond(): pl.pallas_call(bond_kernel, out_shape=(jax.ShapeDtypeStruct((PHYS, NB, BS...  111 us
    reshape x4, local copies, waits for them, and re-layouts, blocks(): return x.reshape(x.shape[0], NB, BS, BS)  11.4 us
    reshape x4, local copies, waits for them, and re-layouts, flat(): return x.reshape(x.shape[0], NB, BS * BS)  11.3 us
    ppermute x1, waiting for transfers between devices, shards(): got_new = lax.ppermute(flat(new2), axes, ahead)  9.96 us
    ppermute x1, starting transfers between devices, shards(): b2 = lax.ppermute(tensor, axes, back)  7.65 us
    another operation x2, local copies, waits for them, and re-layouts, blocks(): return x.reshape(x.shape[0], NB, BS, BS)  6.34 us
    broadcast_in_dim x2, other arithmetic, shards(): return (out_new[None], out_env[None])  4.53 us
    ppermute x1, waiting for transfers between devices, shards(): r2 = lax.ppermute(right, axes, back)  4.36 us
  transfers between devices with their start and end apart: 7, of which 3 were waited for; matrix products, arithmetic and copies ran while one was open for 16% of the time, Pallas kernels for 0%

profile of v1, /device:TPU:6, one launch (start us, length us, event | category | flops | bytes accessed | tf_op | source)
XLA Modules:
  0.0 180.6 jit_solution(5218554089850181093)
XLA Ops:
  0.6 1.9 %collective-permute-start.1 = (bf16[4,32,4096]{2,1,0:T(8,128)(2,1)}, bf16[4,32,4096]{2,1,0:T(8,128)(2,1)S(1)}, u32[]{:S(2)}, u32[]{:S(2)}) collective-permute-start(bf16[4,32,4096]{2,1,0:T(8,128)(2,1)} %bitcast.21), channel_id=1, source_target_pairs={{0,1},{2,3},{4,5},{6,7},{8,9},{10,11},{12,13},{14,15},{16,17},{18,... | collective-permute-start | bytes 3145736 | tf_op jit(solution)/shard_map/ppermute | solution.py:206
  2.6 7.7 %collective-permute-start.3 = (bf16[4,32,4096]{2,1,0:T(8,128)(2,1)}, bf16[4,32,4096]{2,1,0:T(8,128)(2,1)S(1)}, u32[]{:S(2)}, u32[]{:S(2)}) collective-permute-start(bf16[4,32,4096]{2,1,0:T(8,128)(2,1)} %bitcast.22), channel_id=1, source_target_pairs={{2,1},{4,3},{6,5},{8,7},{10,9},{12,11},{14,13},{16,15},{18,17},{20... | collective-permute-start | bytes 3145736 | tf_op jit(solution)/shard_map/ppermute | solution.py:209
  10.2 2.1 %collective-permute-start.2 = (bf16[2,32,4096]{2,1,0:T(8,128)(2,1)}, bf16[2,32,4096]{2,1,0:T(8,128)(2,1)}, u32[]{:S(2)}, u32[]{:S(2)}) collective-permute-start(bf16[2,32,4096]{2,1,0:T(8,128)(2,1)} %bitcast.24), channel_id=1, source_target_pairs={{0,1},{2,3},{4,5},{6,7},{8,9},{10,11},{12,13},{14,15},{16,17},{18,... | collective-permute-start | bytes 1572872 | tf_op jit(solution)/shard_map/ppermute | solution.py:207
  12.3 1.3 collective-permute-start.4
  13.7 1.3 collective-permute-start
  15.0 4.2 %reshape_squeeze.6.b_ref = bf16[4,32,64,64]{3,2,1,0:T(8,128)(2,1)} reshape(bf16[1,4,32,4096]{3,2,1,0:T(8,128)(2,1)} %param.5) | data formatting | bytes 2097152 | tf_op jit(solution)/shard_map/reshape;squeeze | solution.py:189
  19.2 2.1 %reshape_squeeze.7.r_ref = bf16[2,32,64,64]{3,2,1,0:T(8,128)(2,1)} reshape(bf16[1,2,32,4096]{3,2,1,0:T(8,128)(2,1)S(1)} %copy-done.4) | data formatting | bytes 1048576 | tf_op jit(solution)/shard_map/reshape;squeeze | solution.py:189
  21.3 2.7 %reshape.29.l_ref = bf16[2,32,64,64]{3,2,1,0:T(8,128)(2,1)} reshape(bf16[2,32,4096]{2,1,0:T(8,128)(2,1)} %collective-permute-done.2) | data formatting | bytes 1048576 | tf_op jit(solution)/shard_map/reshape | solution.py:189
  24.0 4.4 %collective-permute-done.4 = bf16[2,32,4096]{2,1,0:T(8,128)(2,1)S(1)} collective-permute-done((bf16[2,32,4096]{2,1,0:T(8,128)(2,1)}, bf16[2,32,4096]{2,1,0:T(8,128)(2,1)S(1)}, u32[]{:S(2)}, u32[]{:S(2)}) %collective-permute-start.4) | collective-permute-done | bytes 524320 | tf_op jit(solution)/shard_map/ppermute | solution.py:210
  28.4 2.1 %reshape.32.r_ref = bf16[2,32,64,64]{3,2,1,0:T(8,128)(2,1)} reshape(bf16[2,32,4096]{2,1,0:T(8,128)(2,1)S(1)} %collective-permute-done.4) | data formatting | bytes 1048576 | tf_op jit(solution)/shard_map/reshape | solution.py:189
  30.5 3.3 %reshape.28.a_ref = bf16[4,32,64,64]{3,2,1,0:T(8,128)(2,1)} reshape(bf16[4,32,4096]{2,1,0:T(8,128)(2,1)S(1)} %collective-permute-done.1) | data formatting | bytes 2097152 | tf_op jit(solution)/shard_map/reshape | solution.py:189
  33.8 3.3 %reshape.31.b_ref = bf16[4,32,64,64]{3,2,1,0:T(8,128)(2,1)} reshape(bf16[4,32,4096]{2,1,0:T(8,128)(2,1)S(1)} %collective-permute-done.3) | data formatting | bytes 2097152 | tf_op jit(solution)/shard_map/reshape | solution.py:189
  37.6 55.4 %shard_map.68 = (bf16[4,32,64,64]{3,2,1,0:T(8,128)(2,1)}, bf16[2,32,64,64]{3,2,1,0:T(8,128)(2,1)}) custom-call(f32[4,4]{1,0:T(4,128)} %coup_ref.3, s32[1,32]{1,0:T(1,128)} %copy-done.5, bf16[4,32,64,64]{3,2,1,0:T(8,128)(2,1)} %reshape.28.a_ref, bf16[4,32,64,64]{3,2,1,0:T(8,128)(2,1)} %reshape_squeeze.6.b_ref, bf16[2,32,64,64]{3,2,1,0:T(8,128)(2,1)} %reshape.29.l_ref, ...), custom_call_target="tpu_custom_call" | custom-call | tf_op jit(solution)/shard_map/pallas_call | solution.py:170
  93.0 55.2 %shard_map.69 = (bf16[4,32,64,64]{3,2,1,0:T(8,128)(2,1)}, bf16[2,32,64,64]{3,2,1,0:T(8,128)(2,1)}) custom-call(f32[4,4]{1,0:T(4,128)} %coup_ref.3, s32[1,32]{1,0:T(1,128)} %kept_ref.1, bf16[4,32,64,64]{3,2,1,0:T(8,128)(2,1)} %get-tuple-element.6.a_ref, bf16[4,32,64,64]{3,2,1,0:T(8,128)(2,1)} %reshape.31.b_ref, ...), custom_call_target="tpu_custom_call" | custom-call | tf_op jit(solution)/shard_map/pallas_call | solution.py:170
  148.2 2.9 %reshape.35 = bf16[2,32,4096]{2,1,0:T(8,128)(2,1)} reshape(bf16[2,32,64,64]{3,2,1,0:T(8,128)(2,1)} %get-tuple-element.9) | data formatting | bytes 1048576 | tf_op jit(solution)/shard_map/reshape | solution.py:193
  151.1 1.3 collective-permute-start.6
  152.4 4.3 %reshape.33 = bf16[4,32,4096]{2,1,0:T(8,128)(2,1)} reshape(bf16[4,32,64,64]{3,2,1,0:T(8,128)(2,1)} %get-tuple-element.8) | data formatting | bytes 2097152 | tf_op jit(solution)/shard_map/reshape | solution.py:193
  156.7 1.3 collective-permute-start.5
  158.0 1.6 reshape.34
  159.6 2.5 %reshape.30 = bf16[4,32,4096]{2,1,0:T(8,128)(2,1)} reshape(bf16[4,32,64,64]{3,2,1,0:T(8,128)(2,1)S(1)} %copy-done) | data formatting | bytes 2097152 | tf_op jit(solution)/shard_map/reshape | solution.py:193
  162.1 4.0 %collective-permute-done.6 = bf16[2,32,4096]{2,1,0:T(8,128)(2,1)} collective-permute-done((bf16[2,32,4096]{2,1,0:T(8,128)(2,1)}, bf16[2,32,4096]{2,1,0:T(8,128)(2,1)}, u32[]{:S(2)}, u32[]{:S(2)}) %collective-permute-start.6) | collective-permute-done | bytes 524320 | tf_op jit(solution)/shard_map/ppermute | solution.py:214
  166.1 2.1 %select_bitcast_fusion.1 = bf16[1,2,32,4096]{3,2,1,0:T(8,128)(2,1)} fusion(bf16[2,32,4096]{2,1,0:T(8,128)(2,1)} %reshape.34, bf16[2,32,4096]{2,1,0:T(8,128)(2,1)} %collective-permute-done.6, pred[]{:T(512)S(6)} %eq.9, pred[]{:T(512)S(6)} %eq.8, bf16[1,2,32,4096]{3,2,1,0:T(8,128)(2,1)} %param.6), kind=kLoop, calls=%fused_computation.1 | loop fusion | flops 524288 | bytes 2097154 | tf_op jit(solution)/shard_map/broadcast_in_dim | solution.py:219
  168.2 10.0 %collective-permute-done.5 = bf16[4,32,4096]{2,1,0:T(8,128)(2,1)} collective-permute-done((bf16[4,32,4096]{2,1,0:T(8,128)(2,1)}, bf16[4,32,4096]{2,1,0:T(8,128)(2,1)}, u32[]{:S(2)}, u32[]{:S(2)}) %collective-permute-start.5) | collective-permute-done | bytes 1048608 | tf_op jit(solution)/shard_map/ppermute | solution.py:213
  178.1 2.5 %select_bitcast_fusion = bf16[1,4,32,4096]{3,2,1,0:T(8,128)(2,1)} fusion(bf16[4,32,4096]{2,1,0:T(8,128)(2,1)S(1)} %copy-done.2, bf16[4,32,4096]{2,1,0:T(8,128)(2,1)} %collective-permute-done.5, pred[]{:T(512)S(6)} %eq.9, pred[]{:T(512)S(6)} %eq.8, bf16[1,4,32,4096]{3,2,1,0:T(8,128)(2,1)S(1)} %copy-done.1), kind=kLoop, calls=%fused_computation | loop fusion | flops 1048576 | bytes 4194306 | tf_op jit(solution)/shard_map/broadcast_in_dim | solution.py:219
  (16 shorter events, 0.5 us)
Async XLA Ops:
  0.6 18.6 %copy-start.4 = (bf16[1,2,32,4096]{3,2,1,0:T(8,128)(2,1)S(1)}, bf16[1,2,32,4096]{3,2,1,0:T(8,128)(2,1)}, u32[]{:S(2)}) copy-start(bf16[1,2,32,4096]{3,2,1,0:T(8,128)(2,1)} %param.7) | copy-start | bytes 1572868
  0.6 29.9 %collective-permute-start.1 = (bf16[4,32,4096]{2,1,0:T(8,128)(2,1)}, bf16[4,32,4096]{2,1,0:T(8,128)(2,1)S(1)}, u32[]{:S(2)}, u32[]{:S(2)}) collective-permute-start(bf16[4,32,4096]{2,1,0:T(8,128)(2,1)} %bitcast.21), channel_id=1, source_target_pairs={{0,1},{2,3},{4,5},{6,7},{8,9},{10,11},{12,13},{14,15},{16,17},{18,... | collective-permute-start | bytes 3145736 | tf_op jit(solution)/shard_map/ppermute | solution.py:206
  2.6 31.2 %collective-permute-start.3 = (bf16[4,32,4096]{2,1,0:T(8,128)(2,1)}, bf16[4,32,4096]{2,1,0:T(8,128)(2,1)S(1)}, u32[]{:S(2)}, u32[]{:S(2)}) collective-permute-start(bf16[4,32,4096]{2,1,0:T(8,128)(2,1)} %bitcast.22), channel_id=1, source_target_pairs={{2,1},{4,3},{6,5},{8,7},{10,9},{12,11},{14,13},{16,15},{18,17},{20... | collective-permute-start | bytes 3145736 | tf_op jit(solution)/shard_map/ppermute | solution.py:209
  10.2 11.1 %collective-permute-start.2 = (bf16[2,32,4096]{2,1,0:T(8,128)(2,1)}, bf16[2,32,4096]{2,1,0:T(8,128)(2,1)}, u32[]{:S(2)}, u32[]{:S(2)}) collective-permute-start(bf16[2,32,4096]{2,1,0:T(8,128)(2,1)} %bitcast.24), channel_id=1, source_target_pairs={{0,1},{2,3},{4,5},{6,7},{8,9},{10,11},{12,13},{14,15},{16,17},{18,... | collective-permute-start | bytes 1572872 | tf_op jit(solution)/shard_map/ppermute | solution.py:207
  12.3 16.1 %collective-permute-start.4 = (bf16[2,32,4096]{2,1,0:T(8,128)(2,1)}, bf16[2,32,4096]{2,1,0:T(8,128)(2,1)S(1)}, u32[]{:S(2)}, u32[]{:S(2)}) collective-permute-start(bf16[2,32,4096]{2,1,0:T(8,128)(2,1)} %bitcast.23), channel_id=1, source_target_pairs={{2,1},{4,3},{6,5},{8,7},{10,9},{12,11},{14,13},{16,15},{18,17},{20... | collective-permute-start | bytes 1572872 | tf_op jit(solution)/shard_map/ppermute | solution.py:210
  13.7 23.4 %collective-permute-start = (s32[1,32]{1,0:T(1,128)}, s32[1,32]{1,0:T(1,128)S(1)}, u32[]{:S(2)}, u32[]{:S(2)}) collective-permute-start(s32[1,32]{1,0:T(1,128)} %kept_ref.1), channel_id=1, source_target_pairs={{0,1},{2,3},{4,5},{6,7},{8,9},{10,11},{12,13},{14,15},{16,17},{18,... | collective-permute-start | bytes 392 | tf_op jit(solution)/shard_map/ppermute | solution.py:208
  37.1 0.5 copy-start.5
  148.2 9.8 %copy-start.3 = (bf16[2,32,64,64]{3,2,1,0:T(8,128)(2,1)S(1)}, bf16[2,32,64,64]{3,2,1,0:T(8,128)(2,1)}, u32[]{:S(2)}) copy-start(bf16[2,32,64,64]{3,2,1,0:T(8,128)(2,1)} %get-tuple-element.7.l_ref) | copy-start | bytes 1572868
  151.1 15.0 %collective-permute-start.6 = (bf16[2,32,4096]{2,1,0:T(8,128)(2,1)}, bf16[2,32,4096]{2,1,0:T(8,128)(2,1)}, u32[]{:S(2)}, u32[]{:S(2)}) collective-permute-start(bf16[2,32,4096]{2,1,0:T(8,128)(2,1)} %reshape.35), channel_id=1, source_target_pairs={{1,2},{3,4},{5,6},{7,8},{9,10},{11,12},{13,14},{15,16},{17,18},{19... | collective-permute-start | bytes 1572872 | tf_op jit(solution)/shard_map/ppermute | solution.py:214
  152.4 7.2 %copy-start = (bf16[4,32,64,64]{3,2,1,0:T(8,128)(2,1)S(1)}, bf16[4,32,64,64]{3,2,1,0:T(8,128)(2,1)}, u32[]{:S(2)}) copy-start(bf16[4,32,64,64]{3,2,1,0:T(8,128)(2,1)} %get-tuple-element.6.a_ref) | copy-start | bytes 3145732
  156.7 21.4 %collective-permute-start.5 = (bf16[4,32,4096]{2,1,0:T(8,128)(2,1)}, bf16[4,32,4096]{2,1,0:T(8,128)(2,1)}, u32[]{:S(2)}, u32[]{:S(2)}) collective-permute-start(bf16[4,32,4096]{2,1,0:T(8,128)(2,1)} %reshape.33), channel_id=1, source_target_pairs={{1,2},{3,4},{5,6},{7,8},{9,10},{11,12},{13,14},{15,16},{17,18},{19... | collective-permute-start | bytes 3145736 | tf_op jit(solution)/shard_map/ppermute | solution.py:213
  159.6 18.5 %copy-start.1 = (bf16[1,4,32,4096]{3,2,1,0:T(8,128)(2,1)S(1)}, bf16[1,4,32,4096]{3,2,1,0:T(8,128)(2,1)}, u32[]{:S(2)}) copy-start(bf16[1,4,32,4096]{3,2,1,0:T(8,128)(2,1)} %param.5) | copy-start | bytes 3145732
  162.1 16.1 %copy-start.2 = (bf16[4,32,4096]{2,1,0:T(8,128)(2,1)S(1)}, bf16[4,32,4096]{2,1,0:T(8,128)(2,1)}, u32[]{:S(2)}) copy-start(bf16[4,32,4096]{2,1,0:T(8,128)(2,1)} %reshape.30) | copy-start | bytes 3145732

commit v2 on v1

v2 whole, which is shorter than its diff:
```python
import functools

import jax
import jax.numpy as jnp
from jax import lax
from jax.experimental import pallas as pl
from jax.experimental.pallas import tpu as pltpu
from jax.sharding import PartitionSpec as P

NN = 8
NS = 4
BS = 64
PHYS = 4
ITERS = 4
NB = 32
FLAT = BS * BS
CHARGE_NUMBER = (0, 1, 1, 2)
CHARGE_SPIN = (0, 1, -1, 0)
OCCUPANCY = (0.0, 1.0, 1.0, 2.0)
STEP_SIZE = 0.06
EPSILON = 1e-06
HALF = PHYS // 2
LN = HALF * BS
F32, BF16 = jnp.float32, jnp.bfloat16
LIMIT = 28 * 2**20
VM = pl.BlockSpec(memory_space=pltpu.VMEM)
SM = pl.BlockSpec(memory_space=pltpu.SMEM)
HB = pl.BlockSpec(memory_space=pl.ANY)


def dot(a, b):
    return jnp.dot(a, b, preferred_element_type=F32)


def sector(q, number, spin):
    return (q // NS + number) % NN * NS + (q % NS + spin) % NS


def plus(q, s):
    return sector(q, CHARGE_NUMBER[s], CHARGE_SPIN[s])


def minus(q, s):
    return sector(q, -CHARGE_NUMBER[s], -CHARGE_SPIN[s])


def fold(x):
    total = x[0:8]
    for i in range(1, BS // 8):
        total = total + x[i * 8 : (i + 1) * 8]
    return total


def scaled_copy(src, factor):
    return (src.astype(F32) * factor).astype(BF16)


def krylov_kernel(second, core_of, *refs):
    if second:
        coup, kept, own, got, b_even, b_odd, r_even, r_odd, left_raw = refs[:9]
        outs = refs[9:14]
        scratch = refs[14:]
    else:
        coup, kept, own, got, own_l, got_l, own_r, got_r = refs[:8]
        outs = refs[8:14]
        scratch = refs[14:]
    u, last, small, at, a_flat = outs[:5]
    a_raw, ab, lb, rb, bcat, w, sems, moments, b_raw, r_raw = scratch
    y = last
    core = core_of()

    if not second:
        left_raw = outs[5]

    def moves(odd):
        if second:
            mine = HALF if odd else 0
            pairs = [
                (own, a_raw.at[pl.ds(mine, HALF)]),
                (got, a_raw.at[pl.ds(HALF - mine, HALF)]),
                (b_odd if odd else b_even, b_raw),
                (r_odd if odd else r_even, r_raw),
            ]
        else:
            t_a, t_b = (got, own) if odd else (own, got)
            pairs = [
                (t_a, a_raw),
                (t_b.at[pl.ds(HALF if odd else 0, HALF)], b_raw),
                (got_l if odd else own_l, left_raw),
                (own_r if odd else got_r, r_raw),
            ]
        return [pltpu.make_async_copy(x, z, sems.at[i]) for i, (x, z) in enumerate(pairs)]

    for odd in (False, True):

        @pl.when(core == int(odd))
        def _(odd=odd):
            for copy in moves(odd):
                copy.start()
            for copy in moves(odd):
                copy.wait()

    lane = lax.broadcasted_iota(jnp.int32, (1, LN), 1)
    rows16 = [
        jnp.where(lane < BS, coup[s1, core * HALF], coup[s1, core * HALF + 1]).astype(BF16)
        for s1 in range(PHYS)
    ]

    for ch in range(2):
        rb[...] = r_raw[ch].reshape(NB, BS, BS)
        for q in range(NB):
            for h in range(HALF):
                low, high = plus(q, h), plus(q, HALF + h)
                block = rb[low + core * (high - low)]
                zero = jnp.zeros((BS, BS), BF16)
                parts = [block, zero] if h == 0 else [zero, block]
                w[q, ch * LN + h * BS : ch * LN + (h + 1) * BS] = jnp.concatenate(parts, 1)
    for ch in range(2):
        lb[:, :, ch * BS : (ch + 1) * BS] = left_raw[ch].reshape(NB, BS, BS)
    for h in range(HALF):
        bcat[:, :, h * BS : (h + 1) * BS] = b_raw[h].reshape(NB, BS, BS)

    if second:
        total = jnp.zeros((8, 128), F32)
        for s in range(PHYS):
            for t in range(FLAT // 128):
                x = a_raw[s, :, t * 128 : (t + 1) * 128].astype(F32)
                x = x * x
                total = total + (x[0:8] + x[8:16]) + (x[16:24] + x[24:32])
        factor = lax.rsqrt(jnp.sum(total, keepdims=True) / (PHYS * NB * FLAT) + EPSILON)
    for s in range(PHYS):
        x = a_raw[s]
        if second:
            x = scaled_copy(x, factor)
        a_flat[s] = x
        ab[s] = x.reshape(NB, BS, BS)

    for q in range(NB):
        for s1 in range(PHYS):
            at[q, :, s1 * BS : (s1 + 1) * BS] = ab[s1, minus(q, s1)].T
        lhs = jnp.concatenate([ab[s1, minus(q, s1)] for s1 in range(PHYS)], 0)
        out = dot(lhs, bcat[q]).astype(BF16)
        for s1 in range(PHYS):
            u[0, s1, minus(q, s1)] = out[s1 * BS : (s1 + 1) * BS]

    def product(it, _):
        now, later = u.at[it], u.at[it + 1]
        for q in range(NB):
            x = jnp.concatenate([now[s1, minus(q, s1)] for s1 in range(PHYS)], 0)
            c = jnp.concatenate([now[s1, minus(q, s1)] * rows16[s1] for s1 in range(PHYS)], 0)
            out = dot(jnp.concatenate([x, c], 1), w[q])
            for s1 in range(PHYS):
                y[s1, minus(q, s1)] = out[s1 * BS : (s1 + 1) * BS]
        even = jnp.zeros((8, LN), F32)
        odd = jnp.zeros((8, LN), F32)
        for q in range(NB):
            for pair in range(PHYS // 2):
                xs = [now[pair * 2 + j, q] for j in range(2)]
                cs = [xs[j] * rows16[pair * 2 + j] for j in range(2)]
                rhs = jnp.concatenate([jnp.concatenate(xs, 1), jnp.concatenate(cs, 1)], 0)
                out = dot(lb[q], rhs)
                for j in range(2):
                    s1 = pair * 2 + j
                    old = xs[j].astype(F32)
                    new = old - STEP_SIZE * (out[:, j * LN : (j + 1) * LN] + y[s1, q])
                    y[s1, q] = new
                    later[s1, q] = new.astype(BF16)
                    even = even + fold(old * old)
                    odd = odd + fold(old * new)
        moments[2 * it] = even
        moments[2 * it + 1] = odd
        return 0

    lax.fori_loop(0, ITERS, product, 0)

    row = lax.broadcasted_iota(jnp.int32, (8, 128), 0)
    column = lax.broadcasted_iota(jnp.int32, (8, 128), 1)
    out = jnp.zeros((8, 128), F32)
    for k in range(2 * ITERS):
        out = jnp.where((row == 0) & (column == k), jnp.sum(moments[k], keepdims=True), out)
    for q in range(NB):
        out = jnp.where((row == 1) & (column == q), kept[0, q].astype(F32), out)
    small[...] = out


def project_kernel(owner, core_of, own, got, u, last, at, x_out, v, xb):
    core = core_of()
    mine, other = own[...], got[...]
    both = mine + other
    row = lax.broadcasted_iota(jnp.int32, (8, 128), 0)
    column = lax.broadcasted_iota(jnp.int32, (8, 128), 1)

    def entry(array, r, c):
        return jnp.sum(jnp.where((row == r) & (column == c), array, 0.0), keepdims=True)

    t = [entry(both, 0, k) for k in range(2 * ITERS)]
    a = [jnp.ones((1, 1), F32)]
    for it in range(ITERS):
        den = sum(a[k] * a[j] * t[k + j] for k in range(it + 1) for j in range(it + 1))
        num = sum(a[k] * a[j] * t[k + j + 1] for k in range(it + 1) for j in range(it + 1))
        delta = 1.0 - num / den
        a = (
            [delta * a[0]]
            + [a[k - 1] + delta * a[k] for k in range(1, it + 1)]
            + [a[it]]
        )
    kept = jnp.where(core == owner, mine, other)
    row_ids = lax.broadcasted_iota(jnp.int32, (BS, LN), 0).astype(F32)
    for p in range(NB):
        parts = []
        for s1 in range(PHYS):
            q = minus(p, s1)
            total = last[s1, q]
            for k in range(ITERS):
                total = total + a[k] * u[k, s1, q].astype(F32)
            parts.append(total.astype(BF16))
        out = dot(at[p], jnp.concatenate(parts, 0))
        out = jnp.where(row_ids < entry(kept, 1, p), out, 0.0).astype(BF16)
        for h in range(HALF):
            xb[h, p] = out[:, h * BS : (h + 1) * BS]
    for h in range(HALF):
        x_out[h] = xb[h].reshape(NB, FLAT)


def env_kernel(a_flat, left, at, env, ab, lb, hb, eb):
    for s in range(PHYS):
        ab[s] = a_flat[s].reshape(NB, BS, BS)
    mixed = (left[0].astype(F32) + left[1].astype(F32)).astype(BF16)
    lb[:, :, :BS] = mixed.reshape(NB, BS, BS)
    lb[:, :, BS:] = left[1].reshape(NB, BS, BS)
    for q in range(NB):
        lhs = jnp.concatenate(
            [at[plus(q, s), :, s * BS : (s + 1) * BS] for s in range(PHYS)], 0
        )
        out = dot(lhs, lb[q]).astype(BF16)
        for s in range(PHYS):
            hb[s, q] = out[s * BS : (s + 1) * BS]
    for p in range(NB):
        halves = [hb[s, minus(p, s)] for s in range(PHYS)]
        energy = jnp.concatenate([half[:, :BS] for half in halves], 1)
        density = jnp.concatenate(
            [half[:, BS:] * BF16(OCCUPANCY[s]) for s, half in enumerate(halves)], 1
        )
        stack = jnp.concatenate([ab[s, minus(p, s)] for s in range(PHYS)], 0)
        out = dot(jnp.concatenate([energy, density], 0), stack) * (1.0 / (PHYS * BS))
        out = out.astype(BF16)
        eb[0, p] = out[:BS]
        eb[1, p] = out[BS:]
    for ch in range(2):
        env[ch] = eb[ch].reshape(NB, FLAT)


def shape(*dims, dtype=BF16):
    return jax.ShapeDtypeStruct(dims, dtype)


def params():
    return pltpu.CompilerParams(vmem_limit_bytes=LIMIT)


def krylov(core_of, second, coupling, kept, *arrays):
    outs = [
        shape(ITERS + 1, PHYS, NB, BS, LN),
        shape(PHYS, NB, BS, LN, dtype=F32),
        shape(8, 128, dtype=F32),
        shape(NB, BS, PHYS * BS),
        shape(PHYS, NB, FLAT),
    ]
    if not second:
        outs.append(shape(2, NB, FLAT))
    scratch = [
        pltpu.VMEM((PHYS, NB, FLAT), BF16),
        pltpu.VMEM((PHYS, NB, BS, BS), BF16),
        pltpu.VMEM((NB, BS, 2 * BS), BF16),
        pltpu.VMEM((NB, BS, BS), BF16),
        pltpu.VMEM((NB, BS, LN), BF16),
        pltpu.VMEM((NB, 2 * LN, LN), BF16),
        pltpu.SemaphoreType.DMA((4,)),
        pltpu.VMEM((2 * ITERS, 8, LN), F32),
        pltpu.VMEM((HALF, NB, FLAT), BF16),
        pltpu.VMEM((2, NB, FLAT), BF16),
    ]
    if second:
        specs = [SM, SM] + [HB] * 6 + [VM]
    else:
        specs = [SM, SM] + [HB] * 6
    return pl.pallas_call(
        functools.partial(krylov_kernel, second, core_of),
        out_shape=tuple(outs),
        in_specs=specs,
        out_specs=(VM,) * len(outs),
        scratch_shapes=scratch,
        compiler_params=params(),
        cost_estimate=pl.CostEstimate(flops=10**10, bytes_accessed=2**24, transcendentals=0),
        name="krylov",
    )(coupling, kept, *arrays)


def project(core_of, owner, own, got, u, last, at):
    return pl.pallas_call(
        functools.partial(project_kernel, owner, core_of),
        out_shape=shape(HALF, NB, FLAT),
        in_specs=[VM] * 5,
        out_specs=VM,
        scratch_shapes=[
            pltpu.VMEM((8, 128), F32),
            pltpu.VMEM((HALF, NB, BS, BS), BF16),
        ],
        compiler_params=params(),
        cost_estimate=pl.CostEstimate(flops=10**9, bytes_accessed=2**24, transcendentals=0),
        name="project",
    )(own, got, u, last, at)


def grow(a_flat, left, at):
    return pl.pallas_call(
        env_kernel,
        out_shape=shape(2, NB, FLAT),
        in_specs=[VM] * 3,
        out_specs=VM,
        scratch_shapes=[
            pltpu.VMEM((PHYS, NB, BS, BS), BF16),
            pltpu.VMEM((NB, BS, 2 * BS), BF16),
            pltpu.VMEM((PHYS, NB, BS, 2 * BS), BF16),
            pltpu.VMEM((2, NB, BS, BS), BF16),
        ],
        compiler_params=params(),
        cost_estimate=pl.CostEstimate(flops=10**9, bytes_accessed=2**22, transcendentals=0),
        name="grow",
    )(a_flat, left, at)


def core_index():
    return lax.rem(lax.axis_index("site"), 2)


def shards(tensors, left_env, right_env, kept_rows, coupling):
    across = lax.axis_size("site")
    count = lax.axis_size("sec") * across
    position = lax.axis_index("sec") * across + lax.axis_index("site")
    axes = ("sec", "site")
    tensor, left, right = tensors[0], left_env[0], right_env[0]

    swap = [(i, i ^ 1) for i in range(count)]
    rise = [(i, i + 1) for i in range(0, count, 2)]
    fall = [(i + 1, i) for i in range(0, count, 2)]
    to_even = [(i, i - 2) for i in range(2, count, 2)]
    to_odd = [(i, i - 1) for i in range(2, count, 2)]
    from_even = [(i, i + 2) for i in range(0, count - 2, 2)]
    from_odd = [(i, i + 1) for i in range(1, count - 2, 2)]

    def send(x, pairs):
        return lax.ppermute(x, axes, pairs)

    got_t = send(tensor, swap)
    got_l = send(left, rise)
    got_r = send(right, fall)
    late_t, late_r, got_t, got_l, got_r = lax.optimization_barrier(
        (tensor, right, got_t, got_l, got_r)
    )
    b_even = send(late_t[:HALF], to_even)
    r_even = send(late_r, to_even)
    b_odd = send(late_t[HALF:], to_odd)
    r_odd = send(late_r, to_odd)

    u, last, small, at, a_flat, l_flat = krylov(
        core_index, False, coupling, kept_rows, tensor, got_t, left, got_l, right, got_r
    )
    got_small = send(small, swap)
    env1 = grow(a_flat, l_flat, at)
    x = project(core_index, 0, small, got_small, u, last, at)
    got_x = send(x, swap)

    u, last, small, at, new1 = krylov(
        core_index, True, coupling, kept_rows, x, got_x, b_even, b_odd, r_even, r_odd, env1
    )
    got_small = send(small, swap)
    env2 = grow(new1, env1, at)
    x = project(core_index, 1, small, got_small, u, last, at)
    low = send(x, from_even)
    high = send(x, from_odd)
    got_env = send(env2, from_odd)

    squares = jnp.sum(jnp.square(low.astype(F32))) + jnp.sum(jnp.square(high.astype(F32)))
    factor = lax.rsqrt(squares / (PHYS * NB * FLAT) + EPSILON)
    received = scaled_copy(jnp.concatenate([low, high], 0), factor)
    odd = position % 2 == 1
    first = position == 0
    out_new = jnp.where(odd, new1, jnp.where(first, tensor, received))
    out_env = jnp.where(odd, env1, jnp.where(first, left, got_env))
    return out_new[None], out_env[None]


def solution(mesh):
    sites = P(("sec", "site"), None, None, None)
    return jax.shard_map(
        shards,
        mesh=mesh,
        in_specs=(sites, sites, sites, P(("sec", "site"), None), P()),
        out_specs=(sites, sites),
        check_vma=False,
    )
```

time: 181 us -> 120 us (0.66)
  Pallas kernels: 111 us -> 48.9 us
  local copies, waits for them, and re-layouts: 29.5 us -> 17 us
  starting transfers between devices: 16.8 us -> 26.1 us
  waiting for transfers between devices: 18.4 us -> 20.7 us
    pallas_call x2 -> x6, Pallas kernels: 111 us -> 48.9 us  [the longest x2 34.8 us: krylov(): pl.pallas_call(functools.partial(krylov_kernel, second, core_of), out_sha...]
    reshape x8 -> x0, local copies, waits for them, and re-layouts: 22.7 us -> none  [the longest x4 11.4 us: blocks(): return x.reshape(x.shape[0], NB, BS, BS)]
    unnamed x12 -> x28, local copies, waits for them, and re-layouts: 0.53 us -> 16.9 us
    ppermute x7 -> x13, starting transfers between devices: 16.8 us -> 26.1 us  [send(): return lax.ppermute(x, axes, pairs)]
    another operation x2 -> x0, local copies, waits for them, and re-layouts: 6.34 us -> none  [blocks(): return x.reshape(x.shape[0], NB, BS, BS)]
    ppermute x7 -> x13, waiting for transfers between devices: 18.4 us -> 20.7 us  [send(): return lax.ppermute(x, axes, pairs)]
  transfers between devices with their start and end apart: 7 -> 13, of which waited for: 3 -> 6; matrix products, arithmetic and copies ran while one was open for 16% -> 2% of each run, Pallas kernels for 0% -> 23%
where the time goes in v2:
time: 120 us
  Pallas kernels  48.9 us (41%)
  starting transfers between devices  26.1 us (22%)
  waiting for transfers between devices  20.7 us (17%)
  local copies, waits for them, and re-layouts  17 us (14%)
  other arithmetic  4.91 us (4%)
  between operations  2.18 us (2%)
    pallas_call x2, Pallas kernels, krylov(): pl.pallas_call(functools.partial(krylov_kernel, second, core_of), out_sha...  34.8 us
    ppermute x13, starting transfers between devices, send(): return lax.ppermute(x, axes, pairs)  26.1 us
    ppermute x13, waiting for transfers between devices, send(): return lax.ppermute(x, axes, pairs)  20.7 us
    unnamed x28, local copies, waits for them, and re-layouts  16.9 us
    pallas_call x2, Pallas kernels, project(): pl.pallas_call(functools.partial(project_kernel, owner, core_of), out_sha...  7.36 us
    pallas_call x2, Pallas kernels, grow(): pl.pallas_call(env_kernel, out_shape=shape(2, NB, FLAT), in_specs=[VM] *...  6.77 us
    broadcast_in_dim x2, other arithmetic, shards(): return (out_new[None], out_env[None])  3.16 us
  transfers between devices with their start and end apart: 13, of which 6 were waited for; matrix products, arithmetic and copies ran while one was open for 2% of the time, Pallas kernels for 23%

profile of v2, /device:TPU:6, one launch (start us, length us, event | category | flops | bytes accessed | tf_op | source)
XLA Modules:
  0.0 119.8 jit_solution(4890307853718977592)
XLA Ops:
  0.7 1.3 %collective-permute-start.2 = (bf16[2,32,4096]{2,1,0:T(8,128)(2,1)}, bf16[2,32,4096]{2,1,0:T(8,128)(2,1)S(1)}, u32[]{:S(2)}, u32[]{:S(2)}) collective-permute-start(bf16[2,32,4096]{2,1,0:T(8,128)(2,1)} %bitcast.14), channel_id=1, source_target_pairs={{1,0},{3,2},{5,4},{7,6},{9,8},{11,10},{13,12},{15,14},{17,16},{19,... | collective-permute-start | bytes 1572872 | tf_op jit(solution)/shard_map/ppermute | solution.py:353
  2.0 3.1 %collective-permute-start.1 = (bf16[2,32,4096]{2,1,0:T(8,128)(2,1)}, bf16[2,32,4096]{2,1,0:T(8,128)(2,1)S(1)}, u32[]{:S(2)}, u32[]{:S(2)}) collective-permute-start(bf16[2,32,4096]{2,1,0:T(8,128)(2,1)} %bitcast.12), channel_id=1, source_target_pairs={{0,1},{2,3},{4,5},{6,7},{8,9},{10,11},{12,13},{14,15},{16,17},{18,... | collective-permute-start | bytes 1572872 | tf_op jit(solution)/shard_map/ppermute | solution.py:353
  5.1 1.7 %collective-permute-done.1.refs_5_ = bf16[2,32,4096]{2,1,0:T(8,128)(2,1)S(1)} collective-permute-done((bf16[2,32,4096]{2,1,0:T(8,128)(2,1)}, bf16[2,32,4096]{2,1,0:T(8,128)(2,1)S(1)}, u32[]{:S(2)}, u32[]{:S(2)}) %collective-permute-start.1) | collective-permute-done | bytes 524320 | tf_op jit(solution)/shard_map/ppermute | solution.py:353
  6.8 8.7 %collective-permute-start.7 = (bf16[2,32,4096]{2,1,0:T(8,128)(2,1)}, bf16[2,32,4096]{2,1,0:T(8,128)(2,1)S(1)}, u32[]{:S(2)}, u32[]{:S(2)}) collective-permute-start(bf16[2,32,4096]{2,1,0:T(8,128)(2,1)} %bitcast.15), channel_id=1, source_target_pairs={{2,0},{4,2},{6,4},{8,6},{10,8},{12,10},{14,12},{16,14},{18,16},{20... | collective-permute-start | bytes 1572872 | tf_op jit(solution)/shard_map/ppermute | solution.py:353
  15.5 1.3 %collective-permute-start.8 = (bf16[2,32,4096]{2,1,0:T(8,128)(2,1)}, bf16[2,32,4096]{2,1,0:T(8,128)(2,1)S(1)}, u32[]{:S(2)}, u32[]{:S(2)}) collective-permute-start(bf16[2,32,4096]{2,1,0:T(8,128)(2,1)} %bitcast.16), channel_id=1, source_target_pairs={{2,1},{4,3},{6,5},{8,7},{10,9},{12,11},{14,13},{16,15},{18,17},{20... | collective-permute-start | bytes 1572872 | tf_op jit(solution)/shard_map/ppermute | solution.py:353
  21.5 17.3 %krylov.2 = (bf16[5,4,32,64,128]{4,3,2,1,0:T(8,128)(2,1)S(1)}, f32[4,32,64,128]{3,2,1,0:T(8,128)S(1)}, f32[8,128]{1,0:T(8,128)S(1)}, bf16[32,64,256]{2,1,0:T(8,1...) custom-call(f32[4,4]{1,0:T(4,128)S(1)} %copy-done.11, s32[1,32]{1,0:T(1,128)S(1)} %copy-done.13, ...), custom_call_target="tpu_custom_call" | custom-call | flops 10000000000 | bytes 16777216 | tf_op jit(solution)/shard_map/krylov/pallas_call | solution.py:287
  39.0 2.3 %collective-permute-start.5 = (bf16[2,32,4096]{2,1,0:T(8,128)(2,1)S(1)}, bf16[2,32,4096]{2,1,0:T(8,128)(2,1)S(1)}, u32[]{:S(2)}, u32[]{:S(2)}) collective-permute-start(bf16[2,32,4096]{2,1,0:T(8,128)(2,1)S(1)} %get-tuple-element.35), channel_id=1, source_target_pairs={{2,0},{4,2},{6,4},{8,6},{10,8},{12,10},{14,12},{16,14},{18,16},{20... | collective-permute-start | bytes 1572872 | tf_op jit(solution)/shard_map/ppermute | solution.py:353
  41.3 1.3 %collective-permute-start.6 = (bf16[2,32,4096]{2,1,0:T(8,128)(2,1)S(1)}, bf16[2,32,4096]{2,1,0:T(8,128)(2,1)S(1)}, u32[]{:S(2)}, u32[]{:S(2)}) collective-permute-start(bf16[2,32,4096]{2,1,0:T(8,128)(2,1)S(1)} %get-tuple-element.34), channel_id=1, source_target_pairs={{2,1},{4,3},{6,5},{8,7},{10,9},{12,11},{14,13},{16,15},{18,17},{20... | collective-permute-start | bytes 1572872 | tf_op jit(solution)/shard_map/ppermute | solution.py:353
  42.6 3.7 %project.2.refs_2_ = bf16[2,32,4096]{2,1,0:T(8,128)(2,1)S(1)} custom-call(f32[8,128]{1,0:T(8,128)S(1)} %get-tuple-element.21.own, f32[8,128]{1,0:T(8,128)S(1)} %collective-permute-done.3.got, bf16[5,4,32,64,128]{4,3,2,1,0:T(8,128)(2,1)S(1)} %get-tuple-element.22.u, f32[4,32,64,128]{3,2,1,0:T(8,128)S(1)} %get-tuple-element.23.last, ...), custom_call_target="tpu_custom_call" | custom-call | flops 1000000000 | bytes 16777216 | tf_op jit(solution)/shard_map/project/pallas_call | solution.py:300
  46.6 3.0 %grow.2.refs_8_.left = bf16[2,32,4096]{2,1,0:T(8,128)(2,1)S(1)} custom-call(bf16[4,32,4096]{2,1,0:T(8,128)(2,1)S(1)} %get-tuple-element.27.a_flat, bf16[2,32,4096]{2,1,0:T(8,128)(2,1)S(1)} %get-tuple-element.28.left, bf16[32,64,256]{2,1,0:T(8,128)(2,1)S(1)} %get-tuple-element.24.at), custom_call_target="tpu_custom_call" | custom-call | flops 1000000000 | bytes 4194304 | tf_op jit(solution)/shard_map/grow/pallas_call | solution.py:316
  50.0 3.5 %collective-permute-done.6.refs_5_ = bf16[2,32,4096]{2,1,0:T(8,128)(2,1)S(1)} collective-permute-done((bf16[2,32,4096]{2,1,0:T(8,128)(2,1)S(1)}, bf16[2,32,4096]{2,1,0:T(8,128)(2,1)S(1)}, u32[]{:S(2)}, u32[]{:S(2)}) %collective-permute-start.6) | collective-permute-done | bytes 524320 | tf_op jit(solution)/shard_map/ppermute | solution.py:353
  53.6 17.5 %krylov.3 = (bf16[5,4,32,64,128]{4,3,2,1,0:T(8,128)(2,1)S(1)}, f32[4,32,64,128]{3,2,1,0:T(8,128)S(1)}, f32[8,128]{1,0:T(8,128)S(1)}, bf16[32,64,256]{2,1,0:T(8,128)(2,1)S(1)}, bf16[4,32,4096]{2,1,0:T(8,128)(2,1)S(1)}) custom-call(f32[4,4]{1,0:T(4,128)S(1)} %copy-done.12, s32[1,32]{1,0:T(1,128)S(1)} %copy-done.13, bf16[2,32,4096]{2,1,0:T(8,128)(2,1)S(1)} %project.2.refs_2_, ...), custom_call_target="tpu_custom_call" | custom-call | flops 10000000000 | bytes 16777216 | tf_op jit(solution)/shard_map/krylov/pallas_call | solution.py:287
  71.1 4.0 %copy-done = bf16[5,4,32,64,128]{4,3,2,1,0:T(8,128)(2,1)} copy-done((bf16[5,4,32,64,128]{4,3,2,1,0:T(8,128)(2,1)}, bf16[5,4,32,64,128]{4,3,2,1,0:T(8,128)(2,1)S(1)}, u32[]{:S(2)}) %copy-start) | copy-done | bytes 10485784
  75.1 2.1 %copy-done.2 = f32[4,32,64,128]{3,2,1,0:T(8,128)} copy-done((f32[4,32,64,128]{3,2,1,0:T(8,128)}, f32[4,32,64,128]{3,2,1,0:T(8,128)S(1)}, u32[]{:S(2)}) %copy-start.2) | copy-done | bytes 4194328
  77.2 3.7 %grow.3 = bf16[2,32,4096]{2,1,0:T(8,128)(2,1)} custom-call(bf16[4,32,4096]{2,1,0:T(8,128)(2,1)S(1)} %get-tuple-element.29.a_flat, bf16[2,32,4096]{2,1,0:T(8,128)(2,1)S(1)} %grow.2.refs_8_.left, bf16[32,64,256]{2,1,0:T(8,128)(2,1)S(1)} %get-tuple-element.33.at), custom_call_target="tpu_custom_call" | custom-call | flops 1000000000 | bytes 4194304 | tf_op jit(solution)/shard_map/grow/pallas_call | solution.py:316
  80.9 1.3 %collective-permute-start.12 = (bf16[2,32,4096]{2,1,0:T(8,128)(2,1)}, bf16[2,32,4096]{2,1,0:T(8,128)(2,1)}, u32[]{:S(2)}, u32[]{:S(2)}) collective-permute-start(bf16[2,32,4096]{2,1,0:T(8,128)(2,1)} %grow.3), channel_id=1, source_target_pairs={{1,2},{3,4},{5,6},{7,8},{9,10},{11,12},{13,14},{15,16},{17,18},{19... | collective-permute-start | bytes 1572872 | tf_op jit(solution)/shard_map/ppermute | solution.py:353
  82.2 3.1 %collective-permute-start.9 = (f32[8,128]{1,0:T(8,128)S(1)}, f32[8,128]{1,0:T(8,128)S(1)}, u32[]{:S(2)}, u32[]{:S(2)}) collective-permute-start(f32[8,128]{1,0:T(8,128)S(1)} %get-tuple-element.30.own), channel_id=1, source_target_pairs={{0,1},{1,0},{2,3},{3,2},{4,5},{5,4},{6,7},{7,6},{8,9},{9,8},{10,11... | collective-permute-start | bytes 12296 | tf_op jit(solution)/shard_map/ppermute | solution.py:353
  86.2 4.0 %copy-done.1 = bf16[5,4,32,64,128]{4,3,2,1,0:T(8,128)(2,1)S(1)} copy-done((bf16[5,4,32,64,128]{4,3,2,1,0:T(8,128)(2,1)S(1)}, bf16[5,4,32,64,128]{4,3,2,1,0:T(8,128)(2,1)}, u32[]{:S(2)}) %copy-start.1) | copy-done | bytes 10485784
  90.2 2.2 %copy-done.3 = f32[4,32,64,128]{3,2,1,0:T(8,128)S(1)} copy-done((f32[4,32,64,128]{3,2,1,0:T(8,128)S(1)}, f32[4,32,64,128]{3,2,1,0:T(8,128)}, u32[]{:S(2)}) %copy-start.3) | copy-done | bytes 4194328
  92.4 3.6 %project.3 = bf16[2,32,4096]{2,1,0:T(8,128)(2,1)S(1)} custom-call(f32[8,128]{1,0:T(8,128)S(1)} %get-tuple-element.30.own, f32[8,128]{1,0:T(8,128)S(1)} %collective-permute-done.9.got, bf16[5,4,32,64,128]{4,3,2,1,0:T(8,128)(2,1)S(1)} %copy-done.1, f32[4,32,64,128]{3,2,1,0:T(8,128)S(1)} %copy-done.3, bf16[32,64,256]{2,1,0:T(8,128)(2,1)S(1)} %get-tuple-element.33.at), custom_call_target="tpu_custom_call" | custom-call | flops 1000000000 | bytes 16777216 | tf_op jit(solution)/shard_map/project/pallas_call | solution.py:300
  96.0 1.3 %collective-permute-start.11 = (bf16[2,32,4096]{2,1,0:T(8,128)(2,1)S(1)}, bf16[2,32,4096]{2,1,0:T(8,128)(2,1)S(1)}, u32[]{:S(2)}, u32[]{:S(2)}) collective-permute-start(bf16[2,32,4096]{2,1,0:T(8,128)(2,1)S(1)} %project.3), channel_id=1, source_target_pairs={{1,2},{3,4},{5,6},{7,8},{9,10},{11,12},{13,14},{15,16},{17,18},{19... | collective-permute-start | bytes 1572872 | tf_op jit(solution)/shard_map/ppermute | solution.py:353
  97.3 1.9 %collective-permute-start.10 = (bf16[2,32,4096]{2,1,0:T(8,128)(2,1)S(1)}, bf16[2,32,4096]{2,1,0:T(8,128)(2,1)S(1)}, u32[]{:S(2)}, u32[]{:S(2)}) collective-permute-start(bf16[2,32,4096]{2,1,0:T(8,128)(2,1)S(1)} %project.3), channel_id=1, source_target_pairs={{0,2},{2,4},{4,6},{6,8},{8,10},{10,12},{12,14},{14,16},{16,18},{18... | collective-permute-start | bytes 1572872 | tf_op jit(solution)/shard_map/ppermute | solution.py:353
  99.2 1.9 %select_bitcast_fusion = bf16[1,2,32,4096]{3,2,1,0:T(8,128)(2,1)} fusion(bf16[2,32,4096]{2,1,0:T(8,128)(2,1)S(1)} %copy-done.9, bf16[2,32,4096]{2,1,0:T(8,128)(2,1)} %collective-permute-done.12, pred[]{:T(512)S(6)} %eq.9, pred[]{:T(512)S(6)} %eq.8, bf16[1,2,32,4096]{3,2,1,0:T(8,128)(2,1)S(1)} %copy-done.7), kind=kLoop, calls=%fused_computation.6 | loop fusion | flops 524288 | bytes 2097154 | tf_op jit(solution)/shard_map/broadcast_in_dim | solution.py:391
  101.2 13.2 %collective-permute-done.11 = bf16[2,32,4096]{2,1,0:T(8,128)(2,1)S(1)} collective-permute-done((bf16[2,32,4096]{2,1,0:T(8,128)(2,1)S(1)}, bf16[2,32,4096]{2,1,0:T(8,128)(2,1)S(1)}, u32[]{:S(2)}, u32[]{:S(2)}) %collective-permute-start.11) | collective-permute-done | bytes 524320 | tf_op jit(solution)/shard_map/ppermute | solution.py:353
  (41 shorter events, 10.4 us)
Async XLA Ops:
  0.6 6.2 %collective-permute-start = (bf16[4,32,4096]{2,1,0:T(8,128)(2,1)}, bf16[4,32,4096]{2,1,0:T(8,128)(2,1)S(1)}, u32[]{:S(2)}, u32[]{:S(2)}) collective-permute-start(bf16[4,32,4096]{2,1,0:T(8,128)(2,1)} %bitcast.9), channel_id=1, source_target_pairs={{0,1},{1,0},{2,3},{3,2},{4,5},{5,4},{6,7},{7,6},{8,9},{9,8},{10,11... | collective-permute-start | bytes 3145736 | tf_op jit(solution)/shard_map/ppermute | solution.py:353
  0.7 4.4 %collective-permute-start.2 = (bf16[2,32,4096]{2,1,0:T(8,128)(2,1)}, bf16[2,32,4096]{2,1,0:T(8,128)(2,1)S(1)}, u32[]{:S(2)}, u32[]{:S(2)}) collective-permute-start(bf16[2,32,4096]{2,1,0:T(8,128)(2,1)} %bitcast.14), channel_id=1, source_target_pairs={{1,0},{3,2},{5,4},{7,6},{9,8},{11,10},{13,12},{15,14},{17,16},{19,... | collective-permute-start | bytes 1572872 | tf_op jit(solution)/shard_map/ppermute | solution.py:353
  2.0 4.8 %collective-permute-start.1 = (bf16[2,32,4096]{2,1,0:T(8,128)(2,1)}, bf16[2,32,4096]{2,1,0:T(8,128)(2,1)S(1)}, u32[]{:S(2)}, u32[]{:S(2)}) collective-permute-start(bf16[2,32,4096]{2,1,0:T(8,128)(2,1)} %bitcast.12), channel_id=1, source_target_pairs={{0,1},{2,3},{4,5},{6,7},{8,9},{10,11},{12,13},{14,15},{16,17},{18,... | collective-permute-start | bytes 1572872 | tf_op jit(solution)/shard_map/ppermute | solution.py:353
  6.8 46.8 %collective-permute-start.7 = (bf16[2,32,4096]{2,1,0:T(8,128)(2,1)}, bf16[2,32,4096]{2,1,0:T(8,128)(2,1)S(1)}, u32[]{:S(2)}, u32[]{:S(2)}) collective-permute-start(bf16[2,32,4096]{2,1,0:T(8,128)(2,1)} %bitcast.15), channel_id=1, source_target_pairs={{2,0},{4,2},{6,4},{8,6},{10,8},{12,10},{14,12},{16,14},{18,16},{20... | collective-permute-start | bytes 1572872 | tf_op jit(solution)/shard_map/ppermute | solution.py:353
  15.5 38.1 %collective-permute-start.8 = (bf16[2,32,4096]{2,1,0:T(8,128)(2,1)}, bf16[2,32,4096]{2,1,0:T(8,128)(2,1)S(1)}, u32[]{:S(2)}, u32[]{:S(2)}) collective-permute-start(bf16[2,32,4096]{2,1,0:T(8,128)(2,1)} %bitcast.16), channel_id=1, source_target_pairs={{2,1},{4,3},{6,5},{8,7},{10,9},{12,11},{14,13},{16,15},{18,17},{20... | collective-permute-start | bytes 1572872 | tf_op jit(solution)/shard_map/ppermute | solution.py:353
  16.8 1.2 %copy-start.4 = (bf16[1,4,32,4096]{3,2,1,0:T(8,128)(2,1)S(1)}, bf16[1,4,32,4096]{3,2,1,0:T(8,128)(2,1)}, u32[]{:S(2)}) copy-start(bf16[1,4,32,4096]{3,2,1,0:T(8,128)(2,1)} %param.5) | copy-start | bytes 3145732
  18.0 1.0 copy-start.6
  38.8 3.8 %collective-permute-start.3 = (f32[8,128]{1,0:T(8,128)S(1)}, f32[8,128]{1,0:T(8,128)S(1)}, u32[]{:S(2)}, u32[]{:S(2)}) collective-permute-start(f32[8,128]{1,0:T(8,128)S(1)} %get-tuple-element.21.own), channel_id=1, source_target_pairs={{0,1},{1,0},{2,3},{3,2},{4,5},{5,4},{6,7},{7,6},{8,9},{9,8},{10,11... | collective-permute-start | bytes 12296 | tf_op jit(solution)/shard_map/ppermute | solution.py:353
  39.0 11.1 %collective-permute-start.5 = (bf16[2,32,4096]{2,1,0:T(8,128)(2,1)S(1)}, bf16[2,32,4096]{2,1,0:T(8,128)(2,1)S(1)}, u32[]{:S(2)}, u32[]{:S(2)}) collective-permute-start(bf16[2,32,4096]{2,1,0:T(8,128)(2,1)S(1)} %get-tuple-element.35), channel_id=1, source_target_pairs={{2,0},{4,2},{6,4},{8,6},{10,8},{12,10},{14,12},{16,14},{18,16},{20... | collective-permute-start | bytes 1572872 | tf_op jit(solution)/shard_map/ppermute | solution.py:353
  41.3 12.3 %collective-permute-start.6 = (bf16[2,32,4096]{2,1,0:T(8,128)(2,1)S(1)}, bf16[2,32,4096]{2,1,0:T(8,128)(2,1)S(1)}, u32[]{:S(2)}, u32[]{:S(2)}) collective-permute-start(bf16[2,32,4096]{2,1,0:T(8,128)(2,1)S(1)} %get-tuple-element.34), channel_id=1, source_target_pairs={{2,1},{4,3},{6,5},{8,7},{10,9},{12,11},{14,13},{16,15},{18,17},{20... | collective-permute-start | bytes 1572872 | tf_op jit(solution)/shard_map/ppermute | solution.py:353
  42.6 11.0 %copy-start.12 = (f32[4,4]{1,0:T(4,128)S(1)}, f32[4,4]{1,0:T(4,128)}, u32[]{:S(2)}) copy-start(f32[4,4]{1,0:T(4,128)} %refs_0_.3) | copy-start | bytes 196
  46.4 7.2 %collective-permute-start.4 = (bf16[2,32,4096]{2,1,0:T(8,128)(2,1)S(1)}, bf16[2,32,4096]{2,1,0:T(8,128)(2,1)S(1)}, u32[]{:S(2)}, u32[]{:S(2)}) collective-permute-start(bf16[2,32,4096]{2,1,0:T(8,128)(2,1)S(1)} %project.2.refs_2_), channel_id=1, source_target_pairs={{0,1},{1,0},{2,3},{3,2},{4,5},{5,4},{6,7},{7,6},{8,9},{9,8},{10,11... | collective-permute-start | bytes 1572872 | tf_op jit(solution)/shard_map/ppermute | solution.py:353
  49.7 27.5 %copy-start.8 = (bf16[2,32,4096]{2,1,0:T(8,128)(2,1)}, bf16[2,32,4096]{2,1,0:T(8,128)(2,1)S(1)}, u32[]{:S(2)}) copy-start(bf16[2,32,4096]{2,1,0:T(8,128)(2,1)S(1)} %grow.2.refs_8_.left) | copy-start | bytes 1572868
  71.1 4.0 %copy-start = (bf16[5,4,32,64,128]{4,3,2,1,0:T(8,128)(2,1)}, bf16[5,4,32,64,128]{4,3,2,1,0:T(8,128)(2,1)S(1)}, u32[]{:S(2)}) copy-start(bf16[5,4,32,64,128]{4,3,2,1,0:T(8,128)(2,1)S(1)} %get-tuple-element.31.u) | copy-start | bytes 31457284
  75.1 2.1 %copy-start.2 = (f32[4,32,64,128]{3,2,1,0:T(8,128)}, f32[4,32,64,128]{3,2,1,0:T(8,128)S(1)}, u32[]{:S(2)}) copy-start(f32[4,32,64,128]{3,2,1,0:T(8,128)S(1)} %get-tuple-element.32.last) | copy-start | bytes 12582916
  80.9 18.3 %collective-permute-start.12 = (bf16[2,32,4096]{2,1,0:T(8,128)(2,1)}, bf16[2,32,4096]{2,1,0:T(8,128)(2,1)}, u32[]{:S(2)}, u32[]{:S(2)}) collective-permute-start(bf16[2,32,4096]{2,1,0:T(8,128)(2,1)} %grow.3), channel_id=1, source_target_pairs={{1,2},{3,4},{5,6},{7,8},{9,10},{11,12},{13,14},{15,16},{17,18},{19... | collective-permute-start | bytes 1572872 | tf_op jit(solution)/shard_map/ppermute | solution.py:353
  82.2 4.0 %collective-permute-start.9 = (f32[8,128]{1,0:T(8,128)S(1)}, f32[8,128]{1,0:T(8,128)S(1)}, u32[]{:S(2)}, u32[]{:S(2)}) collective-permute-start(f32[8,128]{1,0:T(8,128)S(1)} %get-tuple-element.30.own), channel_id=1, source_target_pairs={{0,1},{1,0},{2,3},{3,2},{4,5},{5,4},{6,7},{7,6},{8,9},{9,8},{10,11... | collective-permute-start | bytes 12296 | tf_op jit(solution)/shard_map/ppermute | solution.py:353
  86.2 4.0 %copy-start.1 = (bf16[5,4,32,64,128]{4,3,2,1,0:T(8,128)(2,1)S(1)}, bf16[5,4,32,64,128]{4,3,2,1,0:T(8,128)(2,1)}, u32[]{:S(2)}) copy-start(bf16[5,4,32,64,128]{4,3,2,1,0:T(8,128)(2,1)} %copy-done) | copy-start | bytes 31457284
  90.2 2.2 %copy-start.3 = (f32[4,32,64,128]{3,2,1,0:T(8,128)S(1)}, f32[4,32,64,128]{3,2,1,0:T(8,128)}, u32[]{:S(2)}) copy-start(f32[4,32,64,128]{3,2,1,0:T(8,128)} %copy-done.2) | copy-start | bytes 12582916
  92.4 6.9 %copy-start.7 = (bf16[1,2,32,4096]{3,2,1,0:T(8,128)(2,1)S(1)}, bf16[1,2,32,4096]{3,2,1,0:T(8,128)(2,1)}, u32[]{:S(2)}) copy-start(bf16[1,2,32,4096]{3,2,1,0:T(8,128)(2,1)} %param.6) | copy-start | bytes 1572868
  92.4 6.9 %copy-start.9 = (bf16[2,32,4096]{2,1,0:T(8,128)(2,1)S(1)}, bf16[2,32,4096]{2,1,0:T(8,128)(2,1)}, u32[]{:S(2)}) copy-start(bf16[2,32,4096]{2,1,0:T(8,128)(2,1)} %copy-done.8) | copy-start | bytes 1572868
  92.4 26.2 %copy-start.5 = (bf16[1,4,32,4096]{3,2,1,0:T(8,128)(2,1)S(1)}, bf16[1,4,32,4096]{3,2,1,0:T(8,128)(2,1)}, u32[]{:S(2)}) copy-start(bf16[1,4,32,4096]{3,2,1,0:T(8,128)(2,1)} %param.5) | copy-start | bytes 3145732
  96.0 18.4 %collective-permute-start.11 = (bf16[2,32,4096]{2,1,0:T(8,128)(2,1)S(1)}, bf16[2,32,4096]{2,1,0:T(8,128)(2,1)S(1)}, u32[]{:S(2)}, u32[]{:S(2)}) collective-permute-start(bf16[2,32,4096]{2,1,0:T(8,128)(2,1)S(1)} %project.3), channel_id=1, source_target_pairs={{1,2},{3,4},{5,6},{7,8},{9,10},{11,12},{13,14},{15,16},{17,18},{19... | collective-permute-start | bytes 1572872 | tf_op jit(solution)/shard_map/ppermute | solution.py:353
  97.3 19.0 %collective-permute-start.10 = (bf16[2,32,4096]{2,1,0:T(8,128)(2,1)S(1)}, bf16[2,32,4096]{2,1,0:T(8,128)(2,1)S(1)}, u32[]{:S(2)}, u32[]{:S(2)}) collective-permute-start(bf16[2,32,4096]{2,1,0:T(8,128)(2,1)S(1)} %project.3), channel_id=1, source_target_pairs={{0,2},{2,4},{4,6},{6,8},{8,10},{10,12},{12,14},{14,16},{16,18},{18... | collective-permute-start | bytes 1572872 | tf_op jit(solution)/shard_map/ppermute | solution.py:353
  (3 other events, 2.4 us)

commit v3 on v2

--- a/solution.py
+++ b/solution.py
@@ -22,10 +22,10 @@
 HALF = PHYS // 2
 LN = HALF * BS
 F32, BF16 = jnp.float32, jnp.bfloat16
-LIMIT = 28 * 2**20
+MIB = 2**20
 VM = pl.BlockSpec(memory_space=pltpu.VMEM)
 SM = pl.BlockSpec(memory_space=pltpu.SMEM)
-HB = pl.BlockSpec(memory_space=pl.ANY)
+HB = pl.BlockSpec(memory_space=pltpu.HBM)
 
 
 def dot(a, b):
@@ -254,8 +254,8 @@
     return jax.ShapeDtypeStruct(dims, dtype)
 
 
-def params():
-    return pltpu.CompilerParams(vmem_limit_bytes=LIMIT)
+def params(size):
+    return pltpu.CompilerParams(vmem_limit_bytes=size * MIB)
 
 
 def krylov(core_of, second, coupling, kept, *arrays):
@@ -290,8 +290,8 @@
         in_specs=specs,
         out_specs=(VM,) * len(outs),
         scratch_shapes=scratch,
-        compiler_params=params(),
-        cost_estimate=pl.CostEstimate(flops=10**10, bytes_accessed=2**24, transcendentals=0),
+        compiler_params=params(28),
+        cost_estimate=pl.CostEstimate(flops=10**11, bytes_accessed=2**24, transcendentals=0),
         name="krylov",
     )(coupling, kept, *arrays)
 
@@ -306,8 +306,8 @@
             pltpu.VMEM((8, 128), F32),
             pltpu.VMEM((HALF, NB, BS, BS), BF16),
         ],
-        compiler_params=params(),
-        cost_estimate=pl.CostEstimate(flops=10**9, bytes_accessed=2**24, transcendentals=0),
+        compiler_params=params(20),
+        cost_estimate=pl.CostEstimate(flops=10**6, bytes_accessed=2**10, transcendentals=0),
         name="project",
     )(own, got, u, last, at)
 
@@ -324,8 +324,8 @@
             pltpu.VMEM((PHYS, NB, BS, 2 * BS), BF16),
             pltpu.VMEM((2, NB, BS, BS), BF16),
         ],
-        compiler_params=params(),
-        cost_estimate=pl.CostEstimate(flops=10**9, bytes_accessed=2**22, transcendentals=0),
+        compiler_params=params(12),
+        cost_estimate=pl.CostEstimate(flops=10**6, bytes_accessed=2**10, transcendentals=0),
         name="grow",
     )(a_flat, left, at)
 
@@ -355,12 +355,12 @@
     got_t = send(tensor, swap)
     got_l = send(left, rise)
     got_r = send(right, fall)
-    late_t, late_r, got_t, got_l, got_r = lax.optimization_barrier(
-        (tensor, right, got_t, got_l, got_r)
+    low, high, late_r, got_t, got_l, got_r = lax.optimization_barrier(
+        (tensor[:HALF], tensor[HALF:], right, got_t, got_l, got_r)
     )
-    b_even = send(late_t[:HALF], to_even)
+    b_even = send(low, to_even)
+    b_odd = send(high, to_odd)
     r_even = send(late_r, to_even)
-    b_odd = send(late_t[HALF:], to_odd)
     r_odd = send(late_r, to_odd)
 
     u, last, small, at, a_flat, l_flat = krylov(
@@ -369,6 +369,7 @@
     got_small = send(small, swap)
     env1 = grow(a_flat, l_flat, at)
     x = project(core_index, 0, small, got_small, u, last, at)
+    x, b_even, b_odd, r_even, r_odd = lax.optimization_barrier((x, b_even, b_odd, r_even, r_odd))
     got_x = send(x, swap)
 
     u, last, small, at, new1 = krylov(

time: 120 us -> 116 us (0.967)
  waiting for transfers between devices: 20.7 us -> 16.6 us
  Pallas kernels: 48.9 us -> 46.4 us
  other arithmetic: 4.91 us -> 6.19 us
    ppermute x13, waiting for transfers between devices: 20.7 us -> 16.6 us  [send(): return lax.ppermute(x, axes, pairs)]
    pallas_call x2, Pallas kernels: 34.8 us -> 33.2 us  [krylov(): pl.pallas_call(functools.partial(krylov_kernel, second, core_of), out_sha...]
    broadcast_in_dim x2, other arithmetic: 3.16 us -> 4.45 us  [shards(): return (out_new[None], out_env[None])]
    slice x1, local copies, waits for them, and re-layouts: 0.07 us -> 1.28 us  [shards(): tensor[HALF:]]
    unnamed x28 -> x20, local copies, waits for them, and re-layouts: 16.9 us -> 16.9 us
  transfers between devices with their start and end apart: 13 -> 13, of which waited for: 6 -> 5; matrix products, arithmetic and copies ran while one was open for 2% -> 4% of each run, Pallas kernels for 23% -> 23%
where the time goes in v3:
time: 116 us
  Pallas kernels  46.4 us (40%)
  starting transfers between devices  26.3 us (23%)
  local copies, waits for them, and re-layouts  18.2 us (16%)
  waiting for transfers between devices  16.6 us (14%)
  other arithmetic  6.19 us (5%)
  between operations  2.09 us (2%)
    pallas_call x2, Pallas kernels, krylov(): pl.pallas_call(functools.partial(krylov_kernel, second, core_of), out_sha...  33.2 us
    ppermute x13, starting transfers between devices, send(): return lax.ppermute(x, axes, pairs)  26.3 us
    unnamed x20, local copies, waits for them, and re-layouts  16.9 us
    ppermute x13, waiting for transfers between devices, send(): return lax.ppermute(x, axes, pairs)  16.6 us
    pallas_call x2, Pallas kernels, project(): pl.pallas_call(functools.partial(project_kernel, owner, core_of), out_sha...  7.26 us
    pallas_call x2, Pallas kernels, grow(): pl.pallas_call(env_kernel, out_shape=shape(2, NB, FLAT), in_specs=[VM] *...  5.99 us
    broadcast_in_dim x2, other arithmetic, shards(): return (out_new[None], out_env[None])  4.45 us
  transfers between devices with their start and end apart: 13, of which 5 were waited for; matrix products, arithmetic and copies ran while one was open for 4% of the time, Pallas kernels for 23%

profile of v3, /device:TPU:6, one launch (start us, length us, event | category | flops | bytes accessed | tf_op | source)
XLA Modules:
  0.0 115.7 jit_solution(5622983953147286559)
XLA Ops:
  0.7 1.3 %collective-permute-start.2 = (bf16[2,32,4096]{2,1,0:T(8,128)(2,1)}, bf16[2,32,4096]{2,1,0:T(8,128)(2,1)S(1)}, u32[]{:S(2)}, u32[]{:S(2)}) collective-permute-start(bf16[2,32,4096]{2,1,0:T(8,128)(2,1)} %bitcast.17), channel_id=1, source_target_pairs={{1,0},{3,2},{5,4},{7,6},{9,8},{11,10},{13,12},{15,14},{17,16},{19,... | collective-permute-start | bytes 1572872 | tf_op jit(solution)/shard_map/ppermute | solution.py:353
  2.0 3.1 %collective-permute-start.1 = (bf16[2,32,4096]{2,1,0:T(8,128)(2,1)}, bf16[2,32,4096]{2,1,0:T(8,128)(2,1)S(1)}, u32[]{:S(2)}, u32[]{:S(2)}) collective-permute-start(bf16[2,32,4096]{2,1,0:T(8,128)(2,1)} %bitcast.15), channel_id=1, source_target_pairs={{0,1},{2,3},{4,5},{6,7},{8,9},{10,11},{12,13},{14,15},{16,17},{18,... | collective-permute-start | bytes 1572872 | tf_op jit(solution)/shard_map/ppermute | solution.py:353
  5.1 1.3 %slice_bitcast_fusion = (bf16[2,32,4096]{2,1,0:T(8,128)(2,1)S(1)}, bf16[2,32,4096]{2,1,0:T(8,128)(2,1)S(1)}) fusion(bf16[1,4,32,4096]{3,2,1,0:T(8,128)(2,1)} %param.5), kind=kLoop, calls=%fused_computation.7 | loop fusion | bytes 2097152 | tf_op jit(solution)/shard_map/slice | solution.py:359
  6.8 8.7 %collective-permute-start.6 = (bf16[2,32,4096]{2,1,0:T(8,128)(2,1)}, bf16[2,32,4096]{2,1,0:T(8,128)(2,1)S(1)}, u32[]{:S(2)}, u32[]{:S(2)}) collective-permute-start(bf16[2,32,4096]{2,1,0:T(8,128)(2,1)} %bitcast.18), channel_id=1, source_target_pairs={{2,0},{4,2},{6,4},{8,6},{10,8},{12,10},{14,12},{16,14},{18,16},{20... | collective-permute-start | bytes 1572872 | tf_op jit(solution)/shard_map/ppermute | solution.py:353
  15.5 1.3 %collective-permute-start.7 = (bf16[2,32,4096]{2,1,0:T(8,128)(2,1)}, bf16[2,32,4096]{2,1,0:T(8,128)(2,1)S(1)}, u32[]{:S(2)}, u32[]{:S(2)}) collective-permute-start(bf16[2,32,4096]{2,1,0:T(8,128)(2,1)} %bitcast.19), channel_id=1, source_target_pairs={{2,1},{4,3},{6,5},{8,7},{10,9},{12,11},{14,13},{16,15},{18,17},{20... | collective-permute-start | bytes 1572872 | tf_op jit(solution)/shard_map/ppermute | solution.py:353
  16.8 2.3 %collective-permute-start.4 = (bf16[2,32,4096]{2,1,0:T(8,128)(2,1)S(1)}, bf16[2,32,4096]{2,1,0:T(8,128)(2,1)S(1)}, u32[]{:S(2)}, u32[]{:S(2)}) collective-permute-start(bf16[2,32,4096]{2,1,0:T(8,128)(2,1)S(1)} %get-tuple-element.31), channel_id=1, source_target_pairs={{2,0},{4,2},{6,4},{8,6},{10,8},{12,10},{14,12},{16,14},{18,16},{20... | collective-permute-start | bytes 1572872 | tf_op jit(solution)/shard_map/ppermute | solution.py:353
  19.1 1.3 %collective-permute-start.5 = (bf16[2,32,4096]{2,1,0:T(8,128)(2,1)S(1)}, bf16[2,32,4096]{2,1,0:T(8,128)(2,1)S(1)}, u32[]{:S(2)}, u32[]{:S(2)}) collective-permute-start(bf16[2,32,4096]{2,1,0:T(8,128)(2,1)S(1)} %get-tuple-element.32), channel_id=1, source_target_pairs={{2,1},{4,3},{6,5},{8,7},{10,9},{12,11},{14,13},{16,15},{18,17},{20... | collective-permute-start | bytes 1572872 | tf_op jit(solution)/shard_map/ppermute | solution.py:353
  25.1 16.4 %krylov.2 = (bf16[5,4,32,64,128]{4,3,2,1,0:T(8,128)(2,1)S(1)}, f32[4,32,64,128]{3,2,1,0:T(8,128)S(1)}, f32[8,128]{1,0:T(8,128)S(1)}, bf16[32,64,256]{2,1,0:T(8,1...) custom-call(f32[4,4]{1,0:T(4,128)S(1)} %copy-done.8, s32[1,32]{1,0:T(1,128)S(1)} %copy-done.9, ...), custom_call_target="tpu_custom_call" | custom-call | flops 99999997952 | bytes 16777216 | tf_op jit(solution)/shard_map/krylov/pallas_call | solution.py:287
  42.8 3.6 %project.2.refs_2_ = bf16[2,32,4096]{2,1,0:T(8,128)(2,1)S(1)} custom-call(f32[8,128]{1,0:T(8,128)S(1)} %get-tuple-element.27.own, f32[8,128]{1,0:T(8,128)S(1)} %collective-permute-done.3.got, bf16[5,4,32,64,128]{4,3,2,1,0:T(8,128)(2,1)S(1)} %get-tuple-element.28.u, f32[4,32,64,128]{3,2,1,0:T(8,128)S(1)} %get-tuple-element.29.last, ...), custom_call_target="tpu_custom_call" | custom-call | flops 1000000 | bytes 1024 | tf_op jit(solution)/shard_map/project/pallas_call | solution.py:300
  46.9 3.0 %grow.2.refs_8_.left = bf16[2,32,4096]{2,1,0:T(8,128)(2,1)S(1)} custom-call(bf16[4,32,4096]{2,1,0:T(8,128)(2,1)S(1)} %get-tuple-element.39.a_flat, bf16[2,32,4096]{2,1,0:T(8,128)(2,1)S(1)} %get-tuple-element.40.left, bf16[32,64,256]{2,1,0:T(8,128)(2,1)S(1)} %get-tuple-element.30.at), custom_call_target="tpu_custom_call" | custom-call | flops 1000000 | bytes 1024 | tf_op jit(solution)/shard_map/grow/pallas_call | solution.py:316
  49.9 16.8 %krylov.3 = (bf16[5,4,32,64,128]{4,3,2,1,0:T(8,128)(2,1)S(1)}, f32[4,32,64,128]{3,2,1,0:T(8,128)S(1)}, f32[8,128]{1,0:T(8,128)S(1)}, bf16[32,64,256]{2,1,0:T(8,128)(2,1)S(1)}, bf16[4,32,4096]{2,1,0:T(8,128)(2,1)S(1)}) custom-call(f32[4,4]{1,0:T(4,128)S(1)} %copy-done.8, s32[1,32]{1,0:T(1,128)S(1)} %copy-done.9, bf16[2,32,4096]{2,1,0:T(8,128)(2,1)S(1)} %project.2.refs_2_, ...), custom_call_target="tpu_custom_call" | custom-call | flops 99999997952 | bytes 16777216 | tf_op jit(solution)/shard_map/krylov/pallas_call | solution.py:287
  66.7 4.0 %copy-done = bf16[5,4,32,64,128]{4,3,2,1,0:T(8,128)(2,1)} copy-done((bf16[5,4,32,64,128]{4,3,2,1,0:T(8,128)(2,1)}, bf16[5,4,32,64,128]{4,3,2,1,0:T(8,128)(2,1)S(1)}, u32[]{:S(2)}) %copy-start) | copy-done | bytes 10485784
  70.7 2.1 %copy-done.2 = f32[4,32,64,128]{3,2,1,0:T(8,128)} copy-done((f32[4,32,64,128]{3,2,1,0:T(8,128)}, f32[4,32,64,128]{3,2,1,0:T(8,128)S(1)}, u32[]{:S(2)}) %copy-start.2) | copy-done | bytes 4194328
  72.7 3.0 %grow.3 = bf16[2,32,4096]{2,1,0:T(8,128)(2,1)S(1)} custom-call(bf16[4,32,4096]{2,1,0:T(8,128)(2,1)S(1)} %get-tuple-element.41.a_flat, bf16[2,32,4096]{2,1,0:T(8,128)(2,1)S(1)} %grow.2.refs_8_.left, bf16[32,64,256]{2,1,0:T(8,128)(2,1)S(1)} %get-tuple-element.45.at), custom_call_target="tpu_custom_call" | custom-call | flops 1000000 | bytes 1024 | tf_op jit(solution)/shard_map/grow/pallas_call | solution.py:316
  75.7 1.3 %collective-permute-start.12 = (bf16[2,32,4096]{2,1,0:T(8,128)(2,1)S(1)}, bf16[2,32,4096]{2,1,0:T(8,128)(2,1)}, u32[]{:S(2)}, u32[]{:S(2)}) collective-permute-start(bf16[2,32,4096]{2,1,0:T(8,128)(2,1)S(1)} %grow.3), channel_id=1, source_target_pairs={{1,2},{3,4},{5,6},{7,8},{9,10},{11,12},{13,14},{15,16},{17,18},{19... | collective-permute-start | bytes 1572872 | tf_op jit(solution)/shard_map/ppermute | solution.py:353
  77.0 3.1 %collective-permute-start.9 = (f32[8,128]{1,0:T(8,128)S(1)}, f32[8,128]{1,0:T(8,128)S(1)}, u32[]{:S(2)}, u32[]{:S(2)}) collective-permute-start(f32[8,128]{1,0:T(8,128)S(1)} %get-tuple-element.42.own), channel_id=1, source_target_pairs={{0,1},{1,0},{2,3},{3,2},{4,5},{5,4},{6,7},{7,6},{8,9},{9,8},{10,11... | collective-permute-start | bytes 12296 | tf_op jit(solution)/shard_map/ppermute | solution.py:353
  81.0 4.0 %copy-done.1 = bf16[5,4,32,64,128]{4,3,2,1,0:T(8,128)(2,1)S(1)} copy-done((bf16[5,4,32,64,128]{4,3,2,1,0:T(8,128)(2,1)S(1)}, bf16[5,4,32,64,128]{4,3,2,1,0:T(8,128)(2,1)}, u32[]{:S(2)}) %copy-start.1) | copy-done | bytes 10485784
  85.0 2.2 %copy-done.3 = f32[4,32,64,128]{3,2,1,0:T(8,128)S(1)} copy-done((f32[4,32,64,128]{3,2,1,0:T(8,128)S(1)}, f32[4,32,64,128]{3,2,1,0:T(8,128)}, u32[]{:S(2)}) %copy-start.3) | copy-done | bytes 4194328
  87.2 3.6 %project.3 = bf16[2,32,4096]{2,1,0:T(8,128)(2,1)S(1)} custom-call(f32[8,128]{1,0:T(8,128)S(1)} %get-tuple-element.42.own, f32[8,128]{1,0:T(8,128)S(1)} %collective-permute-done.9.got, bf16[5,4,32,64,128]{4,3,2,1,0:T(8,128)(2,1)S(1)} %copy-done.1, f32[4,32,64,128]{3,2,1,0:T(8,128)S(1)} %copy-done.3, bf16[32,64,256]{2,1,0:T(8,128)(2,1)S(1)} %get-tuple-element.45.at), custom_call_target="tpu_custom_call" | custom-call | flops 1000000 | bytes 1024 | tf_op jit(solution)/shard_map/project/pallas_call | solution.py:300
  90.8 1.3 %collective-permute-start.11 = (bf16[2,32,4096]{2,1,0:T(8,128)(2,1)S(1)}, bf16[2,32,4096]{2,1,0:T(8,128)(2,1)S(1)}, u32[]{:S(2)}, u32[]{:S(2)}) collective-permute-start(bf16[2,32,4096]{2,1,0:T(8,128)(2,1)S(1)} %project.3), channel_id=1, source_target_pairs={{1,2},{3,4},{5,6},{7,8},{9,10},{11,12},{13,14},{15,16},{17,18},{19... | collective-permute-start | bytes 1572872 | tf_op jit(solution)/shard_map/ppermute | solution.py:353
  92.1 1.9 %collective-permute-start.10 = (bf16[2,32,4096]{2,1,0:T(8,128)(2,1)S(1)}, bf16[2,32,4096]{2,1,0:T(8,128)(2,1)S(1)}, u32[]{:S(2)}, u32[]{:S(2)}) collective-permute-start(bf16[2,32,4096]{2,1,0:T(8,128)(2,1)S(1)} %project.3), channel_id=1, source_target_pairs={{0,2},{2,4},{4,6},{6,8},{8,10},{10,12},{12,14},{14,16},{16,18},{18... | collective-permute-start | bytes 1572872 | tf_op jit(solution)/shard_map/ppermute | solution.py:353
  94.1 2.0 %select_bitcast_fusion = bf16[1,2,32,4096]{3,2,1,0:T(8,128)(2,1)} fusion(bf16[2,32,4096]{2,1,0:T(8,128)(2,1)S(1)} %grow.2.refs_8_.left, bf16[2,32,4096]{2,1,0:T(8,128)(2,1)} %collective-permute-done.12, pred[]{:T(512)S(6)} %eq.9, pred[]{:T(512)S(6)} %eq.8, bf16[1,2,32,4096]{3,2,1,0:T(8,128)(2,1)S(1)} %copy-done.6), kind=kLoop, calls=%fused_computation.6 | loop fusion | flops 524288 | bytes 2097154 | tf_op jit(solution)/shard_map/broadcast_in_dim | solution.py:392
  96.0 13.2 %collective-permute-done.11 = bf16[2,32,4096]{2,1,0:T(8,128)(2,1)S(1)} collective-permute-done((bf16[2,32,4096]{2,1,0:T(8,128)(2,1)S(1)}, bf16[2,32,4096]{2,1,0:T(8,128)(2,1)S(1)}, u32[]{:S(2)}, u32[]{:S(2)}) %collective-permute-start.11) | collective-permute-done | bytes 524320 | tf_op jit(solution)/shard_map/ppermute | solution.py:353
  113.3 2.5 %fusion.2 = bf16[1,4,32,4096]{3,2,1,0:T(8,128)(2,1)} fusion(bf16[4,32,4096]{2,1,0:T(8,128)(2,1)S(1)} %get-tuple-element.41.a_flat, bf16[2,32,4096]{2,1,0:T(8,128)(2,1)S(1)} %collective-permute-done.11, bf16[2,32,4096]{2,1,0:T(8,128)(2,1)S(1)} %collective-permute-done.10, f32[]{:T(128)S(6)} %rsqrt.3, pred[]{:T(512)S(6)} %eq.9, pred[]{:T(512)S(6)} %eq.8, ...), kind=kLoop, calls=%fused_computation.3 | loop fusion | flops 3145728 | bytes 4194310 | tf_op jit(solution)/shard_map/broadcast_in_dim | solution.py:392
  (33 shorter events, 10.5 us)
Async XLA Ops:
  0.6 6.2 %collective-permute-start = (bf16[4,32,4096]{2,1,0:T(8,128)(2,1)}, bf16[4,32,4096]{2,1,0:T(8,128)(2,1)S(1)}, u32[]{:S(2)}, u32[]{:S(2)}) collective-permute-start(bf16[4,32,4096]{2,1,0:T(8,128)(2,1)} %bitcast.13), channel_id=1, source_target_pairs={{0,1},{1,0},{2,3},{3,2},{4,5},{5,4},{6,7},{7,6},{8,9},{9,8},{10,11... | collective-permute-start | bytes 3145736 | tf_op jit(solution)/shard_map/ppermute | solution.py:353
  0.7 5.7 %collective-permute-start.2 = (bf16[2,32,4096]{2,1,0:T(8,128)(2,1)}, bf16[2,32,4096]{2,1,0:T(8,128)(2,1)S(1)}, u32[]{:S(2)}, u32[]{:S(2)}) collective-permute-start(bf16[2,32,4096]{2,1,0:T(8,128)(2,1)} %bitcast.17), channel_id=1, source_target_pairs={{1,0},{3,2},{5,4},{7,6},{9,8},{11,10},{13,12},{15,14},{17,16},{19,... | collective-permute-start | bytes 1572872 | tf_op jit(solution)/shard_map/ppermute | solution.py:353
  2.0 4.8 %collective-permute-start.1 = (bf16[2,32,4096]{2,1,0:T(8,128)(2,1)}, bf16[2,32,4096]{2,1,0:T(8,128)(2,1)S(1)}, u32[]{:S(2)}, u32[]{:S(2)}) collective-permute-start(bf16[2,32,4096]{2,1,0:T(8,128)(2,1)} %bitcast.15), channel_id=1, source_target_pairs={{0,1},{2,3},{4,5},{6,7},{8,9},{10,11},{12,13},{14,15},{16,17},{18,... | collective-permute-start | bytes 1572872 | tf_op jit(solution)/shard_map/ppermute | solution.py:353
  6.8 39.6 %collective-permute-start.6 = (bf16[2,32,4096]{2,1,0:T(8,128)(2,1)}, bf16[2,32,4096]{2,1,0:T(8,128)(2,1)S(1)}, u32[]{:S(2)}, u32[]{:S(2)}) collective-permute-start(bf16[2,32,4096]{2,1,0:T(8,128)(2,1)} %bitcast.18), channel_id=1, source_target_pairs={{2,0},{4,2},{6,4},{8,6},{10,8},{12,10},{14,12},{16,14},{18,16},{20... | collective-permute-start | bytes 1572872 | tf_op jit(solution)/shard_map/ppermute | solution.py:353
  15.5 30.9 %collective-permute-start.7 = (bf16[2,32,4096]{2,1,0:T(8,128)(2,1)}, bf16[2,32,4096]{2,1,0:T(8,128)(2,1)S(1)}, u32[]{:S(2)}, u32[]{:S(2)}) collective-permute-start(bf16[2,32,4096]{2,1,0:T(8,128)(2,1)} %bitcast.19), channel_id=1, source_target_pairs={{2,1},{4,3},{6,5},{8,7},{10,9},{12,11},{14,13},{16,15},{18,17},{20... | collective-permute-start | bytes 1572872 | tf_op jit(solution)/shard_map/ppermute | solution.py:353
  16.8 29.6 %collective-permute-start.4 = (bf16[2,32,4096]{2,1,0:T(8,128)(2,1)S(1)}, bf16[2,32,4096]{2,1,0:T(8,128)(2,1)S(1)}, u32[]{:S(2)}, u32[]{:S(2)}) collective-permute-start(bf16[2,32,4096]{2,1,0:T(8,128)(2,1)S(1)} %get-tuple-element.31), channel_id=1, source_target_pairs={{2,0},{4,2},{6,4},{8,6},{10,8},{12,10},{14,12},{16,14},{18,16},{20... | collective-permute-start | bytes 1572872 | tf_op jit(solution)/shard_map/ppermute | solution.py:353
  19.1 27.3 %collective-permute-start.5 = (bf16[2,32,4096]{2,1,0:T(8,128)(2,1)S(1)}, bf16[2,32,4096]{2,1,0:T(8,128)(2,1)S(1)}, u32[]{:S(2)}, u32[]{:S(2)}) collective-permute-start(bf16[2,32,4096]{2,1,0:T(8,128)(2,1)S(1)} %get-tuple-element.32), channel_id=1, source_target_pairs={{2,1},{4,3},{6,5},{8,7},{10,9},{12,11},{14,13},{16,15},{18,17},{20... | collective-permute-start | bytes 1572872 | tf_op jit(solution)/shard_map/ppermute | solution.py:353
  20.5 1.2 %copy-start.4 = (bf16[1,4,32,4096]{3,2,1,0:T(8,128)(2,1)S(1)}, bf16[1,4,32,4096]{3,2,1,0:T(8,128)(2,1)}, u32[]{:S(2)}) copy-start(bf16[1,4,32,4096]{3,2,1,0:T(8,128)(2,1)} %param.5) | copy-start | bytes 3145732
  21.7 1.0 copy-start.5
  22.7 1.0 copy-start.7
  23.8 0.7 copy-start.8
  24.5 0.7 copy-start.9
  41.5 1.2 %collective-permute-start.3 = (f32[8,128]{1,0:T(8,128)S(1)}, f32[8,128]{1,0:T(8,128)S(1)}, u32[]{:S(2)}, u32[]{:S(2)}) collective-permute-start(f32[8,128]{1,0:T(8,128)S(1)} %get-tuple-element.27.own), channel_id=1, source_target_pairs={{0,1},{1,0},{2,3},{3,2},{4,5},{5,4},{6,7},{7,6},{8,9},{9,8},{10,11... | collective-permute-start | bytes 12296 | tf_op jit(solution)/shard_map/ppermute | solution.py:353
  46.5 3.4 %collective-permute-start.8 = (bf16[2,32,4096]{2,1,0:T(8,128)(2,1)S(1)}, bf16[2,32,4096]{2,1,0:T(8,128)(2,1)S(1)}, u32[]{:S(2)}, u32[]{:S(2)}) collective-permute-start(bf16[2,32,4096]{2,1,0:T(8,128)(2,1)S(1)} %project.2.refs_2_), channel_id=1, source_target_pairs={{0,1},{1,0},{2,3},{3,2},{4,5},{5,4},{6,7},{7,6},{8,9},{9,8},{10,11... | collective-permute-start | bytes 1572872 | tf_op jit(solution)/shard_map/ppermute | solution.py:353
  66.7 4.0 %copy-start = (bf16[5,4,32,64,128]{4,3,2,1,0:T(8,128)(2,1)}, bf16[5,4,32,64,128]{4,3,2,1,0:T(8,128)(2,1)S(1)}, u32[]{:S(2)}) copy-start(bf16[5,4,32,64,128]{4,3,2,1,0:T(8,128)(2,1)S(1)} %get-tuple-element.43.u) | copy-start | bytes 31457284
  70.7 2.1 %copy-start.2 = (f32[4,32,64,128]{3,2,1,0:T(8,128)}, f32[4,32,64,128]{3,2,1,0:T(8,128)S(1)}, u32[]{:S(2)}) copy-start(f32[4,32,64,128]{3,2,1,0:T(8,128)S(1)} %get-tuple-element.44.last) | copy-start | bytes 12582916
  75.7 18.3 %collective-permute-start.12 = (bf16[2,32,4096]{2,1,0:T(8,128)(2,1)S(1)}, bf16[2,32,4096]{2,1,0:T(8,128)(2,1)}, u32[]{:S(2)}, u32[]{:S(2)}) collective-permute-start(bf16[2,32,4096]{2,1,0:T(8,128)(2,1)S(1)} %grow.3), channel_id=1, source_target_pairs={{1,2},{3,4},{5,6},{7,8},{9,10},{11,12},{13,14},{15,16},{17,18},{19... | collective-permute-start | bytes 1572872 | tf_op jit(solution)/shard_map/ppermute | solution.py:353
  77.0 4.0 %collective-permute-start.9 = (f32[8,128]{1,0:T(8,128)S(1)}, f32[8,128]{1,0:T(8,128)S(1)}, u32[]{:S(2)}, u32[]{:S(2)}) collective-permute-start(f32[8,128]{1,0:T(8,128)S(1)} %get-tuple-element.42.own), channel_id=1, source_target_pairs={{0,1},{1,0},{2,3},{3,2},{4,5},{5,4},{6,7},{7,6},{8,9},{9,8},{10,11... | collective-permute-start | bytes 12296 | tf_op jit(solution)/shard_map/ppermute | solution.py:353
  81.0 4.0 %copy-start.1 = (bf16[5,4,32,64,128]{4,3,2,1,0:T(8,128)(2,1)S(1)}, bf16[5,4,32,64,128]{4,3,2,1,0:T(8,128)(2,1)}, u32[]{:S(2)}) copy-start(bf16[5,4,32,64,128]{4,3,2,1,0:T(8,128)(2,1)} %copy-done) | copy-start | bytes 31457284
  85.0 2.2 %copy-start.3 = (f32[4,32,64,128]{3,2,1,0:T(8,128)S(1)}, f32[4,32,64,128]{3,2,1,0:T(8,128)}, u32[]{:S(2)}) copy-start(f32[4,32,64,128]{3,2,1,0:T(8,128)} %copy-done.2) | copy-start | bytes 12582916
  87.2 6.9 %copy-start.6 = (bf16[1,2,32,4096]{3,2,1,0:T(8,128)(2,1)S(1)}, bf16[1,2,32,4096]{3,2,1,0:T(8,128)(2,1)}, u32[]{:S(2)}) copy-start(bf16[1,2,32,4096]{3,2,1,0:T(8,128)(2,1)} %param.6) | copy-start | bytes 1572868
  90.8 18.4 %collective-permute-start.11 = (bf16[2,32,4096]{2,1,0:T(8,128)(2,1)S(1)}, bf16[2,32,4096]{2,1,0:T(8,128)(2,1)S(1)}, u32[]{:S(2)}, u32[]{:S(2)}) collective-permute-start(bf16[2,32,4096]{2,1,0:T(8,128)(2,1)S(1)} %project.3), channel_id=1, source_target_pairs={{1,2},{3,4},{5,6},{7,8},{9,10},{11,12},{13,14},{15,16},{17,18},{19... | collective-permute-start | bytes 1572872 | tf_op jit(solution)/shard_map/ppermute | solution.py:353
  92.1 19.0 %collective-permute-start.10 = (bf16[2,32,4096]{2,1,0:T(8,128)(2,1)S(1)}, bf16[2,32,4096]{2,1,0:T(8,128)(2,1)S(1)}, u32[]{:S(2)}, u32[]{:S(2)}) collective-permute-start(bf16[2,32,4096]{2,1,0:T(8,128)(2,1)S(1)} %project.3), channel_id=1, source_target_pairs={{0,2},{2,4},{4,6},{6,8},{8,10},{10,12},{12,14},{14,16},{16,18},{18... | collective-permute-start | bytes 1572872 | tf_op jit(solution)/shard_map/ppermute | solution.py:353

commit v4 on v3

--- a/solution.py
+++ b/solution.py
@@ -58,14 +58,14 @@
 def krylov_kernel(second, core_of, *refs):
     if second:
         coup, kept, own, got, b_even, b_odd, r_even, r_odd, left_raw = refs[:9]
-        outs = refs[9:14]
-        scratch = refs[14:]
+        outs = refs[9:15]
+        scratch = refs[15:]
     else:
         coup, kept, own, got, own_l, got_l, own_r, got_r = refs[:8]
         outs = refs[8:14]
         scratch = refs[14:]
     u, last, small, at, a_flat = outs[:5]
-    a_raw, ab, lb, rb, bcat, w, sems, moments, b_raw, r_raw = scratch
+    a_raw, ab, lb, rb, bcat, w, sems, moments, b_raw, r_raw, eb = scratch
     y = last
     core = core_of()
 
@@ -121,13 +121,7 @@
         bcat[:, :, h * BS : (h + 1) * BS] = b_raw[h].reshape(NB, BS, BS)
 
     if second:
-        total = jnp.zeros((8, 128), F32)
-        for s in range(PHYS):
-            for t in range(FLAT // 128):
-                x = a_raw[s, :, t * 128 : (t + 1) * 128].astype(F32)
-                x = x * x
-                total = total + (x[0:8] + x[8:16]) + (x[16:24] + x[24:32])
-        factor = lax.rsqrt(jnp.sum(total, keepdims=True) / (PHYS * NB * FLAT) + EPSILON)
+        factor = norm_factor(sum_squares(a_raw, PHYS))
     for s in range(PHYS):
         x = a_raw[s]
         if second:
@@ -181,6 +175,8 @@
     for q in range(NB):
         out = jnp.where((row == 1) & (column == q), kept[0, q].astype(F32), out)
     small[...] = out
+    if second:
+        env_part(left_raw, at, outs[5], ab, lb, u.at[ITERS], eb)
 
 
 def project_kernel(owner, core_of, own, got, u, last, at, x_out, v, xb):
@@ -222,12 +218,9 @@
         x_out[h] = xb[h].reshape(NB, FLAT)
 
 
-def env_kernel(a_flat, left, at, env, ab, lb, hb, eb):
-    for s in range(PHYS):
-        ab[s] = a_flat[s].reshape(NB, BS, BS)
+def env_part(left, at, env, ab, lb, hb, eb):
     mixed = (left[0].astype(F32) + left[1].astype(F32)).astype(BF16)
     lb[:, :, :BS] = mixed.reshape(NB, BS, BS)
-    lb[:, :, BS:] = left[1].reshape(NB, BS, BS)
     for q in range(NB):
         lhs = jnp.concatenate(
             [at[plus(q, s), :, s * BS : (s + 1) * BS] for s in range(PHYS)], 0
@@ -250,6 +243,47 @@
         env[ch] = eb[ch].reshape(NB, FLAT)
 
 
+def env_kernel(a_flat, left, at, env, ab, lb, hb, eb):
+    for s in range(PHYS):
+        ab[s] = a_flat[s].reshape(NB, BS, BS)
+    lb[:, :, BS:] = left[1].reshape(NB, BS, BS)
+    env_part(left, at, env, ab, lb, hb, eb)
+
+
+def sum_squares(ref, states):
+    total = jnp.zeros((8, 128), F32)
+    for s in range(states):
+        for t in range(FLAT // 128):
+            x = ref[s, :, t * 128 : (t + 1) * 128].astype(F32)
+            x = x * x
+            total = total + (x[0:8] + x[8:16]) + (x[16:24] + x[24:32])
+    return total
+
+
+def norm_factor(total):
+    return lax.rsqrt(jnp.sum(total, keepdims=True) / (PHYS * NB * FLAT) + EPSILON)
+
+
+def choose_kernel(tensor, new, low, high, out):
+    odd = lax.rem(lax.axis_index("site"), 2) == 1
+    first = jnp.logical_and(lax.axis_index("site") == 0, lax.axis_index("sec") == 0)
+
+    @pl.when(odd)
+    def _():
+        out[...] = new[...]
+
+    @pl.when(first)
+    def _():
+        out[...] = tensor[...]
+
+    @pl.when(jnp.logical_not(jnp.logical_or(odd, first)))
+    def _():
+        factor = norm_factor(sum_squares(low, HALF) + sum_squares(high, HALF))
+        for s in range(HALF):
+            out[s] = scaled_copy(low[s], factor)
+            out[HALF + s] = scaled_copy(high[s], factor)
+
+
 def shape(*dims, dtype=BF16):
     return jax.ShapeDtypeStruct(dims, dtype)
 
@@ -265,9 +299,8 @@
         shape(8, 128, dtype=F32),
         shape(NB, BS, PHYS * BS),
         shape(PHYS, NB, FLAT),
+        shape(2, NB, FLAT),
     ]
-    if not second:
-        outs.append(shape(2, NB, FLAT))
     scratch = [
         pltpu.VMEM((PHYS, NB, FLAT), BF16),
         pltpu.VMEM((PHYS, NB, BS, BS), BF16),
@@ -279,6 +312,7 @@
         pltpu.VMEM((2 * ITERS, 8, LN), F32),
         pltpu.VMEM((HALF, NB, FLAT), BF16),
         pltpu.VMEM((2, NB, FLAT), BF16),
+        pltpu.VMEM((2, NB, BS, BS), BF16),
     ]
     if second:
         specs = [SM, SM] + [HB] * 6 + [VM]
@@ -290,7 +324,7 @@
         in_specs=specs,
         out_specs=(VM,) * len(outs),
         scratch_shapes=scratch,
-        compiler_params=params(28),
+        compiler_params=params(30),
         cost_estimate=pl.CostEstimate(flops=10**11, bytes_accessed=2**24, transcendentals=0),
         name="krylov",
     )(coupling, kept, *arrays)
@@ -330,6 +364,17 @@
     )(a_flat, left, at)
 
 
+def choose(tensor, new, low, high):
+    return pl.pallas_call(
+        choose_kernel,
+        out_shape=shape(PHYS, NB, FLAT),
+        in_specs=[VM] * 4,
+        out_specs=VM,
+        compiler_params=params(8),
+        name="choose",
+    )(tensor, new, low, high)
+
+
 def core_index():
     return lax.rem(lax.axis_index("site"), 2)
 
@@ -372,22 +417,18 @@
     x, b_even, b_odd, r_even, r_odd = lax.optimization_barrier((x, b_even, b_odd, r_even, r_odd))
     got_x = send(x, swap)
 
-    u, last, small, at, new1 = krylov(
+    u, last, small, at, new1, env2 = krylov(
         core_index, True, coupling, kept_rows, x, got_x, b_even, b_odd, r_even, r_odd, env1
     )
     got_small = send(small, swap)
-    env2 = grow(new1, env1, at)
     x = project(core_index, 1, small, got_small, u, last, at)
     low = send(x, from_even)
     high = send(x, from_odd)
     got_env = send(env2, from_odd)
 
-    squares = jnp.sum(jnp.square(low.astype(F32))) + jnp.sum(jnp.square(high.astype(F32)))
-    factor = lax.rsqrt(squares / (PHYS * NB * FLAT) + EPSILON)
-    received = scaled_copy(jnp.concatenate([low, high], 0), factor)
     odd = position % 2 == 1
     first = position == 0
-    out_new = jnp.where(odd, new1, jnp.where(first, tensor, received))
+    out_new = choose(tensor, new1, low, high)
     out_env = jnp.where(odd, env1, jnp.where(first, left, got_env))
     return out_new[None], out_env[None]
 

time: 116 us -> 121 us (1.043)
  local copies, waits for them, and re-layouts: 18.2 us -> 23.3 us
  other arithmetic: 6.19 us -> 1.91 us
  Pallas kernels: 46.4 us -> 49.5 us
  waiting for transfers between devices: 16.6 us -> 18.2 us
    unnamed x20 -> x42, local copies, waits for them, and re-layouts: 16.9 us -> 22 us
    pallas_call x2, Pallas kernels: 33.2 us -> 37.5 us  [krylov(): pl.pallas_call(functools.partial(krylov_kernel, second, core_of), out_sha...]
    pallas_call x2 -> x1, Pallas kernels: 5.99 us -> 3.06 us  [grow(): pl.pallas_call(env_kernel, out_shape=shape(2, NB, FLAT), in_specs=[VM] *...]
    broadcast_in_dim x2 -> x1, other arithmetic: 4.45 us -> 1.91 us  [shards(): return (out_new[None], out_env[None])]
    reduce_sum x2 -> x0, other arithmetic: 1.74 us -> none  [the longest x1 0.87 us: shards(): jnp.sum(jnp.square(high.astype(F32)))]
    pallas_call x0 -> x1, Pallas kernels: none -> 1.55 us  [choose(): pl.pallas_call(choose_kernel, out_shape=shape(PHYS, NB, FLAT), in_specs=[...]
    ppermute x13, waiting for transfers between devices: 16.6 us -> 18.2 us  [send(): return lax.ppermute(x, axes, pairs)]
  transfers between devices with their start and end apart: 13 -> 13, of which waited for: 5 -> 5; matrix products, arithmetic and copies ran while one was open for 4% -> 3% of each run, Pallas kernels for 23% -> 23%
where the time goes in v4:
time: 121 us; the launch traced here: 120 us
  Pallas kernels  49.5 us (41%)
  starting transfers between devices  26.3 us (22%)
  local copies, waits for them, and re-layouts  23.3 us (19%)
  waiting for transfers between devices  18.2 us (15%)
  other arithmetic  1.91 us (2%)
    pallas_call x2, Pallas kernels, krylov(): pl.pallas_call(functools.partial(krylov_kernel, second, core_of), out_sha...  37.5 us
    ppermute x13, starting transfers between devices, send(): return lax.ppermute(x, axes, pairs)  26.3 us
    unnamed x42, local copies, waits for them, and re-layouts  22 us
    ppermute x13, waiting for transfers between devices, send(): return lax.ppermute(x, axes, pairs)  18.2 us
    pallas_call x2, Pallas kernels, project(): pl.pallas_call(functools.partial(project_kernel, owner, core_of), out_sha...  7.34 us
    pallas_call x1, Pallas kernels, grow(): pl.pallas_call(env_kernel, out_shape=shape(2, NB, FLAT), in_specs=[VM] *...  3.06 us
  transfers between devices with their start and end apart: 13, of which 5 were waited for; matrix products, arithmetic and copies ran while one was open for 3% of the time, Pallas kernels for 23%

profile of v4, /device:TPU:6, one launch (start us, length us, event | category | flops | bytes accessed | tf_op | source)
XLA Modules:
  0.0 120.0 jit_solution(12392892593726412586)
XLA Ops:
  0.7 1.3 %collective-permute-start.2 = (bf16[2,32,4096]{2,1,0:T(8,128)(2,1)}, bf16[2,32,4096]{2,1,0:T(8,128)(2,1)S(1)}, u32[]{:S(2)}, u32[]{:S(2)}) collective-permute-start(bf16[2,32,4096]{2,1,0:T(8,128)(2,1)} %bitcast.16), channel_id=1, source_target_pairs={{1,0},{3,2},{5,4},{7,6},{9,8},{11,10},{13,12},{15,14},{17,16},{19,... | collective-permute-start | bytes 1572872 | tf_op jit(solution)/shard_map/ppermute | solution.py:398
  2.0 3.1 %collective-permute-start.1 = (bf16[2,32,4096]{2,1,0:T(8,128)(2,1)}, bf16[2,32,4096]{2,1,0:T(8,128)(2,1)S(1)}, u32[]{:S(2)}, u32[]{:S(2)}) collective-permute-start(bf16[2,32,4096]{2,1,0:T(8,128)(2,1)} %bitcast.14), channel_id=1, source_target_pairs={{0,1},{2,3},{4,5},{6,7},{8,9},{10,11},{12,13},{14,15},{16,17},{18,... | collective-permute-start | bytes 1572872 | tf_op jit(solution)/shard_map/ppermute | solution.py:398
  5.1 1.3 %slice_bitcast_fusion = (bf16[2,32,4096]{2,1,0:T(8,128)(2,1)S(1)}, bf16[2,32,4096]{2,1,0:T(8,128)(2,1)S(1)}) fusion(bf16[1,4,32,4096]{3,2,1,0:T(8,128)(2,1)} %param.5), kind=kLoop, calls=%fused_computation.1 | loop fusion | bytes 2097152 | tf_op jit(solution)/shard_map/slice | solution.py:404
  6.8 8.7 %collective-permute-start.6 = (bf16[2,32,4096]{2,1,0:T(8,128)(2,1)}, bf16[2,32,4096]{2,1,0:T(8,128)(2,1)S(1)}, u32[]{:S(2)}, u32[]{:S(2)}) collective-permute-start(bf16[2,32,4096]{2,1,0:T(8,128)(2,1)} %bitcast.17), channel_id=1, source_target_pairs={{2,0},{4,2},{6,4},{8,6},{10,8},{12,10},{14,12},{16,14},{18,16},{20... | collective-permute-start | bytes 1572872 | tf_op jit(solution)/shard_map/ppermute | solution.py:398
  15.5 1.3 %collective-permute-start.7 = (bf16[2,32,4096]{2,1,0:T(8,128)(2,1)}, bf16[2,32,4096]{2,1,0:T(8,128)(2,1)S(1)}, u32[]{:S(2)}, u32[]{:S(2)}) collective-permute-start(bf16[2,32,4096]{2,1,0:T(8,128)(2,1)} %bitcast.18), channel_id=1, source_target_pairs={{2,1},{4,3},{6,5},{8,7},{10,9},{12,11},{14,13},{16,15},{18,17},{20... | collective-permute-start | bytes 1572872 | tf_op jit(solution)/shard_map/ppermute | solution.py:398
  16.8 2.3 %collective-permute-start.4 = (bf16[2,32,4096]{2,1,0:T(8,128)(2,1)S(1)}, bf16[2,32,4096]{2,1,0:T(8,128)(2,1)S(1)}, u32[]{:S(2)}, u32[]{:S(2)}) collective-permute-start(bf16[2,32,4096]{2,1,0:T(8,128)(2,1)S(1)} %get-tuple-element.32), channel_id=1, source_target_pairs={{2,0},{4,2},{6,4},{8,6},{10,8},{12,10},{14,12},{16,14},{18,16},{20... | collective-permute-start | bytes 1572872 | tf_op jit(solution)/shard_map/ppermute | solution.py:398
  19.1 1.3 %collective-permute-start.5 = (bf16[2,32,4096]{2,1,0:T(8,128)(2,1)S(1)}, bf16[2,32,4096]{2,1,0:T(8,128)(2,1)S(1)}, u32[]{:S(2)}, u32[]{:S(2)}) collective-permute-start(bf16[2,32,4096]{2,1,0:T(8,128)(2,1)S(1)} %get-tuple-element.33), channel_id=1, source_target_pairs={{2,1},{4,3},{6,5},{8,7},{10,9},{12,11},{14,13},{16,15},{18,17},{20... | collective-permute-start | bytes 1572872 | tf_op jit(solution)/shard_map/ppermute | solution.py:398
  25.1 17.3 %krylov.2 = (bf16[5,4,32,64,128]{4,3,2,1,0:T(8,128)(2,1)S(1)}, f32[4,32,64,128]{3,2,1,0:T(8,128)S(1)}, f32[8,128]{1,0:T(8,128)S(1)}, bf16[32,64,256]{2,1,0:T(8,1...) custom-call(f32[4,4]{1,0:T(4,128)S(1)} %copy-done.19, s32[1,32]{1,0:T(1,128)S(1)} %copy-done.20, ...), custom_call_target="tpu_custom_call" | custom-call | flops 99999997952 | bytes 16777216 | tf_op jit(solution)/shard_map/krylov/pallas_call | solution.py:321
  43.7 3.7 %project.2.refs_2_ = bf16[2,32,4096]{2,1,0:T(8,128)(2,1)S(1)} custom-call(f32[8,128]{1,0:T(8,128)S(1)} %get-tuple-element.28.own, f32[8,128]{1,0:T(8,128)S(1)} %collective-permute-done.3.got, bf16[5,4,32,64,128]{4,3,2,1,0:T(8,128)(2,1)S(1)} %get-tuple-element.29.u, f32[4,32,64,128]{3,2,1,0:T(8,128)S(1)} %get-tuple-element.30.last, ...), custom_call_target="tpu_custom_call" | custom-call | flops 1000000 | bytes 1024 | tf_op jit(solution)/shard_map/project/pallas_call | solution.py:334
  47.9 3.1 %grow.1.refs_8_ = bf16[2,32,4096]{2,1,0:T(8,128)(2,1)S(1)} custom-call(bf16[4,32,4096]{2,1,0:T(8,128)(2,1)S(1)} %get-tuple-element.40.a_flat, bf16[2,32,4096]{2,1,0:T(8,128)(2,1)S(1)} %get-tuple-element.41.left, bf16[32,64,256]{2,1,0:T(8,128)(2,1)S(1)} %get-tuple-element.31.at), custom_call_target="tpu_custom_call" | custom-call | flops 1000000 | bytes 1024 | tf_op jit(solution)/shard_map/grow/pallas_call | solution.py:350
  55.2 20.2 %krylov.3 = (bf16[5,4,32,64,128]{4,3,2,1,0:T(8,128)(2,1)S(1)}, f32[4,32,64,128]{3,2,1,0:T(8,128)S(1)}, f32[8,128]{1,0:T(8,128)S(1)}, bf16[32,64,256]{2,1,0:T(8,1...) custom-call(f32[4,4]{1,0:T(4,128)S(1)} %copy-done.19, s32[1,32]{1,0:T(1,128)S(1)} %copy-done.20, ...), custom_call_target="tpu_custom_call" | custom-call | flops 99999997952 | bytes 16777216 | tf_op jit(solution)/shard_map/krylov/pallas_call | solution.py:321
  75.4 4.0 %copy-done = bf16[5,4,32,64,128]{4,3,2,1,0:T(8,128)(2,1)} copy-done((bf16[5,4,32,64,128]{4,3,2,1,0:T(8,128)(2,1)}, bf16[5,4,32,64,128]{4,3,2,1,0:T(8,128)(2,1)S(1)}, u32[]{:S(2)}) %copy-start) | copy-done | bytes 10485784
  79.4 2.0 %copy-done.2 = f32[4,32,64,128]{3,2,1,0:T(8,128)} copy-done((f32[4,32,64,128]{3,2,1,0:T(8,128)}, f32[4,32,64,128]{3,2,1,0:T(8,128)S(1)}, u32[]{:S(2)}) %copy-start.2) | copy-done | bytes 4194328
  82.4 1.3 %collective-permute-start.12 = (bf16[2,32,4096]{2,1,0:T(8,128)(2,1)}, bf16[2,32,4096]{2,1,0:T(8,128)(2,1)}, u32[]{:S(2)}, u32[]{:S(2)}) collective-permute-start(bf16[2,32,4096]{2,1,0:T(8,128)(2,1)} %get-tuple-element.47), channel_id=1, source_target_pairs={{1,2},{3,4},{5,6},{7,8},{9,10},{11,12},{13,14},{15,16},{17,18},{19... | collective-permute-start | bytes 1572872 | tf_op jit(solution)/shard_map/ppermute | solution.py:398
  83.7 3.2 %collective-permute-start.9 = (f32[8,128]{1,0:T(8,128)S(1)}, f32[8,128]{1,0:T(8,128)S(1)}, u32[]{:S(2)}, u32[]{:S(2)}) collective-permute-start(f32[8,128]{1,0:T(8,128)S(1)} %get-tuple-element.43.own), channel_id=1, source_target_pairs={{0,1},{1,0},{2,3},{3,2},{4,5},{5,4},{6,7},{7,6},{8,9},{9,8},{10,11... | collective-permute-start | bytes 12296 | tf_op jit(solution)/shard_map/ppermute | solution.py:398
  87.7 4.0 %copy-done.1 = bf16[5,4,32,64,128]{4,3,2,1,0:T(8,128)(2,1)S(1)} copy-done((bf16[5,4,32,64,128]{4,3,2,1,0:T(8,128)(2,1)S(1)}, bf16[5,4,32,64,128]{4,3,2,1,0:T(8,128)(2,1)}, u32[]{:S(2)}) %copy-start.1) | copy-done | bytes 10485784
  91.7 2.2 %copy-done.3 = f32[4,32,64,128]{3,2,1,0:T(8,128)S(1)} copy-done((f32[4,32,64,128]{3,2,1,0:T(8,128)S(1)}, f32[4,32,64,128]{3,2,1,0:T(8,128)}, u32[]{:S(2)}) %copy-start.3) | copy-done | bytes 4194328
  93.9 3.6 %project.3 = bf16[2,32,4096]{2,1,0:T(8,128)(2,1)S(1)} custom-call(f32[8,128]{1,0:T(8,128)S(1)} %get-tuple-element.43.own, f32[8,128]{1,0:T(8,128)S(1)} %collective-permute-done.9.got, bf16[5,4,32,64,128]{4,3,2,1,0:T(8,128)(2,1)S(1)} %copy-done.1, f32[4,32,64,128]{3,2,1,0:T(8,128)S(1)} %copy-done.3, bf16[32,64,256]{2,1,0:T(8,128)(2,1)S(1)} %get-tuple-element.46.at), custom_call_target="tpu_custom_call" | custom-call | flops 1000000 | bytes 1024 | tf_op jit(solution)/shard_map/project/pallas_call | solution.py:334
  97.5 1.9 %collective-permute-start.10 = (bf16[2,32,4096]{2,1,0:T(8,128)(2,1)S(1)}, bf16[2,32,4096]{2,1,0:T(8,128)(2,1)S(1)}, u32[]{:S(2)}, u32[]{:S(2)}) collective-permute-start(bf16[2,32,4096]{2,1,0:T(8,128)(2,1)S(1)} %project.3), channel_id=1, source_target_pairs={{0,2},{2,4},{4,6},{6,8},{8,10},{10,12},{12,14},{14,16},{16,18},{18... | collective-permute-start | bytes 1572872 | tf_op jit(solution)/shard_map/ppermute | solution.py:398
  99.4 1.3 %collective-permute-start.11 = (bf16[2,32,4096]{2,1,0:T(8,128)(2,1)S(1)}, bf16[2,32,4096]{2,1,0:T(8,128)(2,1)S(1)}, u32[]{:S(2)}, u32[]{:S(2)}) collective-permute-start(bf16[2,32,4096]{2,1,0:T(8,128)(2,1)S(1)} %project.3), channel_id=1, source_target_pairs={{1,2},{3,4},{5,6},{7,8},{9,10},{11,12},{13,14},{15,16},{17,18},{19... | collective-permute-start | bytes 1572872 | tf_op jit(solution)/shard_map/ppermute | solution.py:398
  100.8 1.9 %select_bitcast_fusion = bf16[1,2,32,4096]{3,2,1,0:T(8,128)(2,1)} fusion(bf16[2,32,4096]{2,1,0:T(8,128)(2,1)S(1)} %grow.1.refs_8_, bf16[2,32,4096]{2,1,0:T(8,128)(2,1)} %collective-permute-done.12, pred[]{:T(512)S(6)} %eq.9, pred[]{:T(512)S(6)} %eq.8, bf16[1,2,32,4096]{3,2,1,0:T(8,128)(2,1)S(1)} %copy-done.9), kind=kLoop, calls=%fused_computation | loop fusion | flops 524288 | bytes 2097154 | tf_op jit(solution)/shard_map/broadcast_in_dim | solution.py:433
  102.7 14.3 %collective-permute-done.10.low = bf16[2,32,4096]{2,1,0:T(8,128)(2,1)S(1)} collective-permute-done((bf16[2,32,4096]{2,1,0:T(8,128)(2,1)S(1)}, bf16[2,32,4096]{2,1,0:T(8,128)(2,1)S(1)}, u32[]{:S(2)}, u32[]{:S(2)}) %collective-permute-start.10) | collective-permute-done | bytes 524320 | tf_op jit(solution)/shard_map/ppermute | solution.py:398
  117.0 1.4 %collective-permute-done.11.high = bf16[2,32,4096]{2,1,0:T(8,128)(2,1)S(1)} collective-permute-done((bf16[2,32,4096]{2,1,0:T(8,128)(2,1)S(1)}, bf16[2,32,4096]{2,1,0:T(8,128)(2,1)S(1)}, u32[]{:S(2)}, u32[]{:S(2)}) %collective-permute-start.11) | collective-permute-done | bytes 524320 | tf_op jit(solution)/shard_map/ppermute | solution.py:398
  118.4 1.6 %choose.1 = bf16[4,32,4096]{2,1,0:T(8,128)(2,1)} custom-call(bf16[4,32,4096]{2,1,0:T(8,128)(2,1)S(1)} %bitcast.13, bf16[4,32,4096]{2,1,0:T(8,128)(2,1)S(1)} %copy-done.7, bf16[2,32,4096]{2,1,0:T(8,128)(2,1)S(1)} %collective-permute-done.10.low, bf16[2,32,4096]{2,1,0:T(8,128)(2,1)S(1)} %collective-permute-done.11.high), custom_call_target="tpu_custom_call" | custom-call | tf_op jit(solution)/shard_map/choose/pallas_call | solution.py:368
  (52 shorter events, 12.8 us)
Async XLA Ops:
  0.6 6.2 %collective-permute-start = (bf16[4,32,4096]{2,1,0:T(8,128)(2,1)}, bf16[4,32,4096]{2,1,0:T(8,128)(2,1)S(1)}, u32[]{:S(2)}, u32[]{:S(2)}) collective-permute-start(bf16[4,32,4096]{2,1,0:T(8,128)(2,1)} %bitcast.11), channel_id=1, source_target_pairs={{0,1},{1,0},{2,3},{3,2},{4,5},{5,4},{6,7},{7,6},{8,9},{9,8},{10,11... | collective-permute-start | bytes 3145736 | tf_op jit(solution)/shard_map/ppermute | solution.py:398
  0.7 5.7 %collective-permute-start.2 = (bf16[2,32,4096]{2,1,0:T(8,128)(2,1)}, bf16[2,32,4096]{2,1,0:T(8,128)(2,1)S(1)}, u32[]{:S(2)}, u32[]{:S(2)}) collective-permute-start(bf16[2,32,4096]{2,1,0:T(8,128)(2,1)} %bitcast.16), channel_id=1, source_target_pairs={{1,0},{3,2},{5,4},{7,6},{9,8},{11,10},{13,12},{15,14},{17,16},{19,... | collective-permute-start | bytes 1572872 | tf_op jit(solution)/shard_map/ppermute | solution.py:398
  2.0 4.8 %collective-permute-start.1 = (bf16[2,32,4096]{2,1,0:T(8,128)(2,1)}, bf16[2,32,4096]{2,1,0:T(8,128)(2,1)S(1)}, u32[]{:S(2)}, u32[]{:S(2)}) collective-permute-start(bf16[2,32,4096]{2,1,0:T(8,128)(2,1)} %bitcast.14), channel_id=1, source_target_pairs={{0,1},{2,3},{4,5},{6,7},{8,9},{10,11},{12,13},{14,15},{16,17},{18,... | collective-permute-start | bytes 1572872 | tf_op jit(solution)/shard_map/ppermute | solution.py:398
  6.8 40.6 %collective-permute-start.6 = (bf16[2,32,4096]{2,1,0:T(8,128)(2,1)}, bf16[2,32,4096]{2,1,0:T(8,128)(2,1)S(1)}, u32[]{:S(2)}, u32[]{:S(2)}) collective-permute-start(bf16[2,32,4096]{2,1,0:T(8,128)(2,1)} %bitcast.17), channel_id=1, source_target_pairs={{2,0},{4,2},{6,4},{8,6},{10,8},{12,10},{14,12},{16,14},{18,16},{20... | collective-permute-start | bytes 1572872 | tf_op jit(solution)/shard_map/ppermute | solution.py:398
  15.5 32.0 %collective-permute-start.7 = (bf16[2,32,4096]{2,1,0:T(8,128)(2,1)}, bf16[2,32,4096]{2,1,0:T(8,128)(2,1)S(1)}, u32[]{:S(2)}, u32[]{:S(2)}) collective-permute-start(bf16[2,32,4096]{2,1,0:T(8,128)(2,1)} %bitcast.18), channel_id=1, source_target_pairs={{2,1},{4,3},{6,5},{8,7},{10,9},{12,11},{14,13},{16,15},{18,17},{20... | collective-permute-start | bytes 1572872 | tf_op jit(solution)/shard_map/ppermute | solution.py:398
  16.8 30.6 %collective-permute-start.4 = (bf16[2,32,4096]{2,1,0:T(8,128)(2,1)S(1)}, bf16[2,32,4096]{2,1,0:T(8,128)(2,1)S(1)}, u32[]{:S(2)}, u32[]{:S(2)}) collective-permute-start(bf16[2,32,4096]{2,1,0:T(8,128)(2,1)S(1)} %get-tuple-element.32), channel_id=1, source_target_pairs={{2,0},{4,2},{6,4},{8,6},{10,8},{12,10},{14,12},{16,14},{18,16},{20... | collective-permute-start | bytes 1572872 | tf_op jit(solution)/shard_map/ppermute | solution.py:398
  19.1 28.3 %collective-permute-start.5 = (bf16[2,32,4096]{2,1,0:T(8,128)(2,1)S(1)}, bf16[2,32,4096]{2,1,0:T(8,128)(2,1)S(1)}, u32[]{:S(2)}, u32[]{:S(2)}) collective-permute-start(bf16[2,32,4096]{2,1,0:T(8,128)(2,1)S(1)} %get-tuple-element.33), channel_id=1, source_target_pairs={{2,1},{4,3},{6,5},{8,7},{10,9},{12,11},{14,13},{16,15},{18,17},{20... | collective-permute-start | bytes 1572872 | tf_op jit(solution)/shard_map/ppermute | solution.py:398
  42.5 1.2 %collective-permute-start.3 = (f32[8,128]{1,0:T(8,128)S(1)}, f32[8,128]{1,0:T(8,128)S(1)}, u32[]{:S(2)}, u32[]{:S(2)}) collective-permute-start(f32[8,128]{1,0:T(8,128)S(1)} %get-tuple-element.28.own), channel_id=1, source_target_pairs={{0,1},{1,0},{2,3},{3,2},{4,5},{5,4},{6,7},{7,6},{8,9},{9,8},{10,11... | collective-permute-start | bytes 12296 | tf_op jit(solution)/shard_map/ppermute | solution.py:398
  47.4 3.6 %copy-start.11 = (bf16[2,32,4096]{2,1,0:T(8,128)(2,1)}, bf16[2,32,4096]{2,1,0:T(8,128)(2,1)S(1)}, u32[]{:S(2)}) copy-start(bf16[2,32,4096]{2,1,0:T(8,128)(2,1)S(1)} %collective-permute-done.6.refs_6_) | copy-start | bytes 1572868
  47.4 3.6 %copy-start.13 = (bf16[2,32,4096]{2,1,0:T(8,128)(2,1)}, bf16[2,32,4096]{2,1,0:T(8,128)(2,1)S(1)}, u32[]{:S(2)}) copy-start(bf16[2,32,4096]{2,1,0:T(8,128)(2,1)S(1)} %collective-permute-done.7.refs_7_) | copy-start | bytes 1572868
  47.5 3.5 %copy-start.15 = (bf16[2,32,4096]{2,1,0:T(8,128)(2,1)}, bf16[2,32,4096]{2,1,0:T(8,128)(2,1)S(1)}, u32[]{:S(2)}) copy-start(bf16[2,32,4096]{2,1,0:T(8,128)(2,1)S(1)} %collective-permute-done.4.refs_4_) | copy-start | bytes 1572868
  47.5 3.5 %copy-start.17 = (bf16[2,32,4096]{2,1,0:T(8,128)(2,1)}, bf16[2,32,4096]{2,1,0:T(8,128)(2,1)S(1)}, u32[]{:S(2)}) copy-start(bf16[2,32,4096]{2,1,0:T(8,128)(2,1)S(1)} %collective-permute-done.5.refs_5_) | copy-start | bytes 1572868
  47.5 3.5 %collective-permute-start.8 = (bf16[2,32,4096]{2,1,0:T(8,128)(2,1)S(1)}, bf16[2,32,4096]{2,1,0:T(8,128)(2,1)S(1)}, u32[]{:S(2)}, u32[]{:S(2)}) collective-permute-start(bf16[2,32,4096]{2,1,0:T(8,128)(2,1)S(1)} %project.2.refs_2_), channel_id=1, source_target_pairs={{0,1},{1,0},{2,3},{3,2},{4,5},{5,4},{6,7},{7,6},{8,9},{9,8},{10,11... | collective-permute-start | bytes 1572872 | tf_op jit(solution)/shard_map/ppermute | solution.py:398
  55.2 45.5 %copy-start.9 = (bf16[1,2,32,4096]{3,2,1,0:T(8,128)(2,1)S(1)}, bf16[1,2,32,4096]{3,2,1,0:T(8,128)(2,1)}, u32[]{:S(2)}) copy-start(bf16[1,2,32,4096]{3,2,1,0:T(8,128)(2,1)} %param.6) | copy-start | bytes 1572868
  55.2 63.2 %copy-start.5 = (bf16[1,4,32,4096]{3,2,1,0:T(8,128)(2,1)S(1)}, bf16[1,4,32,4096]{3,2,1,0:T(8,128)(2,1)}, u32[]{:S(2)}) copy-start(bf16[1,4,32,4096]{3,2,1,0:T(8,128)(2,1)} %param.5) | copy-start | bytes 3145732
  75.4 4.0 %copy-start = (bf16[5,4,32,64,128]{4,3,2,1,0:T(8,128)(2,1)}, bf16[5,4,32,64,128]{4,3,2,1,0:T(8,128)(2,1)S(1)}, u32[]{:S(2)}) copy-start(bf16[5,4,32,64,128]{4,3,2,1,0:T(8,128)(2,1)S(1)} %get-tuple-element.44.u) | copy-start | bytes 31457284
  79.4 2.0 %copy-start.2 = (f32[4,32,64,128]{3,2,1,0:T(8,128)}, f32[4,32,64,128]{3,2,1,0:T(8,128)S(1)}, u32[]{:S(2)}) copy-start(f32[4,32,64,128]{3,2,1,0:T(8,128)S(1)} %get-tuple-element.45.last) | copy-start | bytes 12582916
  82.4 18.3 %collective-permute-start.12 = (bf16[2,32,4096]{2,1,0:T(8,128)(2,1)}, bf16[2,32,4096]{2,1,0:T(8,128)(2,1)}, u32[]{:S(2)}, u32[]{:S(2)}) collective-permute-start(bf16[2,32,4096]{2,1,0:T(8,128)(2,1)} %get-tuple-element.47), channel_id=1, source_target_pairs={{1,2},{3,4},{5,6},{7,8},{9,10},{11,12},{13,14},{15,16},{17,18},{19... | collective-permute-start | bytes 1572872 | tf_op jit(solution)/shard_map/ppermute | solution.py:398
  83.7 4.0 %collective-permute-start.9 = (f32[8,128]{1,0:T(8,128)S(1)}, f32[8,128]{1,0:T(8,128)S(1)}, u32[]{:S(2)}, u32[]{:S(2)}) collective-permute-start(f32[8,128]{1,0:T(8,128)S(1)} %get-tuple-element.43.own), channel_id=1, source_target_pairs={{0,1},{1,0},{2,3},{3,2},{4,5},{5,4},{6,7},{7,6},{8,9},{9,8},{10,11... | collective-permute-start | bytes 12296 | tf_op jit(solution)/shard_map/ppermute | solution.py:398
  87.7 4.0 %copy-start.1 = (bf16[5,4,32,64,128]{4,3,2,1,0:T(8,128)(2,1)S(1)}, bf16[5,4,32,64,128]{4,3,2,1,0:T(8,128)(2,1)}, u32[]{:S(2)}) copy-start(bf16[5,4,32,64,128]{4,3,2,1,0:T(8,128)(2,1)} %copy-done) | copy-start | bytes 31457284
  91.7 2.2 %copy-start.3 = (f32[4,32,64,128]{3,2,1,0:T(8,128)S(1)}, f32[4,32,64,128]{3,2,1,0:T(8,128)}, u32[]{:S(2)}) copy-start(f32[4,32,64,128]{3,2,1,0:T(8,128)} %copy-done.2) | copy-start | bytes 12582916
  93.9 24.6 %copy-start.7 = (bf16[4,32,4096]{2,1,0:T(8,128)(2,1)S(1)}, bf16[4,32,4096]{2,1,0:T(8,128)(2,1)}, u32[]{:S(2)}) copy-start(bf16[4,32,4096]{2,1,0:T(8,128)(2,1)} %copy-done.6) | copy-start | bytes 3145732
  97.5 19.5 %collective-permute-start.10 = (bf16[2,32,4096]{2,1,0:T(8,128)(2,1)S(1)}, bf16[2,32,4096]{2,1,0:T(8,128)(2,1)S(1)}, u32[]{:S(2)}, u32[]{:S(2)}) collective-permute-start(bf16[2,32,4096]{2,1,0:T(8,128)(2,1)S(1)} %project.3), channel_id=1, source_target_pairs={{0,2},{2,4},{4,6},{6,8},{8,10},{10,12},{12,14},{14,16},{16,18},{18... | collective-permute-start | bytes 1572872 | tf_op jit(solution)/shard_map/ppermute | solution.py:398
  99.4 19.0 %collective-permute-start.11 = (bf16[2,32,4096]{2,1,0:T(8,128)(2,1)S(1)}, bf16[2,32,4096]{2,1,0:T(8,128)(2,1)S(1)}, u32[]{:S(2)}, u32[]{:S(2)}) collective-permute-start(bf16[2,32,4096]{2,1,0:T(8,128)(2,1)S(1)} %project.3), channel_id=1, source_target_pairs={{1,2},{3,4},{5,6},{7,8},{9,10},{11,12},{13,14},{15,16},{17,18},{19... | collective-permute-start | bytes 1572872 | tf_op jit(solution)/shard_map/ppermute | solution.py:398
  (10 other events, 9.8 us)

commit v5 on v4

--- a/solution.py
+++ b/solution.py
@@ -57,27 +57,25 @@
 
 def krylov_kernel(second, core_of, *refs):
     if second:
-        coup, kept, own, got, b_even, b_odd, r_even, r_odd, left_raw = refs[:9]
-        outs = refs[9:15]
-        scratch = refs[15:]
+        coup, kept, a_raw, b_even, b_odd, r_even, r_odd, left_raw = refs[:8]
+        outs = refs[8:11]
+        scratch = refs[11:]
     else:
         coup, kept, own, got, own_l, got_l, own_r, got_r = refs[:8]
         outs = refs[8:14]
         scratch = refs[14:]
-    u, last, small, at, a_flat = outs[:5]
-    a_raw, ab, lb, rb, bcat, w, sems, moments, b_raw, r_raw, eb = scratch
+    u, last, small = outs[:3]
+    ab, lb, rb, bcat, w, sems, moments, b_raw, r_raw = scratch[:9]
     y = last
     core = core_of()
 
     if not second:
-        left_raw = outs[5]
+        at, a_flat, left_raw = outs[3:]
+        a_raw = scratch[9]
 
     def moves(odd):
         if second:
-            mine = HALF if odd else 0
             pairs = [
-                (own, a_raw.at[pl.ds(mine, HALF)]),
-                (got, a_raw.at[pl.ds(HALF - mine, HALF)]),
                 (b_odd if odd else b_even, b_raw),
                 (r_odd if odd else r_even, r_raw),
             ]
@@ -120,18 +118,16 @@
     for h in range(HALF):
         bcat[:, :, h * BS : (h + 1) * BS] = b_raw[h].reshape(NB, BS, BS)
 
-    if second:
-        factor = norm_factor(sum_squares(a_raw, PHYS))
     for s in range(PHYS):
         x = a_raw[s]
-        if second:
-            x = scaled_copy(x, factor)
-        a_flat[s] = x
+        if not second:
+            a_flat[s] = x
         ab[s] = x.reshape(NB, BS, BS)
 
     for q in range(NB):
-        for s1 in range(PHYS):
-            at[q, :, s1 * BS : (s1 + 1) * BS] = ab[s1, minus(q, s1)].T
+        if not second:
+            for s1 in range(PHYS):
+                at[q, :, s1 * BS : (s1 + 1) * BS] = ab[s1, minus(q, s1)].T
         lhs = jnp.concatenate([ab[s1, minus(q, s1)] for s1 in range(PHYS)], 0)
         out = dot(lhs, bcat[q]).astype(BF16)
         for s1 in range(PHYS):
@@ -175,8 +171,6 @@
     for q in range(NB):
         out = jnp.where((row == 1) & (column == q), kept[0, q].astype(F32), out)
     small[...] = out
-    if second:
-        env_part(left_raw, at, outs[5], ab, lb, u.at[ITERS], eb)
 
 
 def project_kernel(owner, core_of, own, got, u, last, at, x_out, v, xb):
@@ -264,6 +258,21 @@
     return lax.rsqrt(jnp.sum(total, keepdims=True) / (PHYS * NB * FLAT) + EPSILON)
 
 
+def prepare_kernel(core_of, own, got, left, new, at, env, ab, lb, hb, eb):
+    core = core_of()
+    factor = norm_factor(sum_squares(own, HALF) + sum_squares(got, HALF))
+    for h in range(HALF):
+        new[core * HALF + h] = scaled_copy(own[h], factor)
+        new[(1 - core) * HALF + h] = scaled_copy(got[h], factor)
+    for s in range(PHYS):
+        ab[s] = new[s].reshape(NB, BS, BS)
+    for q in range(NB):
+        for s1 in range(PHYS):
+            at[q, :, s1 * BS : (s1 + 1) * BS] = ab[s1, minus(q, s1)].T
+    lb[:, :, BS:] = left[1].reshape(NB, BS, BS)
+    env_part(left, at, env, ab, lb, hb, eb)
+
+
 def choose_kernel(tensor, new, low, high, out):
     odd = lax.rem(lax.axis_index("site"), 2) == 1
     first = jnp.logical_and(lax.axis_index("site") == 0, lax.axis_index("sec") == 0)
@@ -297,12 +306,10 @@
         shape(ITERS + 1, PHYS, NB, BS, LN),
         shape(PHYS, NB, BS, LN, dtype=F32),
         shape(8, 128, dtype=F32),
-        shape(NB, BS, PHYS * BS),
-        shape(PHYS, NB, FLAT),
-        shape(2, NB, FLAT),
     ]
+    if not second:
+        outs += [shape(NB, BS, PHYS * BS), shape(PHYS, NB, FLAT), shape(2, NB, FLAT)]
     scratch = [
-        pltpu.VMEM((PHYS, NB, FLAT), BF16),
         pltpu.VMEM((PHYS, NB, BS, BS), BF16),
         pltpu.VMEM((NB, BS, 2 * BS), BF16),
         pltpu.VMEM((NB, BS, BS), BF16),
@@ -312,19 +319,19 @@
         pltpu.VMEM((2 * ITERS, 8, LN), F32),
         pltpu.VMEM((HALF, NB, FLAT), BF16),
         pltpu.VMEM((2, NB, FLAT), BF16),
-        pltpu.VMEM((2, NB, BS, BS), BF16),
     ]
     if second:
-        specs = [SM, SM] + [HB] * 6 + [VM]
+        specs = [SM, SM, VM] + [HB] * 4 + [VM]
     else:
         specs = [SM, SM] + [HB] * 6
+        scratch.append(pltpu.VMEM((PHYS, NB, FLAT), BF16))
     return pl.pallas_call(
         functools.partial(krylov_kernel, second, core_of),
         out_shape=tuple(outs),
         in_specs=specs,
         out_specs=(VM,) * len(outs),
         scratch_shapes=scratch,
-        compiler_params=params(30),
+        compiler_params=params(28),
         cost_estimate=pl.CostEstimate(flops=10**11, bytes_accessed=2**24, transcendentals=0),
         name="krylov",
     )(coupling, kept, *arrays)
@@ -364,6 +371,28 @@
     )(a_flat, left, at)
 
 
+def prepare(core_of, own, got, left):
+    return pl.pallas_call(
+        functools.partial(prepare_kernel, core_of),
+        out_shape=(
+            shape(PHYS, NB, FLAT),
+            shape(NB, BS, PHYS * BS),
+            shape(2, NB, FLAT),
+        ),
+        in_specs=[VM] * 3,
+        out_specs=(VM,) * 3,
+        scratch_shapes=[
+            pltpu.VMEM((PHYS, NB, BS, BS), BF16),
+            pltpu.VMEM((NB, BS, 2 * BS), BF16),
+            pltpu.VMEM((PHYS, NB, BS, 2 * BS), BF16),
+            pltpu.VMEM((2, NB, BS, BS), BF16),
+        ],
+        compiler_params=params(12),
+        cost_estimate=pl.CostEstimate(flops=10**6, bytes_accessed=2**10, transcendentals=0),
+        name="prepare",
+    )(own, got, left)
+
+
 def choose(tensor, new, low, high):
     return pl.pallas_call(
         choose_kernel,
@@ -417,14 +446,16 @@
     x, b_even, b_odd, r_even, r_odd = lax.optimization_barrier((x, b_even, b_odd, r_even, r_odd))
     got_x = send(x, swap)
 
-    u, last, small, at, new1, env2 = krylov(
-        core_index, True, coupling, kept_rows, x, got_x, b_even, b_odd, r_even, r_odd, env1
+    new1, at, env2 = prepare(core_index, x, got_x, env1)
+    got_env = send(env2, from_odd)
+    u, last, small = krylov(
+        core_index, True, coupling, kept_rows, new1, b_even, b_odd, r_even, r_odd, env1
     )
     got_small = send(small, swap)
     x = project(core_index, 1, small, got_small, u, last, at)
     low = send(x, from_even)
     high = send(x, from_odd)
-    got_env = send(env2, from_odd)
+    got_env, low, high = lax.optimization_barrier((got_env, low, high))
 
     odd = position % 2 == 1
     first = position == 0

time: 121 us -> 104 us (0.86)
  local copies, waits for them, and re-layouts: 23.3 us -> 5.93 us
  Pallas kernels: 49.5 us -> 51.1 us
    unnamed x42 -> x12, local copies, waits for them, and re-layouts: 22 us -> 4.64 us
    pallas_call x0 -> x1, Pallas kernels: none -> 5.88 us  [prepare(): pl.pallas_call(functools.partial(prepare_kernel, core_of), out_shape=(sha...]
    pallas_call x2, Pallas kernels: 37.5 us -> 32.2 us  [krylov(): pl.pallas_call(functools.partial(krylov_kernel, second, core_of), out_sha...]
  transfers between devices with their start and end apart: 13 -> 13, of which waited for: 5 -> 5; matrix products, arithmetic and copies ran while one was open for 3% -> 1% of each run, Pallas kernels for 23% -> 26%
where the time goes in v5:
time: 104 us; the launch traced here: 103 us
  Pallas kernels  51.1 us (49%)
  starting transfers between devices  25.2 us (24%)
  waiting for transfers between devices  18 us (17%)
  local copies, waits for them, and re-layouts  5.93 us (6%)
  other arithmetic  2.06 us (2%)
    pallas_call x2, Pallas kernels, krylov(): pl.pallas_call(functools.partial(krylov_kernel, second, core_of), out_sha...  32.2 us
    ppermute x13, starting transfers between devices, send(): return lax.ppermute(x, axes, pairs)  25.2 us
    ppermute x13, waiting for transfers between devices, send(): return lax.ppermute(x, axes, pairs)  18 us
    pallas_call x2, Pallas kernels, project(): pl.pallas_call(functools.partial(project_kernel, owner, core_of), out_sha...  7.27 us
    pallas_call x1, Pallas kernels, prepare(): pl.pallas_call(functools.partial(prepare_kernel, core_of), out_shape=(sha...  5.88 us
    unnamed x12, local copies, waits for them, and re-layouts  4.64 us
    pallas_call x1, Pallas kernels, grow(): pl.pallas_call(env_kernel, out_shape=shape(2, NB, FLAT), in_specs=[VM] *...  3.03 us
    pallas_call x1, Pallas kernels, choose(): pl.pallas_call(choose_kernel, out_shape=shape(PHYS, NB, FLAT), in_specs=[...  2.75 us
  transfers between devices with their start and end apart: 13, of which 5 were waited for; matrix products, arithmetic and copies ran while one was open for 1% of the time, Pallas kernels for 26%

profile of v5, /device:TPU:6, one launch (start us, length us, event | category | flops | bytes accessed | tf_op | source)
XLA Modules:
  0.0 103.2 jit_solution(8187441857328583765)
XLA Ops:
  0.7 1.3 %collective-permute-start.2 = (bf16[2,32,4096]{2,1,0:T(8,128)(2,1)}, bf16[2,32,4096]{2,1,0:T(8,128)(2,1)S(1)}, u32[]{:S(2)}, u32[]{:S(2)}) collective-permute-start(bf16[2,32,4096]{2,1,0:T(8,128)(2,1)} %bitcast.16), channel_id=1, source_target_pairs={{1,0},{3,2},{5,4},{7,6},{9,8},{11,10},{13,12},{15,14},{17,16},{19,... | collective-permute-start | bytes 1572872 | tf_op jit(solution)/shard_map/ppermute | solution.py:427
  2.0 3.1 %collective-permute-start.1 = (bf16[2,32,4096]{2,1,0:T(8,128)(2,1)}, bf16[2,32,4096]{2,1,0:T(8,128)(2,1)S(1)}, u32[]{:S(2)}, u32[]{:S(2)}) collective-permute-start(bf16[2,32,4096]{2,1,0:T(8,128)(2,1)} %bitcast.14), channel_id=1, source_target_pairs={{0,1},{2,3},{4,5},{6,7},{8,9},{10,11},{12,13},{14,15},{16,17},{18,... | collective-permute-start | bytes 1572872 | tf_op jit(solution)/shard_map/ppermute | solution.py:427
  5.1 1.3 %slice_bitcast_fusion = (bf16[2,32,4096]{2,1,0:T(8,128)(2,1)S(1)}, bf16[2,32,4096]{2,1,0:T(8,128)(2,1)S(1)}) fusion(bf16[1,4,32,4096]{3,2,1,0:T(8,128)(2,1)} %param.5), kind=kLoop, calls=%fused_computation.1 | loop fusion | bytes 2097152 | tf_op jit(solution)/shard_map/slice | solution.py:433
  6.8 8.7 %collective-permute-start.6 = (bf16[2,32,4096]{2,1,0:T(8,128)(2,1)}, bf16[2,32,4096]{2,1,0:T(8,128)(2,1)S(1)}, u32[]{:S(2)}, u32[]{:S(2)}) collective-permute-start(bf16[2,32,4096]{2,1,0:T(8,128)(2,1)} %bitcast.17), channel_id=1, source_target_pairs={{2,0},{4,2},{6,4},{8,6},{10,8},{12,10},{14,12},{16,14},{18,16},{20... | collective-permute-start | bytes 1572872 | tf_op jit(solution)/shard_map/ppermute | solution.py:427
  15.5 1.3 %collective-permute-start.7 = (bf16[2,32,4096]{2,1,0:T(8,128)(2,1)}, bf16[2,32,4096]{2,1,0:T(8,128)(2,1)S(1)}, u32[]{:S(2)}, u32[]{:S(2)}) collective-permute-start(bf16[2,32,4096]{2,1,0:T(8,128)(2,1)} %bitcast.18), channel_id=1, source_target_pairs={{2,1},{4,3},{6,5},{8,7},{10,9},{12,11},{14,13},{16,15},{18,17},{20... | collective-permute-start | bytes 1572872 | tf_op jit(solution)/shard_map/ppermute | solution.py:427
  16.8 2.3 %collective-permute-start.4 = (bf16[2,32,4096]{2,1,0:T(8,128)(2,1)S(1)}, bf16[2,32,4096]{2,1,0:T(8,128)(2,1)S(1)}, u32[]{:S(2)}, u32[]{:S(2)}) collective-permute-start(bf16[2,32,4096]{2,1,0:T(8,128)(2,1)S(1)} %get-tuple-element.35), channel_id=1, source_target_pairs={{2,0},{4,2},{6,4},{8,6},{10,8},{12,10},{14,12},{16,14},{18,16},{20... | collective-permute-start | bytes 1572872 | tf_op jit(solution)/shard_map/ppermute | solution.py:427
  19.1 1.3 %collective-permute-start.5 = (bf16[2,32,4096]{2,1,0:T(8,128)(2,1)S(1)}, bf16[2,32,4096]{2,1,0:T(8,128)(2,1)S(1)}, u32[]{:S(2)}, u32[]{:S(2)}) collective-permute-start(bf16[2,32,4096]{2,1,0:T(8,128)(2,1)S(1)} %get-tuple-element.36), channel_id=1, source_target_pairs={{2,1},{4,3},{6,5},{8,7},{10,9},{12,11},{14,13},{16,15},{18,17},{20... | collective-permute-start | bytes 1572872 | tf_op jit(solution)/shard_map/ppermute | solution.py:427
  20.5 1.2 %copy-done = bf16[1,4,32,4096]{3,2,1,0:T(8,128)(2,1)S(1)} copy-done((bf16[1,4,32,4096]{3,2,1,0:T(8,128)(2,1)S(1)}, bf16[1,4,32,4096]{3,2,1,0:T(8,128)(2,1)}, u32[]{:S(2)}) %copy-start) | copy-done | bytes 1048600
  21.7 1.0 %copy-done.2 = bf16[1,2,32,4096]{3,2,1,0:T(8,128)(2,1)S(1)} copy-done((bf16[1,2,32,4096]{3,2,1,0:T(8,128)(2,1)S(1)}, bf16[1,2,32,4096]{3,2,1,0:T(8,128)(2,1)}, u32[]{:S(2)}) %copy-start.2) | copy-done | bytes 524312
  25.1 16.4 %krylov.2 = (bf16[5,4,32,64,128]{4,3,2,1,0:T(8,128)(2,1)S(1)}, f32[4,32,64,128]{3,2,1,0:T(8,128)S(1)}, f32[8,128]{1,0:T(8,128)S(1)}, bf16[32,64,256]{2,1,0:T(8,1...) custom-call(f32[4,4]{1,0:T(4,128)S(1)} %copy-done.4, s32[1,32]{1,0:T(1,128)S(1)} %copy-done.5, ...), custom_call_target="tpu_custom_call" | custom-call | flops 99999997952 | bytes 16777216 | tf_op jit(solution)/shard_map/krylov/pallas_call | solution.py:328
  41.6 1.2 %collective-permute-done.3.got = f32[8,128]{1,0:T(8,128)S(1)} collective-permute-done((f32[8,128]{1,0:T(8,128)S(1)}, f32[8,128]{1,0:T(8,128)S(1)}, u32[]{:S(2)}, u32[]{:S(2)}) %collective-permute-start.3) | collective-permute-done | bytes 4128 | tf_op jit(solution)/shard_map/ppermute | solution.py:427
  42.8 3.6 %project.2.own = bf16[2,32,4096]{2,1,0:T(8,128)(2,1)S(1)} custom-call(f32[8,128]{1,0:T(8,128)S(1)} %get-tuple-element.31.own, f32[8,128]{1,0:T(8,128)S(1)} %collective-permute-done.3.got, bf16[5,4,32,64,128]{4,3,2,1,0:T(8,128)(2,1)S(1)} %get-tuple-element.32.u, f32[4,32,64,128]{3,2,1,0:T(8,128)S(1)} %get-tuple-element.33.last, ...), custom_call_target="tpu_custom_call" | custom-call | flops 1000000 | bytes 1024 | tf_op jit(solution)/shard_map/project/pallas_call | solution.py:341
  46.9 3.0 %grow.1.left.refs_7_ = bf16[2,32,4096]{2,1,0:T(8,128)(2,1)S(1)} custom-call(bf16[4,32,4096]{2,1,0:T(8,128)(2,1)S(1)} %get-tuple-element.39.a_flat, bf16[2,32,4096]{2,1,0:T(8,128)(2,1)S(1)} %get-tuple-element.40.left, bf16[32,64,256]{2,1,0:T(8,128)(2,1)S(1)} %get-tuple-element.34.at), custom_call_target="tpu_custom_call" | custom-call | flops 1000000 | bytes 1024 | tf_op jit(solution)/shard_map/grow/pallas_call | solution.py:357
  49.9 5.9 %prepare.1 = (bf16[4,32,4096]{2,1,0:T(8,128)(2,1)S(1)}, bf16[32,64,256]{2,1,0:T(8,128)(2,1)S(1)}, bf16[2,32,4096]{2,1,0:T(8,128)(2,1)}) custom-call(bf16[2,32,4096]{2,1,0:T(8,128)(2,1)S(1)} %project.2.own, bf16[2,32,4096]{2,1,0:T(8,128)(2,1)S(1)} %collective-permute-done.8.got, bf16[2,32,4096]{2,1,0:T(8,128)(2,1)S(1)} %grow.1.left.refs_7_), custom_call_target="tpu_custom_call" | custom-call | flops 1000000 | bytes 1024 | tf_op jit(solution)/shard_map/prepare/pallas_call | solution.py:375
  55.8 15.8 %krylov.3 = (bf16[5,4,32,64,128]{4,3,2,1,0:T(8,128)(2,1)S(1)}, f32[4,32,64,128]{3,2,1,0:T(8,128)S(1)}, f32[8,128]{1,0:T(8,128)S(1)}) custom-call(f32[4,4]{1,0:T(4,128)S(1)} %copy-done.4, s32[1,32]{1,0:T(1,128)S(1)} %copy-done.5, bf16[4,32,4096]{2,1,0:T(8,128)(2,1)S(1)} %get-tuple-element.41.refs_2_.new, ...), custom_call_target="tpu_custom_call" | custom-call | flops 99999997952 | bytes 16777216 | tf_op jit(solution)/shard_map/krylov/pallas_call | solution.py:328
  72.1 1.3 %collective-permute-start.9 = (bf16[2,32,4096]{2,1,0:T(8,128)(2,1)}, bf16[2,32,4096]{2,1,0:T(8,128)(2,1)}, u32[]{:S(2)}, u32[]{:S(2)}) collective-permute-start(bf16[2,32,4096]{2,1,0:T(8,128)(2,1)} %get-tuple-element.42), channel_id=1, source_target_pairs={{1,2},{3,4},{5,6},{7,8},{9,10},{11,12},{13,14},{15,16},{17,18},{19... | collective-permute-start | bytes 1572872 | tf_op jit(solution)/shard_map/ppermute | solution.py:427
  73.4 3.6 %project.3 = bf16[2,32,4096]{2,1,0:T(8,128)(2,1)S(1)} custom-call(f32[8,128]{1,0:T(8,128)S(1)} %get-tuple-element.47.own, f32[8,128]{1,0:T(8,128)S(1)} %collective-permute-done.10.got, bf16[5,4,32,64,128]{4,3,2,1,0:T(8,128)(2,1)S(1)} %get-tuple-element.48.u, f32[4,32,64,128]{3,2,1,0:T(8,128)S(1)} %get-tuple-element.49.last, ...), custom_call_target="tpu_custom_call" | custom-call | flops 1000000 | bytes 1024 | tf_op jit(solution)/shard_map/project/pallas_call | solution.py:341
  77.0 3.5 %collective-permute-start.11 = (bf16[2,32,4096]{2,1,0:T(8,128)(2,1)S(1)}, bf16[2,32,4096]{2,1,0:T(8,128)(2,1)}, u32[]{:S(2)}, u32[]{:S(2)}) collective-permute-start(bf16[2,32,4096]{2,1,0:T(8,128)(2,1)S(1)} %project.3), channel_id=1, source_target_pairs={{0,2},{2,4},{4,6},{6,8},{8,10},{10,12},{12,14},{14,16},{16,18},{18... | collective-permute-start | bytes 1572872 | tf_op jit(solution)/shard_map/ppermute | solution.py:427
  80.6 1.3 %collective-permute-start.12 = (bf16[2,32,4096]{2,1,0:T(8,128)(2,1)S(1)}, bf16[2,32,4096]{2,1,0:T(8,128)(2,1)}, u32[]{:S(2)}, u32[]{:S(2)}) collective-permute-start(bf16[2,32,4096]{2,1,0:T(8,128)(2,1)S(1)} %project.3), channel_id=1, source_target_pairs={{1,2},{3,4},{5,6},{7,8},{9,10},{11,12},{13,14},{15,16},{17,18},{19... | collective-permute-start | bytes 1572872 | tf_op jit(solution)/shard_map/ppermute | solution.py:427
  81.9 5.5 %collective-permute-done.9 = bf16[2,32,4096]{2,1,0:T(8,128)(2,1)} collective-permute-done((bf16[2,32,4096]{2,1,0:T(8,128)(2,1)}, bf16[2,32,4096]{2,1,0:T(8,128)(2,1)}, u32[]{:S(2)}, u32[]{:S(2)}) %collective-permute-start.9) | collective-permute-done | bytes 524320 | tf_op jit(solution)/shard_map/ppermute | solution.py:427
  87.4 8.3 %collective-permute-done.11.low = bf16[2,32,4096]{2,1,0:T(8,128)(2,1)} collective-permute-done((bf16[2,32,4096]{2,1,0:T(8,128)(2,1)S(1)}, bf16[2,32,4096]{2,1,0:T(8,128)(2,1)}, u32[]{:S(2)}, u32[]{:S(2)}) %collective-permute-start.11) | collective-permute-done | bytes 524320 | tf_op jit(solution)/shard_map/ppermute | solution.py:427
  95.6 2.7 %collective-permute-done.12.high = bf16[2,32,4096]{2,1,0:T(8,128)(2,1)} collective-permute-done((bf16[2,32,4096]{2,1,0:T(8,128)(2,1)S(1)}, bf16[2,32,4096]{2,1,0:T(8,128)(2,1)}, u32[]{:S(2)}, u32[]{:S(2)}) %collective-permute-start.12) | collective-permute-done | bytes 524320 | tf_op jit(solution)/shard_map/ppermute | solution.py:427
  98.4 2.8 %choose.1 = bf16[4,32,4096]{2,1,0:T(8,128)(2,1)} custom-call(bf16[4,32,4096]{2,1,0:T(8,128)(2,1)S(1)} %bitcast.13, bf16[4,32,4096]{2,1,0:T(8,128)(2,1)S(1)} %get-tuple-element.41.refs_2_.new, bf16[2,32,4096]{2,1,0:T(8,128)(2,1)} %collective-permute-done.11.low, bf16[2,32,4096]{2,1,0:T(8,128)(2,1)} %collective-permute-done.12.high), custom_call_target="tpu_custom_call" | custom-call | tf_op jit(solution)/shard_map/choose/pallas_call | solution.py:397
  101.1 2.1 %select_bitcast_fusion = bf16[1,2,32,4096]{3,2,1,0:T(8,128)(2,1)} fusion(bf16[2,32,4096]{2,1,0:T(8,128)(2,1)S(1)} %grow.1.left.refs_7_, bf16[2,32,4096]{2,1,0:T(8,128)(2,1)} %collective-permute-done.9, pred[]{:T(512)S(6)} %eq.9, pred[]{:T(512)S(6)} %eq.8, bf16[1,2,32,4096]{3,2,1,0:T(8,128)(2,1)} %param.6), kind=kLoop, calls=%fused_computation | loop fusion | flops 524288 | bytes 2097154 | tf_op jit(solution)/shard_map/broadcast_in_dim | solution.py:464
  (23 shorter events, 3.9 us)
Async XLA Ops:
  0.6 6.2 %collective-permute-start = (bf16[4,32,4096]{2,1,0:T(8,128)(2,1)}, bf16[4,32,4096]{2,1,0:T(8,128)(2,1)S(1)}, u32[]{:S(2)}, u32[]{:S(2)}) collective-permute-start(bf16[4,32,4096]{2,1,0:T(8,128)(2,1)} %bitcast.11), channel_id=1, source_target_pairs={{0,1},{1,0},{2,3},{3,2},{4,5},{5,4},{6,7},{7,6},{8,9},{9,8},{10,11... | collective-permute-start | bytes 3145736 | tf_op jit(solution)/shard_map/ppermute | solution.py:427
  0.7 5.7 %collective-permute-start.2 = (bf16[2,32,4096]{2,1,0:T(8,128)(2,1)}, bf16[2,32,4096]{2,1,0:T(8,128)(2,1)S(1)}, u32[]{:S(2)}, u32[]{:S(2)}) collective-permute-start(bf16[2,32,4096]{2,1,0:T(8,128)(2,1)} %bitcast.16), channel_id=1, source_target_pairs={{1,0},{3,2},{5,4},{7,6},{9,8},{11,10},{13,12},{15,14},{17,16},{19,... | collective-permute-start | bytes 1572872 | tf_op jit(solution)/shard_map/ppermute | solution.py:427
  2.0 4.8 %collective-permute-start.1 = (bf16[2,32,4096]{2,1,0:T(8,128)(2,1)}, bf16[2,32,4096]{2,1,0:T(8,128)(2,1)S(1)}, u32[]{:S(2)}, u32[]{:S(2)}) collective-permute-start(bf16[2,32,4096]{2,1,0:T(8,128)(2,1)} %bitcast.14), channel_id=1, source_target_pairs={{0,1},{2,3},{4,5},{6,7},{8,9},{10,11},{12,13},{14,15},{16,17},{18,... | collective-permute-start | bytes 1572872 | tf_op jit(solution)/shard_map/ppermute | solution.py:427
  6.8 39.6 %collective-permute-start.6 = (bf16[2,32,4096]{2,1,0:T(8,128)(2,1)}, bf16[2,32,4096]{2,1,0:T(8,128)(2,1)S(1)}, u32[]{:S(2)}, u32[]{:S(2)}) collective-permute-start(bf16[2,32,4096]{2,1,0:T(8,128)(2,1)} %bitcast.17), channel_id=1, source_target_pairs={{2,0},{4,2},{6,4},{8,6},{10,8},{12,10},{14,12},{16,14},{18,16},{20... | collective-permute-start | bytes 1572872 | tf_op jit(solution)/shard_map/ppermute | solution.py:427
  15.5 30.9 %collective-permute-start.7 = (bf16[2,32,4096]{2,1,0:T(8,128)(2,1)}, bf16[2,32,4096]{2,1,0:T(8,128)(2,1)S(1)}, u32[]{:S(2)}, u32[]{:S(2)}) collective-permute-start(bf16[2,32,4096]{2,1,0:T(8,128)(2,1)} %bitcast.18), channel_id=1, source_target_pairs={{2,1},{4,3},{6,5},{8,7},{10,9},{12,11},{14,13},{16,15},{18,17},{20... | collective-permute-start | bytes 1572872 | tf_op jit(solution)/shard_map/ppermute | solution.py:427
  16.8 29.6 %collective-permute-start.4 = (bf16[2,32,4096]{2,1,0:T(8,128)(2,1)S(1)}, bf16[2,32,4096]{2,1,0:T(8,128)(2,1)S(1)}, u32[]{:S(2)}, u32[]{:S(2)}) collective-permute-start(bf16[2,32,4096]{2,1,0:T(8,128)(2,1)S(1)} %get-tuple-element.35), channel_id=1, source_target_pairs={{2,0},{4,2},{6,4},{8,6},{10,8},{12,10},{14,12},{16,14},{18,16},{20... | collective-permute-start | bytes 1572872 | tf_op jit(solution)/shard_map/ppermute | solution.py:427
  19.1 27.3 %collective-permute-start.5 = (bf16[2,32,4096]{2,1,0:T(8,128)(2,1)S(1)}, bf16[2,32,4096]{2,1,0:T(8,128)(2,1)S(1)}, u32[]{:S(2)}, u32[]{:S(2)}) collective-permute-start(bf16[2,32,4096]{2,1,0:T(8,128)(2,1)S(1)} %get-tuple-element.36), channel_id=1, source_target_pairs={{2,1},{4,3},{6,5},{8,7},{10,9},{12,11},{14,13},{16,15},{18,17},{20... | collective-permute-start | bytes 1572872 | tf_op jit(solution)/shard_map/ppermute | solution.py:427
  20.5 1.2 %copy-start = (bf16[1,4,32,4096]{3,2,1,0:T(8,128)(2,1)S(1)}, bf16[1,4,32,4096]{3,2,1,0:T(8,128)(2,1)}, u32[]{:S(2)}) copy-start(bf16[1,4,32,4096]{3,2,1,0:T(8,128)(2,1)} %param.5) | copy-start | bytes 3145732
  21.7 1.0 %copy-start.2 = (bf16[1,2,32,4096]{3,2,1,0:T(8,128)(2,1)S(1)}, bf16[1,2,32,4096]{3,2,1,0:T(8,128)(2,1)}, u32[]{:S(2)}) copy-start(bf16[1,2,32,4096]{3,2,1,0:T(8,128)(2,1)} %param.6) | copy-start | bytes 1572868
  22.7 1.0 %copy-start.3 = (bf16[1,2,32,4096]{3,2,1,0:T(8,128)(2,1)S(1)}, bf16[1,2,32,4096]{3,2,1,0:T(8,128)(2,1)}, u32[]{:S(2)}) copy-start(bf16[1,2,32,4096]{3,2,1,0:T(8,128)(2,1)} %param.7) | copy-start | bytes 1572868
  23.8 0.7 copy-start.4
  24.5 0.7 copy-start.5
  41.5 1.2 %collective-permute-start.3 = (f32[8,128]{1,0:T(8,128)S(1)}, f32[8,128]{1,0:T(8,128)S(1)}, u32[]{:S(2)}, u32[]{:S(2)}) collective-permute-start(f32[8,128]{1,0:T(8,128)S(1)} %get-tuple-element.31.own), channel_id=1, source_target_pairs={{0,1},{1,0},{2,3},{3,2},{4,5},{5,4},{6,7},{7,6},{8,9},{9,8},{10,11... | collective-permute-start | bytes 12296 | tf_op jit(solution)/shard_map/ppermute | solution.py:427
  46.5 3.5 %collective-permute-start.8 = (bf16[2,32,4096]{2,1,0:T(8,128)(2,1)S(1)}, bf16[2,32,4096]{2,1,0:T(8,128)(2,1)S(1)}, u32[]{:S(2)}, u32[]{:S(2)}) collective-permute-start(bf16[2,32,4096]{2,1,0:T(8,128)(2,1)S(1)} %project.2.own), channel_id=1, source_target_pairs={{0,1},{1,0},{2,3},{3,2},{4,5},{5,4},{6,7},{7,6},{8,9},{9,8},{10,11... | collective-permute-start | bytes 1572872 | tf_op jit(solution)/shard_map/ppermute | solution.py:427
  71.6 26.7 %copy-start.1 = (bf16[1,4,32,4096]{3,2,1,0:T(8,128)(2,1)S(1)}, bf16[1,4,32,4096]{3,2,1,0:T(8,128)(2,1)}, u32[]{:S(2)}) copy-start(bf16[1,4,32,4096]{3,2,1,0:T(8,128)(2,1)} %param.5) | copy-start | bytes 3145732
  71.6 1.8 %collective-permute-start.10 = (f32[8,128]{1,0:T(8,128)S(1)}, f32[8,128]{1,0:T(8,128)S(1)}, u32[]{:S(2)}, u32[]{:S(2)}) collective-permute-start(f32[8,128]{1,0:T(8,128)S(1)} %get-tuple-element.47.own), channel_id=1, source_target_pairs={{0,1},{1,0},{2,3},{3,2},{4,5},{5,4},{6,7},{7,6},{8,9},{9,8},{10,11... | collective-permute-start | bytes 12296 | tf_op jit(solution)/shard_map/ppermute | solution.py:427
  72.1 15.3 %collective-permute-start.9 = (bf16[2,32,4096]{2,1,0:T(8,128)(2,1)}, bf16[2,32,4096]{2,1,0:T(8,128)(2,1)}, u32[]{:S(2)}, u32[]{:S(2)}) collective-permute-start(bf16[2,32,4096]{2,1,0:T(8,128)(2,1)} %get-tuple-element.42), channel_id=1, source_target_pairs={{1,2},{3,4},{5,6},{7,8},{9,10},{11,12},{13,14},{15,16},{17,18},{19... | collective-permute-start | bytes 1572872 | tf_op jit(solution)/shard_map/ppermute | solution.py:427
  77.0 18.6 %collective-permute-start.11 = (bf16[2,32,4096]{2,1,0:T(8,128)(2,1)S(1)}, bf16[2,32,4096]{2,1,0:T(8,128)(2,1)}, u32[]{:S(2)}, u32[]{:S(2)}) collective-permute-start(bf16[2,32,4096]{2,1,0:T(8,128)(2,1)S(1)} %project.3), channel_id=1, source_target_pairs={{0,2},{2,4},{4,6},{6,8},{8,10},{10,12},{12,14},{14,16},{16,18},{18... | collective-permute-start | bytes 1572872 | tf_op jit(solution)/shard_map/ppermute | solution.py:427
  80.6 17.8 %collective-permute-start.12 = (bf16[2,32,4096]{2,1,0:T(8,128)(2,1)S(1)}, bf16[2,32,4096]{2,1,0:T(8,128)(2,1)}, u32[]{:S(2)}, u32[]{:S(2)}) collective-permute-start(bf16[2,32,4096]{2,1,0:T(8,128)(2,1)S(1)} %project.3), channel_id=1, source_target_pairs={{1,2},{3,4},{5,6},{7,8},{9,10},{11,12},{13,14},{15,16},{17,18},{19... | collective-permute-start | bytes 1572872 | tf_op jit(solution)/shard_map/ppermute | solution.py:427

commit v6 on v5

--- a/solution.py
+++ b/solution.py
@@ -273,17 +273,19 @@
     env_part(left, at, env, ab, lb, hb, eb)
 
 
-def choose_kernel(tensor, new, low, high, out):
+def choose_kernel(tensor, new, low, high, left, env, got_env, out, out_env):
     odd = lax.rem(lax.axis_index("site"), 2) == 1
     first = jnp.logical_and(lax.axis_index("site") == 0, lax.axis_index("sec") == 0)
 
     @pl.when(odd)
     def _():
         out[...] = new[...]
+        out_env[...] = env[...]
 
     @pl.when(first)
     def _():
         out[...] = tensor[...]
+        out_env[...] = left[...]
 
     @pl.when(jnp.logical_not(jnp.logical_or(odd, first)))
     def _():
@@ -291,6 +293,7 @@
         for s in range(HALF):
             out[s] = scaled_copy(low[s], factor)
             out[HALF + s] = scaled_copy(high[s], factor)
+        out_env[...] = got_env[...]
 
 
 def shape(*dims, dtype=BF16):
@@ -393,15 +396,15 @@
     )(own, got, left)
 
 
-def choose(tensor, new, low, high):
+def choose(*arrays):
     return pl.pallas_call(
         choose_kernel,
-        out_shape=shape(PHYS, NB, FLAT),
-        in_specs=[VM] * 4,
-        out_specs=VM,
-        compiler_params=params(8),
+        out_shape=(shape(PHYS, NB, FLAT), shape(2, NB, FLAT)),
+        in_specs=[VM] * 7,
+        out_specs=(VM, VM),
+        compiler_params=params(12),
         name="choose",
-    )(tensor, new, low, high)
+    )(*arrays)
 
 
 def core_index():
@@ -411,7 +414,6 @@
 def shards(tensors, left_env, right_env, kept_rows, coupling):
     across = lax.axis_size("site")
     count = lax.axis_size("sec") * across
-    position = lax.axis_index("sec") * across + lax.axis_index("site")
     axes = ("sec", "site")
     tensor, left, right = tensors[0], left_env[0], right_env[0]
 
@@ -453,14 +455,12 @@
     )
     got_small = send(small, swap)
     x = project(core_index, 1, small, got_small, u, last, at)
+    x, got_env = lax.optimization_barrier((x, got_env))
     low = send(x, from_even)
     high = send(x, from_odd)
     got_env, low, high = lax.optimization_barrier((got_env, low, high))
 
-    odd = position % 2 == 1
-    first = position == 0
-    out_new = choose(tensor, new1, low, high)
-    out_env = jnp.where(odd, env1, jnp.where(first, left, got_env))
+    out_new, out_env = choose(tensor, new1, low, high, left, env1, got_env)
     return out_new[None], out_env[None]
 
 

time: 104 us -> 105 us (level)
  waiting for transfers between devices: 18 us -> 21.1 us
  other arithmetic: 2.06 us -> 0 us
    ppermute x13, waiting for transfers between devices: 18 us -> 21.1 us  [send(): return lax.ppermute(x, axes, pairs)]
    broadcast_in_dim x1 -> x0, other arithmetic: 2.06 us -> none  [shards(): return (out_new[None], out_env[None])]
    pallas_call x2, Pallas kernels: 32.2 us -> 34.1 us  [krylov(): pl.pallas_call(functools.partial(krylov_kernel, second, core_of), out_sha...]
    unnamed x12 -> x14, local copies, waits for them, and re-layouts: 4.64 us -> 4.65 us
  transfers between devices with their start and end apart: 13 -> 13, of which waited for: 5 -> 5; matrix products, arithmetic and copies ran while one was open for 1% -> 1% of each run, Pallas kernels for 26% -> 43%
where the time goes in v6:
time: 105 us; the launch traced here: 104 us
  Pallas kernels  51.5 us (49%)
  starting transfers between devices  24.9 us (24%)
  waiting for transfers between devices  21.1 us (20%)
  local copies, waits for them, and re-layouts  5.92 us (6%)
    pallas_call x2, Pallas kernels, krylov(): pl.pallas_call(functools.partial(krylov_kernel, second, core_of), out_sha...  34.1 us
    ppermute x13, starting transfers between devices, send(): return lax.ppermute(x, axes, pairs)  24.9 us
    ppermute x13, waiting for transfers between devices, send(): return lax.ppermute(x, axes, pairs)  21.1 us
    pallas_call x2, Pallas kernels, project(): pl.pallas_call(functools.partial(project_kernel, owner, core_of), out_sha...  7.43 us
    pallas_call x1, Pallas kernels, prepare(): pl.pallas_call(functools.partial(prepare_kernel, core_of), out_shape=(sha...  5.13 us
    unnamed x14, local copies, waits for them, and re-layouts  4.65 us
    pallas_call x1, Pallas kernels, grow(): pl.pallas_call(env_kernel, out_shape=shape(2, NB, FLAT), in_specs=[VM] *...  3.06 us
  transfers between devices with their start and end apart: 13, of which 5 were waited for; matrix products, arithmetic and copies ran while one was open for 1% of the time, Pallas kernels for 43%

profile of v6, /device:TPU:6, one launch (start us, length us, event | category | flops | bytes accessed | tf_op | source)
XLA Modules:
  0.0 104.3 jit_solution(3224839182971155704)
XLA Ops:
  0.7 2.4 %collective-permute-start.1 = (bf16[2,32,4096]{2,1,0:T(8,128)(2,1)}, bf16[2,32,4096]{2,1,0:T(8,128)(2,1)S(1)}, u32[]{:S(2)}, u32[]{:S(2)}) collective-permute-start(bf16[2,32,4096]{2,1,0:T(8,128)(2,1)} %bitcast.12), channel_id=1, source_target_pairs={{0,1},{2,3},{4,5},{6,7},{8,9},{10,11},{12,13},{14,15},{16,17},{18,... | collective-permute-start | bytes 1572872 | tf_op jit(solution)/shard_map/ppermute | solution.py:429
  3.2 1.3 %collective-permute-start.2 = (bf16[2,32,4096]{2,1,0:T(8,128)(2,1)}, bf16[2,32,4096]{2,1,0:T(8,128)(2,1)S(1)}, u32[]{:S(2)}, u32[]{:S(2)}) collective-permute-start(bf16[2,32,4096]{2,1,0:T(8,128)(2,1)} %bitcast.15), channel_id=1, source_target_pairs={{1,0},{3,2},{5,4},{7,6},{9,8},{11,10},{13,12},{15,14},{17,16},{19,... | collective-permute-start | bytes 1572872 | tf_op jit(solution)/shard_map/ppermute | solution.py:429
  4.5 1.3 %slice_bitcast_fusion = (bf16[2,32,4096]{2,1,0:T(8,128)(2,1)S(1)}, bf16[2,32,4096]{2,1,0:T(8,128)(2,1)S(1)}) fusion(bf16[1,4,32,4096]{3,2,1,0:T(8,128)(2,1)} %param.5), kind=kLoop, calls=%fused_computation | loop fusion | bytes 2097152 | tf_op jit(solution)/shard_map/slice | solution.py:435
  5.7 1.4 %collective-permute-done.2.refs_7_ = bf16[2,32,4096]{2,1,0:T(8,128)(2,1)S(1)} collective-permute-done((bf16[2,32,4096]{2,1,0:T(8,128)(2,1)}, bf16[2,32,4096]{2,1,0:T(8,128)(2,1)S(1)}, u32[]{:S(2)}, u32[]{:S(2)}) %collective-permute-start.2) | collective-permute-done | bytes 524320 | tf_op jit(solution)/shard_map/ppermute | solution.py:429
  7.2 8.7 %collective-permute-start.6 = (bf16[2,32,4096]{2,1,0:T(8,128)(2,1)}, bf16[2,32,4096]{2,1,0:T(8,128)(2,1)S(1)}, u32[]{:S(2)}, u32[]{:S(2)}) collective-permute-start(bf16[2,32,4096]{2,1,0:T(8,128)(2,1)} %bitcast.16), channel_id=1, source_target_pairs={{2,0},{4,2},{6,4},{8,6},{10,8},{12,10},{14,12},{16,14},{18,16},{20... | collective-permute-start | bytes 1572872 | tf_op jit(solution)/shard_map/ppermute | solution.py:429
  15.8 1.3 %collective-permute-start.7 = (bf16[2,32,4096]{2,1,0:T(8,128)(2,1)}, bf16[2,32,4096]{2,1,0:T(8,128)(2,1)S(1)}, u32[]{:S(2)}, u32[]{:S(2)}) collective-permute-start(bf16[2,32,4096]{2,1,0:T(8,128)(2,1)} %bitcast.17), channel_id=1, source_target_pairs={{2,1},{4,3},{6,5},{8,7},{10,9},{12,11},{14,13},{16,15},{18,17},{20... | collective-permute-start | bytes 1572872 | tf_op jit(solution)/shard_map/ppermute | solution.py:429
  17.2 2.3 %collective-permute-start.4 = (bf16[2,32,4096]{2,1,0:T(8,128)(2,1)S(1)}, bf16[2,32,4096]{2,1,0:T(8,128)(2,1)S(1)}, u32[]{:S(2)}, u32[]{:S(2)}) collective-permute-start(bf16[2,32,4096]{2,1,0:T(8,128)(2,1)S(1)} %get-tuple-element.39), channel_id=1, source_target_pairs={{2,0},{4,2},{6,4},{8,6},{10,8},{12,10},{14,12},{16,14},{18,16},{20... | collective-permute-start | bytes 1572872 | tf_op jit(solution)/shard_map/ppermute | solution.py:429
  19.5 1.3 %collective-permute-start.5 = (bf16[2,32,4096]{2,1,0:T(8,128)(2,1)S(1)}, bf16[2,32,4096]{2,1,0:T(8,128)(2,1)S(1)}, u32[]{:S(2)}, u32[]{:S(2)}) collective-permute-start(bf16[2,32,4096]{2,1,0:T(8,128)(2,1)S(1)} %get-tuple-element.40), channel_id=1, source_target_pairs={{2,1},{4,3},{6,5},{8,7},{10,9},{12,11},{14,13},{16,15},{18,17},{20... | collective-permute-start | bytes 1572872 | tf_op jit(solution)/shard_map/ppermute | solution.py:429
  20.8 1.2 %copy-done = bf16[1,4,32,4096]{3,2,1,0:T(8,128)(2,1)S(1)} copy-done((bf16[1,4,32,4096]{3,2,1,0:T(8,128)(2,1)S(1)}, bf16[1,4,32,4096]{3,2,1,0:T(8,128)(2,1)}, u32[]{:S(2)}) %copy-start) | copy-done | bytes 1048600
  22.0 1.0 copy-done.2
  25.5 17.3 %krylov.2 = (bf16[5,4,32,64,128]{4,3,2,1,0:T(8,128)(2,1)S(1)}, f32[4,32,64,128]{3,2,1,0:T(8,128)S(1)}, f32[8,128]{1,0:T(8,128)S(1)}, bf16[32,64,256]{2,1,0:T(8,1...) custom-call(f32[4,4]{1,0:T(4,128)S(1)} %copy-done.5, s32[1,32]{1,0:T(1,128)S(1)} %copy-done.6, ...), custom_call_target="tpu_custom_call" | custom-call | flops 99999997952 | bytes 16777216 | tf_op jit(solution)/shard_map/krylov/pallas_call | solution.py:331
  42.9 1.2 %collective-permute-done.3.got = f32[8,128]{1,0:T(8,128)S(1)} collective-permute-done((f32[8,128]{1,0:T(8,128)S(1)}, f32[8,128]{1,0:T(8,128)S(1)}, u32[]{:S(2)}, u32[]{:S(2)}) %collective-permute-start.3) | collective-permute-done | bytes 4128 | tf_op jit(solution)/shard_map/ppermute | solution.py:429
  44.1 3.7 %project.2.own = bf16[2,32,4096]{2,1,0:T(8,128)(2,1)S(1)} custom-call(f32[8,128]{1,0:T(8,128)S(1)} %get-tuple-element.35.own, f32[8,128]{1,0:T(8,128)S(1)} %collective-permute-done.3.got, bf16[5,4,32,64,128]{4,3,2,1,0:T(8,128)(2,1)S(1)} %get-tuple-element.36.u, f32[4,32,64,128]{3,2,1,0:T(8,128)S(1)} %get-tuple-element.37.last, ...), custom_call_target="tpu_custom_call" | custom-call | flops 1000000 | bytes 1024 | tf_op jit(solution)/shard_map/project/pallas_call | solution.py:344
  48.2 3.1 %grow.1.left.refs_7_.env = bf16[2,32,4096]{2,1,0:T(8,128)(2,1)S(1)} custom-call(bf16[4,32,4096]{2,1,0:T(8,128)(2,1)S(1)} %get-tuple-element.43.a_flat, bf16[2,32,4096]{2,1,0:T(8,128)(2,1)S(1)} %get-tuple-element.44.left, bf16[32,64,256]{2,1,0:T(8,128)(2,1)S(1)} %get-tuple-element.38.at), custom_call_target="tpu_custom_call" | custom-call | flops 1000000 | bytes 1024 | tf_op jit(solution)/shard_map/grow/pallas_call | solution.py:360
  51.3 5.1 %prepare.1 = (bf16[4,32,4096]{2,1,0:T(8,128)(2,1)S(1)}, bf16[32,64,256]{2,1,0:T(8,128)(2,1)S(1)}, bf16[2,32,4096]{2,1,0:T(8,128)(2,1)S(1)}) custom-call(bf16[2,32,4096]{2,1,0:T(8,128)(2,1)S(1)} %project.2.own, bf16[2,32,4096]{2,1,0:T(8,128)(2,1)S(1)} %collective-permute-done.8.got, bf16[2,32,4096]{2,1,0:T(8,128)(2,1)S(1)} %grow.1.left.refs_7_.env), custom_call_target="tpu_custom_call" | custom-call | flops 1000000 | bytes 1024 | tf_op jit(solution)/shard_map/prepare/pallas_call | solution.py:378
  56.5 1.3 %collective-permute-start.10 = (bf16[2,32,4096]{2,1,0:T(8,128)(2,1)S(1)}, bf16[2,32,4096]{2,1,0:T(8,128)(2,1)S(1)}, u32[]{:S(2)}, u32[]{:S(2)}) collective-permute-start(bf16[2,32,4096]{2,1,0:T(8,128)(2,1)S(1)} %get-tuple-element.54), channel_id=1, source_target_pairs={{1,2},{3,4},{5,6},{7,8},{9,10},{11,12},{13,14},{15,16},{17,18},{19... | collective-permute-start | bytes 1572872 | tf_op jit(solution)/shard_map/ppermute | solution.py:429
  57.8 16.8 %krylov.3 = (bf16[5,4,32,64,128]{4,3,2,1,0:T(8,128)(2,1)S(1)}, f32[4,32,64,128]{3,2,1,0:T(8,128)S(1)}, f32[8,128]{1,0:T(8,128)S(1)}) custom-call(f32[4,4]{1,0:T(4,128)S(1)} %copy-done.5, s32[1,32]{1,0:T(1,128)S(1)} %copy-done.6, bf16[4,32,4096]{2,1,0:T(8,128)(2,1)S(1)} %get-tuple-element.45.refs_2_.new, ...), custom_call_target="tpu_custom_call" | custom-call | flops 99999997952 | bytes 16777216 | tf_op jit(solution)/shard_map/krylov/pallas_call | solution.py:331
  74.6 2.5 %collective-permute-start.9 = (f32[8,128]{1,0:T(8,128)S(1)}, f32[8,128]{1,0:T(8,128)S(1)}, u32[]{:S(2)}, u32[]{:S(2)}) collective-permute-start(f32[8,128]{1,0:T(8,128)S(1)} %get-tuple-element.50.own), channel_id=1, source_target_pairs={{0,1},{1,0},{2,3},{3,2},{4,5},{5,4},{6,7},{7,6},{8,9},{9,8},{10,11... | collective-permute-start | bytes 12296 | tf_op jit(solution)/shard_map/ppermute | solution.py:429
  77.9 3.7 %project.3 = bf16[2,32,4096]{2,1,0:T(8,128)(2,1)S(1)} custom-call(f32[8,128]{1,0:T(8,128)S(1)} %get-tuple-element.50.own, f32[8,128]{1,0:T(8,128)S(1)} %collective-permute-done.9.got, bf16[5,4,32,64,128]{4,3,2,1,0:T(8,128)(2,1)S(1)} %get-tuple-element.51.u, f32[4,32,64,128]{3,2,1,0:T(8,128)S(1)} %get-tuple-element.52.last, ...), custom_call_target="tpu_custom_call" | custom-call | flops 1000000 | bytes 1024 | tf_op jit(solution)/shard_map/project/pallas_call | solution.py:344
  81.6 1.9 %collective-permute-start.11 = (bf16[2,32,4096]{2,1,0:T(8,128)(2,1)S(1)}, bf16[2,32,4096]{2,1,0:T(8,128)(2,1)S(1)}, u32[]{:S(2)}, u32[]{:S(2)}) collective-permute-start(bf16[2,32,4096]{2,1,0:T(8,128)(2,1)S(1)} %project.3), channel_id=1, source_target_pairs={{0,2},{2,4},{4,6},{6,8},{8,10},{10,12},{12,14},{14,16},{16,18},{18... | collective-permute-start | bytes 1572872 | tf_op jit(solution)/shard_map/ppermute | solution.py:429
  83.5 1.3 %collective-permute-start.12 = (bf16[2,32,4096]{2,1,0:T(8,128)(2,1)S(1)}, bf16[2,32,4096]{2,1,0:T(8,128)(2,1)S(1)}, u32[]{:S(2)}, u32[]{:S(2)}) collective-permute-start(bf16[2,32,4096]{2,1,0:T(8,128)(2,1)S(1)} %project.3), channel_id=1, source_target_pairs={{1,2},{3,4},{5,6},{7,8},{9,10},{11,12},{13,14},{15,16},{17,18},{19... | collective-permute-start | bytes 1572872 | tf_op jit(solution)/shard_map/ppermute | solution.py:429
  84.8 16.3 %collective-permute-done.11.low = bf16[2,32,4096]{2,1,0:T(8,128)(2,1)S(1)} collective-permute-done((bf16[2,32,4096]{2,1,0:T(8,128)(2,1)S(1)}, bf16[2,32,4096]{2,1,0:T(8,128)(2,1)S(1)}, u32[]{:S(2)}, u32[]{:S(2)}) %collective-permute-start.11) | collective-permute-done | bytes 524320 | tf_op jit(solution)/shard_map/ppermute | solution.py:429
  101.1 1.4 %collective-permute-done.12.high = bf16[2,32,4096]{2,1,0:T(8,128)(2,1)S(1)} collective-permute-done((bf16[2,32,4096]{2,1,0:T(8,128)(2,1)S(1)}, bf16[2,32,4096]{2,1,0:T(8,128)(2,1)S(1)}, u32[]{:S(2)}, u32[]{:S(2)}) %collective-permute-start.12) | collective-permute-done | bytes 524320 | tf_op jit(solution)/shard_map/ppermute | solution.py:429
  102.5 1.8 %choose.1 = (bf16[4,32,4096]{2,1,0:T(8,128)(2,1)}, bf16[2,32,4096]{2,1,0:T(8,128)(2,1)}) custom-call(bf16[4,32,4096]{2,1,0:T(8,128)(2,1)S(1)} %bitcast.11, bf16[4,32,4096]{2,1,0:T(8,128)(2,1)S(1)} %get-tuple-element.45.refs_2_.new, bf16[2,32,4096]{2,1,0:T(8,128)(2,1)S(1)} %collective-permute-done.11.low, ...), custom_call_target="tpu_custom_call" | custom-call | tf_op jit(solution)/shard_map/choose/pallas_call | solution.py:400
  (24 shorter events, 3.8 us)
Async XLA Ops:
  0.6 6.5 %collective-permute-start = (bf16[4,32,4096]{2,1,0:T(8,128)(2,1)}, bf16[4,32,4096]{2,1,0:T(8,128)(2,1)S(1)}, u32[]{:S(2)}, u32[]{:S(2)}) collective-permute-start(bf16[4,32,4096]{2,1,0:T(8,128)(2,1)} %bitcast.9), channel_id=1, source_target_pairs={{0,1},{1,0},{2,3},{3,2},{4,5},{5,4},{6,7},{7,6},{8,9},{9,8},{10,11... | collective-permute-start | bytes 3145736 | tf_op jit(solution)/shard_map/ppermute | solution.py:429
  0.7 5.0 %collective-permute-start.1 = (bf16[2,32,4096]{2,1,0:T(8,128)(2,1)}, bf16[2,32,4096]{2,1,0:T(8,128)(2,1)S(1)}, u32[]{:S(2)}, u32[]{:S(2)}) collective-permute-start(bf16[2,32,4096]{2,1,0:T(8,128)(2,1)} %bitcast.12), channel_id=1, source_target_pairs={{0,1},{2,3},{4,5},{6,7},{8,9},{10,11},{12,13},{14,15},{16,17},{18,... | collective-permute-start | bytes 1572872 | tf_op jit(solution)/shard_map/ppermute | solution.py:429
  3.2 4.0 %collective-permute-start.2 = (bf16[2,32,4096]{2,1,0:T(8,128)(2,1)}, bf16[2,32,4096]{2,1,0:T(8,128)(2,1)S(1)}, u32[]{:S(2)}, u32[]{:S(2)}) collective-permute-start(bf16[2,32,4096]{2,1,0:T(8,128)(2,1)} %bitcast.15), channel_id=1, source_target_pairs={{1,0},{3,2},{5,4},{7,6},{9,8},{11,10},{13,12},{15,14},{17,16},{19,... | collective-permute-start | bytes 1572872 | tf_op jit(solution)/shard_map/ppermute | solution.py:429
  7.2 40.6 %collective-permute-start.6 = (bf16[2,32,4096]{2,1,0:T(8,128)(2,1)}, bf16[2,32,4096]{2,1,0:T(8,128)(2,1)S(1)}, u32[]{:S(2)}, u32[]{:S(2)}) collective-permute-start(bf16[2,32,4096]{2,1,0:T(8,128)(2,1)} %bitcast.16), channel_id=1, source_target_pairs={{2,0},{4,2},{6,4},{8,6},{10,8},{12,10},{14,12},{16,14},{18,16},{20... | collective-permute-start | bytes 1572872 | tf_op jit(solution)/shard_map/ppermute | solution.py:429
  15.8 32.0 %collective-permute-start.7 = (bf16[2,32,4096]{2,1,0:T(8,128)(2,1)}, bf16[2,32,4096]{2,1,0:T(8,128)(2,1)S(1)}, u32[]{:S(2)}, u32[]{:S(2)}) collective-permute-start(bf16[2,32,4096]{2,1,0:T(8,128)(2,1)} %bitcast.17), channel_id=1, source_target_pairs={{2,1},{4,3},{6,5},{8,7},{10,9},{12,11},{14,13},{16,15},{18,17},{20... | collective-permute-start | bytes 1572872 | tf_op jit(solution)/shard_map/ppermute | solution.py:429
  17.2 30.6 %collective-permute-start.4 = (bf16[2,32,4096]{2,1,0:T(8,128)(2,1)S(1)}, bf16[2,32,4096]{2,1,0:T(8,128)(2,1)S(1)}, u32[]{:S(2)}, u32[]{:S(2)}) collective-permute-start(bf16[2,32,4096]{2,1,0:T(8,128)(2,1)S(1)} %get-tuple-element.39), channel_id=1, source_target_pairs={{2,0},{4,2},{6,4},{8,6},{10,8},{12,10},{14,12},{16,14},{18,16},{20... | collective-permute-start | bytes 1572872 | tf_op jit(solution)/shard_map/ppermute | solution.py:429
  19.5 28.3 %collective-permute-start.5 = (bf16[2,32,4096]{2,1,0:T(8,128)(2,1)S(1)}, bf16[2,32,4096]{2,1,0:T(8,128)(2,1)S(1)}, u32[]{:S(2)}, u32[]{:S(2)}) collective-permute-start(bf16[2,32,4096]{2,1,0:T(8,128)(2,1)S(1)} %get-tuple-element.40), channel_id=1, source_target_pairs={{2,1},{4,3},{6,5},{8,7},{10,9},{12,11},{14,13},{16,15},{18,17},{20... | collective-permute-start | bytes 1572872 | tf_op jit(solution)/shard_map/ppermute | solution.py:429
  20.8 1.2 %copy-start = (bf16[1,4,32,4096]{3,2,1,0:T(8,128)(2,1)S(1)}, bf16[1,4,32,4096]{3,2,1,0:T(8,128)(2,1)}, u32[]{:S(2)}) copy-start(bf16[1,4,32,4096]{3,2,1,0:T(8,128)(2,1)} %param.5) | copy-start | bytes 3145732
  22.0 1.0 copy-start.2
  23.1 1.0 copy-start.4
  24.1 0.7 copy-start.5
  24.8 0.7 copy-start.6
  42.8 1.2 %collective-permute-start.3 = (f32[8,128]{1,0:T(8,128)S(1)}, f32[8,128]{1,0:T(8,128)S(1)}, u32[]{:S(2)}, u32[]{:S(2)}) collective-permute-start(f32[8,128]{1,0:T(8,128)S(1)} %get-tuple-element.35.own), channel_id=1, source_target_pairs={{0,1},{1,0},{2,3},{3,2},{4,5},{5,4},{6,7},{7,6},{8,9},{9,8},{10,11... | collective-permute-start | bytes 12296 | tf_op jit(solution)/shard_map/ppermute | solution.py:429
  47.8 3.5 %collective-permute-start.8 = (bf16[2,32,4096]{2,1,0:T(8,128)(2,1)S(1)}, bf16[2,32,4096]{2,1,0:T(8,128)(2,1)S(1)}, u32[]{:S(2)}, u32[]{:S(2)}) collective-permute-start(bf16[2,32,4096]{2,1,0:T(8,128)(2,1)S(1)} %project.2.own), channel_id=1, source_target_pairs={{0,1},{1,0},{2,3},{3,2},{4,5},{5,4},{6,7},{7,6},{8,9},{9,8},{10,11... | collective-permute-start | bytes 1572872 | tf_op jit(solution)/shard_map/ppermute | solution.py:429
  56.5 25.1 %collective-permute-start.10 = (bf16[2,32,4096]{2,1,0:T(8,128)(2,1)S(1)}, bf16[2,32,4096]{2,1,0:T(8,128)(2,1)S(1)}, u32[]{:S(2)}, u32[]{:S(2)}) collective-permute-start(bf16[2,32,4096]{2,1,0:T(8,128)(2,1)S(1)} %get-tuple-element.54), channel_id=1, source_target_pairs={{1,2},{3,4},{5,6},{7,8},{9,10},{11,12},{13,14},{15,16},{17,18},{19... | collective-permute-start | bytes 1572872 | tf_op jit(solution)/shard_map/ppermute | solution.py:429
  74.6 27.9 %copy-start.1 = (bf16[1,4,32,4096]{3,2,1,0:T(8,128)(2,1)S(1)}, bf16[1,4,32,4096]{3,2,1,0:T(8,128)(2,1)}, u32[]{:S(2)}) copy-start(bf16[1,4,32,4096]{3,2,1,0:T(8,128)(2,1)} %param.5) | copy-start | bytes 3145732
  74.6 27.9 %copy-start.3 = (bf16[1,2,32,4096]{3,2,1,0:T(8,128)(2,1)S(1)}, bf16[1,2,32,4096]{3,2,1,0:T(8,128)(2,1)}, u32[]{:S(2)}) copy-start(bf16[1,2,32,4096]{3,2,1,0:T(8,128)(2,1)} %param.6) | copy-start | bytes 1572868
  74.6 3.3 %collective-permute-start.9 = (f32[8,128]{1,0:T(8,128)S(1)}, f32[8,128]{1,0:T(8,128)S(1)}, u32[]{:S(2)}, u32[]{:S(2)}) collective-permute-start(f32[8,128]{1,0:T(8,128)S(1)} %get-tuple-element.50.own), channel_id=1, source_target_pairs={{0,1},{1,0},{2,3},{3,2},{4,5},{5,4},{6,7},{7,6},{8,9},{9,8},{10,11... | collective-permute-start | bytes 12296 | tf_op jit(solution)/shard_map/ppermute | solution.py:429
  81.6 19.5 %collective-permute-start.11 = (bf16[2,32,4096]{2,1,0:T(8,128)(2,1)S(1)}, bf16[2,32,4096]{2,1,0:T(8,128)(2,1)S(1)}, u32[]{:S(2)}, u32[]{:S(2)}) collective-permute-start(bf16[2,32,4096]{2,1,0:T(8,128)(2,1)S(1)} %project.3), channel_id=1, source_target_pairs={{0,2},{2,4},{4,6},{6,8},{8,10},{10,12},{12,14},{14,16},{16,18},{18... | collective-permute-start | bytes 1572872 | tf_op jit(solution)/shard_map/ppermute | solution.py:429
  83.5 19.0 %collective-permute-start.12 = (bf16[2,32,4096]{2,1,0:T(8,128)(2,1)S(1)}, bf16[2,32,4096]{2,1,0:T(8,128)(2,1)S(1)}, u32[]{:S(2)}, u32[]{:S(2)}) collective-permute-start(bf16[2,32,4096]{2,1,0:T(8,128)(2,1)S(1)} %project.3), channel_id=1, source_target_pairs={{1,2},{3,4},{5,6},{7,8},{9,10},{11,12},{13,14},{15,16},{17,18},{19... | collective-permute-start | bytes 1572872 | tf_op jit(solution)/shard_map/ppermute | solution.py:429

commit v7 on v6

--- a/solution.py
+++ b/solution.py
@@ -436,7 +436,6 @@
     )
     b_even = send(low, to_even)
     b_odd = send(high, to_odd)
-    r_even = send(late_r, to_even)
     r_odd = send(late_r, to_odd)
 
     u, last, small, at, a_flat, l_flat = krylov(
@@ -445,8 +444,9 @@
     got_small = send(small, swap)
     env1 = grow(a_flat, l_flat, at)
     x = project(core_index, 0, small, got_small, u, last, at)
-    x, b_even, b_odd, r_even, r_odd = lax.optimization_barrier((x, b_even, b_odd, r_even, r_odd))
+    x, b_even, b_odd, r_odd = lax.optimization_barrier((x, b_even, b_odd, r_odd))
     got_x = send(x, swap)
+    r_even = send(r_odd, fall)
 
     new1, at, env2 = prepare(core_index, x, got_x, env1)
     got_env = send(env2, from_odd)

time: 105 us -> 103 us (0.981)
  starting transfers between devices: 24.9 us -> 22.7 us
    ppermute x13, starting transfers between devices: 24.9 us -> 22.7 us  [send(): return lax.ppermute(x, axes, pairs)]
  transfers between devices with their start and end apart: 13 -> 13, of which waited for: 5 -> 5; matrix products, arithmetic and copies ran while one was open for 1% -> 1% of each run, Pallas kernels for 43% -> 49%
where the time goes in v7:
time: 103 us; the launch traced here: 102 us
  Pallas kernels  51.5 us (50%)
  starting transfers between devices  22.7 us (22%)
  waiting for transfers between devices  21.1 us (20%)
  local copies, waits for them, and re-layouts  5.92 us (6%)
    pallas_call x2, Pallas kernels, krylov(): pl.pallas_call(functools.partial(krylov_kernel, second, core_of), out_sha...  34.1 us
    ppermute x13, starting transfers between devices, send(): return lax.ppermute(x, axes, pairs)  22.7 us
    ppermute x13, waiting for transfers between devices, send(): return lax.ppermute(x, axes, pairs)  21.1 us
    pallas_call x2, Pallas kernels, project(): pl.pallas_call(functools.partial(project_kernel, owner, core_of), out_sha...  7.43 us
    pallas_call x1, Pallas kernels, prepare(): pl.pallas_call(functools.partial(prepare_kernel, core_of), out_shape=(sha...  5.13 us
    unnamed x14, local copies, waits for them, and re-layouts  4.65 us
    pallas_call x1, Pallas kernels, grow(): pl.pallas_call(env_kernel, out_shape=shape(2, NB, FLAT), in_specs=[VM] *...  3.07 us
  transfers between devices with their start and end apart: 13, of which 5 were waited for; matrix products, arithmetic and copies ran while one was open for 1% of the time, Pallas kernels for 49%

profile of v7, /device:TPU:6, one launch (start us, length us, event | category | flops | bytes accessed | tf_op | source)
XLA Modules:
  0.0 102.1 jit_solution(12821964292890798439)
XLA Ops:
  0.7 2.4 %collective-permute-start.1 = (bf16[2,32,4096]{2,1,0:T(8,128)(2,1)}, bf16[2,32,4096]{2,1,0:T(8,128)(2,1)S(1)}, u32[]{:S(2)}, u32[]{:S(2)}) collective-permute-start(bf16[2,32,4096]{2,1,0:T(8,128)(2,1)} %bitcast.12), channel_id=1, source_target_pairs={{0,1},{2,3},{4,5},{6,7},{8,9},{10,11},{12,13},{14,15},{16,17},{18,... | collective-permute-start | bytes 1572872 | tf_op jit(solution)/shard_map/ppermute | solution.py:429
  3.2 1.3 %collective-permute-start.2 = (bf16[2,32,4096]{2,1,0:T(8,128)(2,1)}, bf16[2,32,4096]{2,1,0:T(8,128)(2,1)S(1)}, u32[]{:S(2)}, u32[]{:S(2)}) collective-permute-start(bf16[2,32,4096]{2,1,0:T(8,128)(2,1)} %bitcast.15), channel_id=1, source_target_pairs={{1,0},{3,2},{5,4},{7,6},{9,8},{11,10},{13,12},{15,14},{17,16},{19,... | collective-permute-start | bytes 1572872 | tf_op jit(solution)/shard_map/ppermute | solution.py:429
  4.5 1.3 %slice_bitcast_fusion = (bf16[2,32,4096]{2,1,0:T(8,128)(2,1)S(1)}, bf16[2,32,4096]{2,1,0:T(8,128)(2,1)S(1)}) fusion(bf16[1,4,32,4096]{3,2,1,0:T(8,128)(2,1)} %param.5), kind=kLoop, calls=%fused_computation | loop fusion | bytes 2097152 | tf_op jit(solution)/shard_map/slice | solution.py:435
  5.7 1.4 %collective-permute-done.2.refs_7_ = bf16[2,32,4096]{2,1,0:T(8,128)(2,1)S(1)} collective-permute-done((bf16[2,32,4096]{2,1,0:T(8,128)(2,1)}, bf16[2,32,4096]{2,1,0:T(8,128)(2,1)S(1)}, u32[]{:S(2)}, u32[]{:S(2)}) %collective-permute-start.2) | collective-permute-done | bytes 524320 | tf_op jit(solution)/shard_map/ppermute | solution.py:429
  7.2 8.7 %collective-permute-start.4 = (bf16[2,32,4096]{2,1,0:T(8,128)(2,1)S(1)}, bf16[2,32,4096]{2,1,0:T(8,128)(2,1)S(1)}, u32[]{:S(2)}, u32[]{:S(2)}) collective-permute-start(bf16[2,32,4096]{2,1,0:T(8,128)(2,1)S(1)} %get-tuple-element.38), channel_id=1, source_target_pairs={{2,0},{4,2},{6,4},{8,6},{10,8},{12,10},{14,12},{16,14},{18,16},{20... | collective-permute-start | bytes 1572872 | tf_op jit(solution)/shard_map/ppermute | solution.py:429
  15.8 1.3 %collective-permute-start.5 = (bf16[2,32,4096]{2,1,0:T(8,128)(2,1)S(1)}, bf16[2,32,4096]{2,1,0:T(8,128)(2,1)S(1)}, u32[]{:S(2)}, u32[]{:S(2)}) collective-permute-start(bf16[2,32,4096]{2,1,0:T(8,128)(2,1)S(1)} %get-tuple-element.39), channel_id=1, source_target_pairs={{2,1},{4,3},{6,5},{8,7},{10,9},{12,11},{14,13},{16,15},{18,17},{20... | collective-permute-start | bytes 1572872 | tf_op jit(solution)/shard_map/ppermute | solution.py:429
  17.2 1.3 %collective-permute-start.6 = (bf16[2,32,4096]{2,1,0:T(8,128)(2,1)}, bf16[2,32,4096]{2,1,0:T(8,128)(2,1)S(1)}, u32[]{:S(2)}, u32[]{:S(2)}) collective-permute-start(bf16[2,32,4096]{2,1,0:T(8,128)(2,1)} %bitcast.16), channel_id=1, source_target_pairs={{2,1},{4,3},{6,5},{8,7},{10,9},{12,11},{14,13},{16,15},{18,17},{20... | collective-permute-start | bytes 1572872 | tf_op jit(solution)/shard_map/ppermute | solution.py:429
  18.5 1.2 %copy-done = bf16[1,4,32,4096]{3,2,1,0:T(8,128)(2,1)S(1)} copy-done((bf16[1,4,32,4096]{3,2,1,0:T(8,128)(2,1)S(1)}, bf16[1,4,32,4096]{3,2,1,0:T(8,128)(2,1)}, u32[]{:S(2)}) %copy-start) | copy-done | bytes 1048600
  19.7 1.0 %copy-done.2 = bf16[1,2,32,4096]{3,2,1,0:T(8,128)(2,1)S(1)} copy-done((bf16[1,2,32,4096]{3,2,1,0:T(8,128)(2,1)S(1)}, bf16[1,2,32,4096]{3,2,1,0:T(8,128)(2,1)}, u32[]{:S(2)}) %copy-start.2) | copy-done | bytes 524312
  23.1 17.3 %krylov.2 = (bf16[5,4,32,64,128]{4,3,2,1,0:T(8,128)(2,1)S(1)}, f32[4,32,64,128]{3,2,1,0:T(8,128)S(1)}, f32[8,128]{1,0:T(8,128)S(1)}, bf16[32,64,256]{2,1,0:T(8,1...) custom-call(f32[4,4]{1,0:T(4,128)S(1)} %copy-done.5, s32[1,32]{1,0:T(1,128)S(1)} %copy-done.6, ...), custom_call_target="tpu_custom_call" | custom-call | flops 99999997952 | bytes 16777216 | tf_op jit(solution)/shard_map/krylov/pallas_call | solution.py:331
  40.6 1.2 %collective-permute-done.3.got = f32[8,128]{1,0:T(8,128)S(1)} collective-permute-done((f32[8,128]{1,0:T(8,128)S(1)}, f32[8,128]{1,0:T(8,128)S(1)}, u32[]{:S(2)}, u32[]{:S(2)}) %collective-permute-start.3) | collective-permute-done | bytes 4128 | tf_op jit(solution)/shard_map/ppermute | solution.py:429
  41.7 3.7 %project.2.own = bf16[2,32,4096]{2,1,0:T(8,128)(2,1)S(1)} custom-call(f32[8,128]{1,0:T(8,128)S(1)} %get-tuple-element.34.own, f32[8,128]{1,0:T(8,128)S(1)} %collective-permute-done.3.got, bf16[5,4,32,64,128]{4,3,2,1,0:T(8,128)(2,1)S(1)} %get-tuple-element.35.u, f32[4,32,64,128]{3,2,1,0:T(8,128)S(1)} %get-tuple-element.36.last, ...), custom_call_target="tpu_custom_call" | custom-call | flops 1000000 | bytes 1024 | tf_op jit(solution)/shard_map/project/pallas_call | solution.py:344
  45.7 1.5 %collective-permute-start.8 = (bf16[2,32,4096]{2,1,0:T(8,128)(2,1)S(1)}, bf16[2,32,4096]{2,1,0:T(8,128)(2,1)S(1)}, u32[]{:S(2)}, u32[]{:S(2)}) collective-permute-start(bf16[2,32,4096]{2,1,0:T(8,128)(2,1)S(1)} %collective-permute-done.6.refs_6_), channel_id=1, source_target_pairs={{1,0},{3,2},{5,4},{7,6},{9,8},{11,10},{13,12},{15,14},{17,16},{19,... | collective-permute-start | bytes 1572872 | tf_op jit(solution)/shard_map/ppermute | solution.py:429
  47.2 3.1 %grow.1.left.refs_7_.env = bf16[2,32,4096]{2,1,0:T(8,128)(2,1)S(1)} custom-call(bf16[4,32,4096]{2,1,0:T(8,128)(2,1)S(1)} %get-tuple-element.42.a_flat, bf16[2,32,4096]{2,1,0:T(8,128)(2,1)S(1)} %get-tuple-element.43.left, bf16[32,64,256]{2,1,0:T(8,128)(2,1)S(1)} %get-tuple-element.37.at), custom_call_target="tpu_custom_call" | custom-call | flops 1000000 | bytes 1024 | tf_op jit(solution)/shard_map/grow/pallas_call | solution.py:360
  50.3 5.1 %prepare.1 = (bf16[4,32,4096]{2,1,0:T(8,128)(2,1)S(1)}, bf16[32,64,256]{2,1,0:T(8,128)(2,1)S(1)}, bf16[2,32,4096]{2,1,0:T(8,128)(2,1)S(1)}) custom-call(bf16[2,32,4096]{2,1,0:T(8,128)(2,1)S(1)} %project.2.own, bf16[2,32,4096]{2,1,0:T(8,128)(2,1)S(1)} %collective-permute-done.7.got, bf16[2,32,4096]{2,1,0:T(8,128)(2,1)S(1)} %grow.1.left.refs_7_.env), custom_call_target="tpu_custom_call" | custom-call | flops 1000000 | bytes 1024 | tf_op jit(solution)/shard_map/prepare/pallas_call | solution.py:378
  55.4 1.3 %collective-permute-start.10 = (bf16[2,32,4096]{2,1,0:T(8,128)(2,1)S(1)}, bf16[2,32,4096]{2,1,0:T(8,128)(2,1)S(1)}, u32[]{:S(2)}, u32[]{:S(2)}) collective-permute-start(bf16[2,32,4096]{2,1,0:T(8,128)(2,1)S(1)} %get-tuple-element.52), channel_id=1, source_target_pairs={{1,2},{3,4},{5,6},{7,8},{9,10},{11,12},{13,14},{15,16},{17,18},{19... | collective-permute-start | bytes 1572872 | tf_op jit(solution)/shard_map/ppermute | solution.py:429
  56.7 16.8 %krylov.3 = (bf16[5,4,32,64,128]{4,3,2,1,0:T(8,128)(2,1)S(1)}, f32[4,32,64,128]{3,2,1,0:T(8,128)S(1)}, f32[8,128]{1,0:T(8,128)S(1)}) custom-call(f32[4,4]{1,0:T(4,128)S(1)} %copy-done.5, s32[1,32]{1,0:T(1,128)S(1)} %copy-done.6, bf16[4,32,4096]{2,1,0:T(8,128)(2,1)S(1)} %get-tuple-element.44.refs_2_.new, ...), custom_call_target="tpu_custom_call" | custom-call | flops 99999997952 | bytes 16777216 | tf_op jit(solution)/shard_map/krylov/pallas_call | solution.py:331
  73.6 1.3 %collective-permute-start.9 = (f32[8,128]{1,0:T(8,128)S(1)}, f32[8,128]{1,0:T(8,128)S(1)}, u32[]{:S(2)}, u32[]{:S(2)}) collective-permute-start(f32[8,128]{1,0:T(8,128)S(1)} %get-tuple-element.48.own), channel_id=1, source_target_pairs={{0,1},{1,0},{2,3},{3,2},{4,5},{5,4},{6,7},{7,6},{8,9},{9,8},{10,11... | collective-permute-start | bytes 12296 | tf_op jit(solution)/shard_map/ppermute | solution.py:429
  75.7 3.7 %project.3 = bf16[2,32,4096]{2,1,0:T(8,128)(2,1)S(1)} custom-call(f32[8,128]{1,0:T(8,128)S(1)} %get-tuple-element.48.own, f32[8,128]{1,0:T(8,128)S(1)} %collective-permute-done.9.got, bf16[5,4,32,64,128]{4,3,2,1,0:T(8,128)(2,1)S(1)} %get-tuple-element.49.u, f32[4,32,64,128]{3,2,1,0:T(8,128)S(1)} %get-tuple-element.50.last, ...), custom_call_target="tpu_custom_call" | custom-call | flops 1000000 | bytes 1024 | tf_op jit(solution)/shard_map/project/pallas_call | solution.py:344
  79.4 1.9 %collective-permute-start.11 = (bf16[2,32,4096]{2,1,0:T(8,128)(2,1)S(1)}, bf16[2,32,4096]{2,1,0:T(8,128)(2,1)S(1)}, u32[]{:S(2)}, u32[]{:S(2)}) collective-permute-start(bf16[2,32,4096]{2,1,0:T(8,128)(2,1)S(1)} %project.3), channel_id=1, source_target_pairs={{0,2},{2,4},{4,6},{6,8},{8,10},{10,12},{12,14},{14,16},{16,18},{18... | collective-permute-start | bytes 1572872 | tf_op jit(solution)/shard_map/ppermute | solution.py:429
  81.3 1.3 %collective-permute-start.12 = (bf16[2,32,4096]{2,1,0:T(8,128)(2,1)S(1)}, bf16[2,32,4096]{2,1,0:T(8,128)(2,1)S(1)}, u32[]{:S(2)}, u32[]{:S(2)}) collective-permute-start(bf16[2,32,4096]{2,1,0:T(8,128)(2,1)S(1)} %project.3), channel_id=1, source_target_pairs={{1,2},{3,4},{5,6},{7,8},{9,10},{11,12},{13,14},{15,16},{17,18},{19... | collective-permute-start | bytes 1572872 | tf_op jit(solution)/shard_map/ppermute | solution.py:429
  82.6 16.3 %collective-permute-done.11.low = bf16[2,32,4096]{2,1,0:T(8,128)(2,1)S(1)} collective-permute-done((bf16[2,32,4096]{2,1,0:T(8,128)(2,1)S(1)}, bf16[2,32,4096]{2,1,0:T(8,128)(2,1)S(1)}, u32[]{:S(2)}, u32[]{:S(2)}) %collective-permute-start.11) | collective-permute-done | bytes 524320 | tf_op jit(solution)/shard_map/ppermute | solution.py:429
  98.9 1.4 %collective-permute-done.12.high = bf16[2,32,4096]{2,1,0:T(8,128)(2,1)S(1)} collective-permute-done((bf16[2,32,4096]{2,1,0:T(8,128)(2,1)S(1)}, bf16[2,32,4096]{2,1,0:T(8,128)(2,1)S(1)}, u32[]{:S(2)}, u32[]{:S(2)}) %collective-permute-start.12) | collective-permute-done | bytes 524320 | tf_op jit(solution)/shard_map/ppermute | solution.py:429
  100.3 1.8 %choose.1 = (bf16[4,32,4096]{2,1,0:T(8,128)(2,1)}, bf16[2,32,4096]{2,1,0:T(8,128)(2,1)}) custom-call(bf16[4,32,4096]{2,1,0:T(8,128)(2,1)S(1)} %bitcast.11, bf16[4,32,4096]{2,1,0:T(8,128)(2,1)S(1)} %get-tuple-element.44.refs_2_.new, bf16[2,32,4096]{2,1,0:T(8,128)(2,1)S(1)} %collective-permute-done.11.low, ...), custom_call_target="tpu_custom_call" | custom-call | tf_op jit(solution)/shard_map/choose/pallas_call | solution.py:400
  (24 shorter events, 3.7 us)
Async XLA Ops:
  0.6 6.5 %collective-permute-start = (bf16[4,32,4096]{2,1,0:T(8,128)(2,1)}, bf16[4,32,4096]{2,1,0:T(8,128)(2,1)S(1)}, u32[]{:S(2)}, u32[]{:S(2)}) collective-permute-start(bf16[4,32,4096]{2,1,0:T(8,128)(2,1)} %bitcast.9), channel_id=1, source_target_pairs={{0,1},{1,0},{2,3},{3,2},{4,5},{5,4},{6,7},{7,6},{8,9},{9,8},{10,11... | collective-permute-start | bytes 3145736 | tf_op jit(solution)/shard_map/ppermute | solution.py:429
  0.7 5.0 %collective-permute-start.1 = (bf16[2,32,4096]{2,1,0:T(8,128)(2,1)}, bf16[2,32,4096]{2,1,0:T(8,128)(2,1)S(1)}, u32[]{:S(2)}, u32[]{:S(2)}) collective-permute-start(bf16[2,32,4096]{2,1,0:T(8,128)(2,1)} %bitcast.12), channel_id=1, source_target_pairs={{0,1},{2,3},{4,5},{6,7},{8,9},{10,11},{12,13},{14,15},{16,17},{18,... | collective-permute-start | bytes 1572872 | tf_op jit(solution)/shard_map/ppermute | solution.py:429
  3.2 4.0 %collective-permute-start.2 = (bf16[2,32,4096]{2,1,0:T(8,128)(2,1)}, bf16[2,32,4096]{2,1,0:T(8,128)(2,1)S(1)}, u32[]{:S(2)}, u32[]{:S(2)}) collective-permute-start(bf16[2,32,4096]{2,1,0:T(8,128)(2,1)} %bitcast.15), channel_id=1, source_target_pairs={{1,0},{3,2},{5,4},{7,6},{9,8},{11,10},{13,12},{15,14},{17,16},{19,... | collective-permute-start | bytes 1572872 | tf_op jit(solution)/shard_map/ppermute | solution.py:429
  7.2 38.3 %collective-permute-start.4 = (bf16[2,32,4096]{2,1,0:T(8,128)(2,1)S(1)}, bf16[2,32,4096]{2,1,0:T(8,128)(2,1)S(1)}, u32[]{:S(2)}, u32[]{:S(2)}) collective-permute-start(bf16[2,32,4096]{2,1,0:T(8,128)(2,1)S(1)} %get-tuple-element.38), channel_id=1, source_target_pairs={{2,0},{4,2},{6,4},{8,6},{10,8},{12,10},{14,12},{16,14},{18,16},{20... | collective-permute-start | bytes 1572872 | tf_op jit(solution)/shard_map/ppermute | solution.py:429
  15.8 29.6 %collective-permute-start.5 = (bf16[2,32,4096]{2,1,0:T(8,128)(2,1)S(1)}, bf16[2,32,4096]{2,1,0:T(8,128)(2,1)S(1)}, u32[]{:S(2)}, u32[]{:S(2)}) collective-permute-start(bf16[2,32,4096]{2,1,0:T(8,128)(2,1)S(1)} %get-tuple-element.39), channel_id=1, source_target_pairs={{2,1},{4,3},{6,5},{8,7},{10,9},{12,11},{14,13},{16,15},{18,17},{20... | collective-permute-start | bytes 1572872 | tf_op jit(solution)/shard_map/ppermute | solution.py:429
  17.2 28.3 %collective-permute-start.6 = (bf16[2,32,4096]{2,1,0:T(8,128)(2,1)}, bf16[2,32,4096]{2,1,0:T(8,128)(2,1)S(1)}, u32[]{:S(2)}, u32[]{:S(2)}) collective-permute-start(bf16[2,32,4096]{2,1,0:T(8,128)(2,1)} %bitcast.16), channel_id=1, source_target_pairs={{2,1},{4,3},{6,5},{8,7},{10,9},{12,11},{14,13},{16,15},{18,17},{20... | collective-permute-start | bytes 1572872 | tf_op jit(solution)/shard_map/ppermute | solution.py:429
  18.5 1.2 %copy-start = (bf16[1,4,32,4096]{3,2,1,0:T(8,128)(2,1)S(1)}, bf16[1,4,32,4096]{3,2,1,0:T(8,128)(2,1)}, u32[]{:S(2)}) copy-start(bf16[1,4,32,4096]{3,2,1,0:T(8,128)(2,1)} %param.5) | copy-start | bytes 3145732
  19.7 1.0 %copy-start.2 = (bf16[1,2,32,4096]{3,2,1,0:T(8,128)(2,1)S(1)}, bf16[1,2,32,4096]{3,2,1,0:T(8,128)(2,1)}, u32[]{:S(2)}) copy-start(bf16[1,2,32,4096]{3,2,1,0:T(8,128)(2,1)} %param.6) | copy-start | bytes 1572868
  20.8 1.0 %copy-start.4 = (bf16[1,2,32,4096]{3,2,1,0:T(8,128)(2,1)S(1)}, bf16[1,2,32,4096]{3,2,1,0:T(8,128)(2,1)}, u32[]{:S(2)}) copy-start(bf16[1,2,32,4096]{3,2,1,0:T(8,128)(2,1)} %param.7) | copy-start | bytes 1572868
  21.8 0.7 copy-start.5
  22.5 0.7 copy-start.6
  40.5 1.2 %collective-permute-start.3 = (f32[8,128]{1,0:T(8,128)S(1)}, f32[8,128]{1,0:T(8,128)S(1)}, u32[]{:S(2)}, u32[]{:S(2)}) collective-permute-start(f32[8,128]{1,0:T(8,128)S(1)} %get-tuple-element.34.own), channel_id=1, source_target_pairs={{0,1},{1,0},{2,3},{3,2},{4,5},{5,4},{6,7},{7,6},{8,9},{9,8},{10,11... | collective-permute-start | bytes 12296 | tf_op jit(solution)/shard_map/ppermute | solution.py:429
  45.5 4.8 %collective-permute-start.7 = (bf16[2,32,4096]{2,1,0:T(8,128)(2,1)S(1)}, bf16[2,32,4096]{2,1,0:T(8,128)(2,1)S(1)}, u32[]{:S(2)}, u32[]{:S(2)}) collective-permute-start(bf16[2,32,4096]{2,1,0:T(8,128)(2,1)S(1)} %project.2.own), channel_id=1, source_target_pairs={{0,1},{1,0},{2,3},{3,2},{4,5},{5,4},{6,7},{7,6},{8,9},{9,8},{10,11... | collective-permute-start | bytes 1572872 | tf_op jit(solution)/shard_map/ppermute | solution.py:429
  45.7 11.0 %collective-permute-start.8 = (bf16[2,32,4096]{2,1,0:T(8,128)(2,1)S(1)}, bf16[2,32,4096]{2,1,0:T(8,128)(2,1)S(1)}, u32[]{:S(2)}, u32[]{:S(2)}) collective-permute-start(bf16[2,32,4096]{2,1,0:T(8,128)(2,1)S(1)} %collective-permute-done.6.refs_6_), channel_id=1, source_target_pairs={{1,0},{3,2},{5,4},{7,6},{9,8},{11,10},{13,12},{15,14},{17,16},{19,... | collective-permute-start | bytes 1572872 | tf_op jit(solution)/shard_map/ppermute | solution.py:429
  55.4 24.0 %collective-permute-start.10 = (bf16[2,32,4096]{2,1,0:T(8,128)(2,1)S(1)}, bf16[2,32,4096]{2,1,0:T(8,128)(2,1)S(1)}, u32[]{:S(2)}, u32[]{:S(2)}) collective-permute-start(bf16[2,32,4096]{2,1,0:T(8,128)(2,1)S(1)} %get-tuple-element.52), channel_id=1, source_target_pairs={{1,2},{3,4},{5,6},{7,8},{9,10},{11,12},{13,14},{15,16},{17,18},{19... | collective-permute-start | bytes 1572872 | tf_op jit(solution)/shard_map/ppermute | solution.py:429
  73.5 26.8 %copy-start.1 = (bf16[1,4,32,4096]{3,2,1,0:T(8,128)(2,1)S(1)}, bf16[1,4,32,4096]{3,2,1,0:T(8,128)(2,1)}, u32[]{:S(2)}) copy-start(bf16[1,4,32,4096]{3,2,1,0:T(8,128)(2,1)} %param.5) | copy-start | bytes 3145732
  73.5 26.8 %copy-start.3 = (bf16[1,2,32,4096]{3,2,1,0:T(8,128)(2,1)S(1)}, bf16[1,2,32,4096]{3,2,1,0:T(8,128)(2,1)}, u32[]{:S(2)}) copy-start(bf16[1,2,32,4096]{3,2,1,0:T(8,128)(2,1)} %param.6) | copy-start | bytes 1572868
  73.6 2.1 %collective-permute-start.9 = (f32[8,128]{1,0:T(8,128)S(1)}, f32[8,128]{1,0:T(8,128)S(1)}, u32[]{:S(2)}, u32[]{:S(2)}) collective-permute-start(f32[8,128]{1,0:T(8,128)S(1)} %get-tuple-element.48.own), channel_id=1, source_target_pairs={{0,1},{1,0},{2,3},{3,2},{4,5},{5,4},{6,7},{7,6},{8,9},{9,8},{10,11... | collective-permute-start | bytes 12296 | tf_op jit(solution)/shard_map/ppermute | solution.py:429
  79.4 19.5 %collective-permute-start.11 = (bf16[2,32,4096]{2,1,0:T(8,128)(2,1)S(1)}, bf16[2,32,4096]{2,1,0:T(8,128)(2,1)S(1)}, u32[]{:S(2)}, u32[]{:S(2)}) collective-permute-start(bf16[2,32,4096]{2,1,0:T(8,128)(2,1)S(1)} %project.3), channel_id=1, source_target_pairs={{0,2},{2,4},{4,6},{6,8},{8,10},{10,12},{12,14},{14,16},{16,18},{18... | collective-permute-start | bytes 1572872 | tf_op jit(solution)/shard_map/ppermute | solution.py:429
  81.3 19.0 %collective-permute-start.12 = (bf16[2,32,4096]{2,1,0:T(8,128)(2,1)S(1)}, bf16[2,32,4096]{2,1,0:T(8,128)(2,1)S(1)}, u32[]{:S(2)}, u32[]{:S(2)}) collective-permute-start(bf16[2,32,4096]{2,1,0:T(8,128)(2,1)S(1)} %project.3), channel_id=1, source_target_pairs={{1,2},{3,4},{5,6},{7,8},{9,10},{11,12},{13,14},{15,16},{17,18},{19... | collective-permute-start | bytes 1572872 | tf_op jit(solution)/shard_map/ppermute | solution.py:429
